TPU v7x, 32 devices: a whole 2x2x4 slice. The times are simulated.
32 devices in a mesh: req: 8 (over z, y), tp: 4 (over x, core).
Axes of the slice: x: 2, y: 2, z: 4, core: 2. Of those that a mesh axis runs over, the one named last changes fastest.
Arguments:
- tokens: bfloat16 [128, 2048], P('req'), may hold values from -6 to 6
- lengths: int32 [128], P('req'), may hold values from 1 to 8192, 32768 in all
- pool_order: int32 [128], replicated, may hold values from 0 to 127, each once
- positions: int32 [128], P('req'), may hold values from 0 to 16383
- slot_mask: int32 [32768], P('req'), may hold values 0 or 1
- kv_cache: bfloat16 [32768, 2, 1024], P('req', None, 'tp'), may hold values from -420 to 420
- attn_gain: bfloat16 [2048], replicated, may hold values from 0.25 to 1.75
- w_query: bfloat16 [2048, 2048], P(None, 'tp'), may hold values from -0.125 to 0.125
- w_key: bfloat16 [2048, 1024], P(None, 'tp'), may hold values from -0.125 to 0.125
- w_value: bfloat16 [2048, 1024], P(None, 'tp'), may hold values from -0.125 to 0.125
- w_out: bfloat16 [2048, 2048], P('tp'), may hold values from -0.125 to 0.125
- ffn_gain: bfloat16 [2048], replicated, may hold values from 0.25 to 1.75
- w_gate: bfloat16 [2048, 4096], P(None, 'tp'), may hold values from -0.125 to 0.125
- w_up: bfloat16 [2048, 4096], P(None, 'tp'), may hold values from -0.125 to 0.125
- w_down: bfloat16 [4096, 2048], P('tp'), may hold values from -0.09375 to 0.09375
Outputs:
- hidden_out: float32 [128, 2048], P('req')
- new_kv: float32 [128, 2, 1024], P('req', None, 'tp')
Inputs may be any that keep to these rules, and one draw needn't show every extreme that they name: The lengths add up to 32768, so the requests' caches fill the pool end to end; the largest is exactly 8192. `pool_order`: each request appears exactly once.
All inputs are finite; a program needn't handle non-finite values. No bound on the sum of `lengths` or of `slot_mask` on one device may be relied on, other than what follows from the above.
Results may differ from a plain program's by a relative error of at most 0.013.
The roundings to bfloat16 on the way count: a program that leaves them out, or rounds other values in their place, can miss the bound.
Values may be sent and summed in bfloat16 or wider, within the bound.
No kernel may reach another device: no remote copies, remote signals or barrier semaphores. Data moves between devices by JAX's collectives and lax.ppermute only.
A program may use at most 192 MiB of HBM per device.

v0:
```python
import math

import jax
import jax.numpy as jnp
from jax import lax
from jax.sharding import PartitionSpec as P

HEAD_DIM = 128


ROPE_BASE = 1000000.0
EPS = 1e-05
FLOOR = -1e30


def joined(part, axis, combine):
    gathered = jax.tree.map(lambda a: lax.all_gather(a, axis), part)

    def take(source):
        return jax.tree.map(lambda a: lax.dynamic_index_in_dim(a, source, 0, False), gathered)

    return lax.fori_loop(
        1, lax.axis_size(axis), lambda source, state: combine(state, take(source)), take(0)
    )


def rms_norm(rows, gain):
    mean_sq = jnp.mean(rows * rows, axis=-1, keepdims=True)
    return rows * lax.rsqrt(mean_sq + EPS) * gain.astype(jnp.float32)


def rotate(vectors, places):
    width = vectors.shape[-1]
    half = width // 2
    freq = ROPE_BASE ** (-(jnp.arange(half, dtype=jnp.float32) * 2.0) / width)
    angle = places.astype(jnp.float32)[:, None] * freq[None, :]
    cosine = jnp.cos(angle)[:, None, :]
    sine = jnp.sin(angle)[:, None, :]
    first = vectors[..., :half]
    second = vectors[..., half:]
    return jnp.concatenate(
        [first * cosine - second * sine, second * cosine + first * sine], axis=-1
    )


def combine_parts(first, second):
    peak = jnp.maximum(first[0], second[0])
    left = jnp.exp(first[0] - peak)
    right = jnp.exp(second[0] - peak)
    return (
        peak,
        first[1] * left + second[1] * right,
        first[2] * left[..., None] + second[2] * right[..., None],
    )


def per_device(
    tokens,
    lengths,
    pool_order,
    positions,
    slot_mask,
    kv_cache,
    attn_gain,
    w_query,
    w_key,
    w_value,
    w_out,
    ffn_gain,
    w_gate,
    w_up,
    w_down,
):
    count = tokens.shape[0]
    head_dim = HEAD_DIM
    kv_local = w_key.shape[1] // head_dim
    q_local = w_query.shape[1] // head_dim
    group = q_local // kv_local
    slot_count = kv_cache.shape[0]
    scale = 1.0 / math.sqrt(head_dim)
    highest = lax.Precision.HIGHEST
    all_lengths = lax.all_gather(lengths, "req", axis=0, tiled=True)
    total_reqs = all_lengths.shape[0]
    ordered = all_lengths[pool_order]
    ends = jnp.cumsum(ordered)
    base = lax.axis_index("req") * slot_count
    slot_ids = base + jnp.arange(slot_count, dtype=jnp.int32)
    place = jnp.searchsorted(ends, slot_ids, side="right")
    owner = pool_order[place]
    belongs = owner[:, None] == jnp.arange(total_reqs, dtype=jnp.int32)[None, :]
    belongs_f = belongs.astype(jnp.float32)
    rows = tokens.astype(jnp.float32)
    normed = rms_norm(rows, attn_gain).astype(jnp.bfloat16)
    query = rotate(
        jnp.dot(normed, w_query, preferred_element_type=jnp.float32).reshape(
            count, q_local, head_dim
        ),
        positions,
    ).astype(jnp.bfloat16)
    key_full = rotate(
        jnp.dot(normed, w_key, preferred_element_type=jnp.float32).reshape(
            count, kv_local, head_dim
        ),
        positions,
    )
    value_full = jnp.dot(normed, w_value, preferred_element_type=jnp.float32)
    new_kv = jnp.stack([key_full.reshape(count, kv_local * head_dim), value_full], axis=1)
    new_key = key_full.astype(jnp.bfloat16)
    new_value = value_full.astype(jnp.bfloat16)
    everyone = lax.all_gather(query.reshape(count, q_local * head_dim), "req", axis=0, tiled=True)
    picked = everyone[owner].reshape(slot_count, kv_local, group, head_dim)
    keys = kv_cache[:, 0, :].reshape(slot_count, kv_local, head_dim)
    values = kv_cache[:, 1, :].reshape(slot_count, kv_local, head_dim)
    scores = jnp.einsum("skgd,skd->skg", picked, keys, preferred_element_type=jnp.float32) * scale
    live = (slot_mask == 1)[:, None, None]
    scores = jnp.where(live, scores, FLOOR)
    peak_heads = []
    for head in range(kv_local):
        masked = jnp.where(belongs[:, :, None], scores[:, head, :][:, None, :], FLOOR)
        peak_heads.append(jnp.max(masked, axis=0))
    peak = jnp.stack(peak_heads, axis=1)
    weights = jnp.where(live, jnp.exp(scores - peak[owner]), 0.0)
    total = jnp.dot(
        belongs_f.T,
        weights.reshape(slot_count, kv_local * group),
        precision=highest,
        preferred_element_type=jnp.float32,
    ).reshape(total_reqs, kv_local, group)
    sum_heads = []
    for head in range(kv_local):
        spread = belongs_f[:, :, None] * weights[:, head, :][:, None, :]
        head_values = values[:, head, :].astype(jnp.float32)
        sum_heads.append(
            jnp.einsum(
                "srg,sd->rgd",
                spread,
                head_values,
                precision=highest,
                preferred_element_type=jnp.float32,
            )
        )
    summed = jnp.stack(sum_heads, axis=1)
    start = lax.axis_index("req") * count
    merged = joined((peak, total, summed), "req", combine_parts)
    own_peak = lax.dynamic_slice_in_dim(merged[0], start, count, 0)
    own_total = lax.dynamic_slice_in_dim(merged[1], start, count, 0)
    own_sum = lax.dynamic_slice_in_dim(merged[2], start, count, 0)
    own_query = query.reshape(count, kv_local, group, head_dim)
    own_score = (
        jnp.einsum("nkgd,nkd->nkg", own_query, new_key, preferred_element_type=jnp.float32) * scale
    )
    final_peak = jnp.maximum(own_peak, own_score)
    old_part = jnp.exp(own_peak - final_peak)
    new_part = jnp.exp(own_score - final_peak)
    denom = own_total * old_part + new_part
    numer = own_sum * old_part[..., None] + new_part[..., None] * new_value.reshape(
        count, kv_local, 1, head_dim
    ).astype(jnp.float32)
    context = (numer / denom[..., None]).reshape(count, q_local * head_dim).astype(jnp.bfloat16)
    partial_attn = jnp.dot(context, w_out, preferred_element_type=jnp.float32)
    mid = rows + lax.psum(partial_attn, "tp")
    normed_mid = rms_norm(mid, ffn_gain).astype(jnp.bfloat16)
    gate = jnp.dot(normed_mid, w_gate, preferred_element_type=jnp.float32)
    upper = jnp.dot(normed_mid, w_up, preferred_element_type=jnp.float32)
    act = (jax.nn.silu(gate) * upper).astype(jnp.bfloat16)
    down_part = jnp.dot(act, w_down, preferred_element_type=jnp.float32)
    hidden_out = mid + lax.psum(down_part, "tp")
    return (hidden_out, new_kv)


def solution(mesh):
    placed = (
        P("req", None),
        P("req"),
        P(),
        P("req"),
        P("req"),
        P("req", None, "tp"),
        P(),
        P(None, "tp"),
        P(None, "tp"),
        P(None, "tp"),
        P("tp", None),
        P(),
        P(None, "tp"),
        P(None, "tp"),
        P("tp", None),
    )
    return jax.shard_map(
        per_device,
        mesh=mesh,
        in_specs=placed,
        out_specs=(P("req", None), P("req", None, "tp")),
        check_vma=False,
    )
```

profile of v0, /device:TPU:0, one launch (start us, length us, event | category | flops | bytes accessed | tf_op | source)
XLA Modules:
  0.0 602.6 jit_solution(14756776496958116122)
XLA Ops:
  9.1 2.1 fusion.46
  12.1 32.3 %all_gather.22 = bf16[128,512]{1,0:T(8,128)(2,1)S(1)} all-gather(bf16[16,512]{1,0:T(8,128)(2,1)S(1)} %bitcast.106), channel_id=1, replica_groups=mesh['req'=8,'tp'=4] {'req'}, dimensions={0}, use_global_device_ids=true | all-gather | bytes 147456 | tf_op jit(solution)/shard_map/all_gather | solution.py:110
  44.4 1.2 dynamic-slice
  47.2 10.8 %all-reduce = s32[128]{0:T(128)S(1)} all-reduce(s32[128]{0:T(128)S(1)} %dynamic-update-slice), channel_id=1, replica_groups=mesh['req'=8,'tp'=4] {'req'}, use_global_device_ids=true, to_apply=%add | all-reduce | flops 128 | bytes 1024
  58.7 1.2 gather_fusion.1
  60.3 198.4 %while.44 = (s32[]{:T(128)}, u32[4096]{0:T(1024)S(1)}, u32[4096]{0:T(1024)S(1)}, s32[128]{0:T(128)S(1)}, s32[]{:T(128)}, /*index=5*/s32[]{:T(128)}, s32[]{:T(128)}, s32[]{}) while((s32[]{:T(128)}, u32[4096]{0:T(1024)S(1)}, u32[4096]{0:T(1024)S(1)}, s32[128]{0:T(128)S(1)}, s32[]{:T(128)}, /*index=5*/s32[]{:T(128)}, s32[]{:T(128)}, ...), condition=%wide.region_2.3_spmd.clone, body=%wide.region_1.2_spmd.clone.sunk | while | flops 81924 | bytes 254065 | solution.py:88
  60.3 24.7 %gather_fusion = s32[4096]{0:T(1024)S(1)} fusion(s32[128]{0:T(128)S(1)} %get-tuple-element.479, u32[4096]{0:T(1024)S(1)} %broadcast_clamp_fusion.3), kind=kCustom, calls=%fused_computation.clone.clone.1 | custom fusion | bytes 49152 | tf_op jit(solution)/shard_map/jit(searchsorted)/jit(_searchsorted_scan_impl)/vmap(jit(_searchsorted_scan_impl))/while/body/eval_jaxpr/gather | solution.py:88
  85.1 24.7 %gather_fusion = s32[4096]{0:T(1024)S(1)} fusion(s32[128]{0:T(128)S(1)} %get-tuple-element.479, u32[4096]{0:T(1024)S(1)} %broadcast_clamp_fusion.3), kind=kCustom, calls=%fused_computation.clone.clone.1 | custom fusion | bytes 49152 | tf_op jit(solution)/shard_map/jit(searchsorted)/jit(_searchsorted_scan_impl)/vmap(jit(_searchsorted_scan_impl))/while/body/eval_jaxpr/gather | solution.py:88
  109.9 24.7 %gather_fusion = s32[4096]{0:T(1024)S(1)} fusion(s32[128]{0:T(128)S(1)} %get-tuple-element.479, u32[4096]{0:T(1024)S(1)} %broadcast_clamp_fusion.3), kind=kCustom, calls=%fused_computation.clone.clone.1 | custom fusion | bytes 49152 | tf_op jit(solution)/shard_map/jit(searchsorted)/jit(_searchsorted_scan_impl)/vmap(jit(_searchsorted_scan_impl))/while/body/eval_jaxpr/gather | solution.py:88
  134.7 24.7 %gather_fusion = s32[4096]{0:T(1024)S(1)} fusion(s32[128]{0:T(128)S(1)} %get-tuple-element.479, u32[4096]{0:T(1024)S(1)} %broadcast_clamp_fusion.3), kind=kCustom, calls=%fused_computation.clone.clone.1 | custom fusion | bytes 49152 | tf_op jit(solution)/shard_map/jit(searchsorted)/jit(_searchsorted_scan_impl)/vmap(jit(_searchsorted_scan_impl))/while/body/eval_jaxpr/gather | solution.py:88
  159.5 24.7 %gather_fusion = s32[4096]{0:T(1024)S(1)} fusion(s32[128]{0:T(128)S(1)} %get-tuple-element.479, u32[4096]{0:T(1024)S(1)} %broadcast_clamp_fusion.3), kind=kCustom, calls=%fused_computation.clone.clone.1 | custom fusion | bytes 49152 | tf_op jit(solution)/shard_map/jit(searchsorted)/jit(_searchsorted_scan_impl)/vmap(jit(_searchsorted_scan_impl))/while/body/eval_jaxpr/gather | solution.py:88
  184.3 24.7 %gather_fusion = s32[4096]{0:T(1024)S(1)} fusion(s32[128]{0:T(128)S(1)} %get-tuple-element.479, u32[4096]{0:T(1024)S(1)} %broadcast_clamp_fusion.3), kind=kCustom, calls=%fused_computation.clone.clone.1 | custom fusion | bytes 49152 | tf_op jit(solution)/shard_map/jit(searchsorted)/jit(_searchsorted_scan_impl)/vmap(jit(_searchsorted_scan_impl))/while/body/eval_jaxpr/gather | solution.py:88
  209.1 24.7 %gather_fusion = s32[4096]{0:T(1024)S(1)} fusion(s32[128]{0:T(128)S(1)} %get-tuple-element.479, u32[4096]{0:T(1024)S(1)} %broadcast_clamp_fusion.3), kind=kCustom, calls=%fused_computation.clone.clone.1 | custom fusion | bytes 49152 | tf_op jit(solution)/shard_map/jit(searchsorted)/jit(_searchsorted_scan_impl)/vmap(jit(_searchsorted_scan_impl))/while/body/eval_jaxpr/gather | solution.py:88
  233.9 24.7 %gather_fusion = s32[4096]{0:T(1024)S(1)} fusion(s32[128]{0:T(128)S(1)} %get-tuple-element.479, u32[4096]{0:T(1024)S(1)} %broadcast_clamp_fusion.3), kind=kCustom, calls=%fused_computation.clone.clone.1 | custom fusion | bytes 49152 | tf_op jit(solution)/shard_map/jit(searchsorted)/jit(_searchsorted_scan_impl)/vmap(jit(_searchsorted_scan_impl))/while/body/eval_jaxpr/gather | solution.py:88
  259.3 24.7 %gather_fusion.2 = s32[4096]{0:T(1024)S(1)} fusion(s32[128]{0:T(128)S(1)} %copy-done.1, s32[4096]{0:T(1024)S(1)} %fusion.35), kind=kCustom, calls=%fused_computation.2 | custom fusion | bytes 49152 | tf_op jit(solution)/shard_map/gather | solution.py:89
  284.0 3.0 fusion.22
  287.1 17.3 %gather_fusion.3 = bf16[4096,512]{1,0:T(8,128)(2,1)} fusion(bf16[128,512]{1,0:T(8,128)(2,1)S(1)} %all_gather.22, s32[4096]{0:T(1024)S(1)} %broadcast_clamp_fusion.1), kind=kCustom, calls=%fused_computation.3 | custom fusion | bytes 8404992 | tf_op jit(solution)/shard_map/gather | solution.py:111
  304.4 7.0 %reshape.198 = bf16[4096,2,2,128]{3,2,1,0:T(2,128)(2,1)} reshape(bf16[4096,512]{1,0:T(8,128)(2,1)} %gather_fusion.3) | data formatting | bytes 8388608 | tf_op jit(solution)/shard_map/reshape | solution.py:111
  311.4 10.1 %fusion.51 = (bf16[4096,1,256]{2,1,0:T(2,128)(2,1)}, bf16[4096,1,256]{2,1,0:T(2,128)(2,1)}) fusion(bf16[4096,2,256]{2,1,0:T(2,128)(2,1)} %param.24), kind=kLoop, calls=%fused_computation.100 | loop fusion | bytes 8388608 | tf_op jit(solution)/shard_map/slice | solution.py:113
  321.5 9.7 %copy.121 = bf16[4096,1,256]{0,2,1:T(8,128)(2,1)} copy(bf16[4096,1,256]{2,1,0:T(2,128)(2,1)} %get-tuple-element.357) | data formatting | bytes 4194304
  331.2 10.1 %copy.114 = bf16[4096,2,128,1]{2,3,1,0:T(2,128)(2,1)} copy(bf16[4096,2,128,1]{0,2,1,3:T(8,128)(2,1)} %bitcast.93) | data formatting | bytes 4194304 | tf_op jit(solution)/shard_map/reshape;squeeze | solution.py:112
  341.4 10.9 %fusion.53 = f32[4096,2,1,2]{3,2,1,0:T(1,128)S(1)} fusion(bf16[4096,2,2,128]{3,2,1,0:T(2,128)(2,1)} %reshape.198, bf16[4096,2,128,1]{2,3,1,0:T(2,128)(2,1)} %copy.114), kind=kOutput, calls=%fused_computation.102 | convolution fusion | flops 4194304 | bytes 6356992 | tf_op jit(solution)/shard_map/skgd,skd->skg/dot_general | solution.py:114
  352.2 14.4 %multiply_select_fusion = f32[4096,2,2]{2,1,0:T(2,128)S(1)} fusion(f32[4096,2,2]{2,1,0:T(2,128)S(1)} %bitcast.89, pred[4096]{0:T(1024)(128)(4,1)S(1)} %broadcast_compare_fusion), kind=kLoop, calls=%fused_computation.27 | loop fusion | flops 32768 | bytes 135168 | tf_op jit(solution)/shard_map/jit(_where)/select_n | solution.py:116
  366.7 4.5 fusion.52
  371.2 2.2 copy.96
  373.4 2.2 copy.97
  375.6 2.7 select_reduce_fusion.1
  378.5 28.6 %gather_fusion.4 = f32[4096,2,2]{2,1,0:T(2,128)} fusion(f32[128,2,2]{2,1,0:T(2,128)S(1)} %copy.98, s32[4096]{0:T(1024)S(1)} %broadcast_clamp_fusion.1), kind=kCustom, calls=%fused_computation.4 | custom fusion | bytes 147456 | tf_op jit(solution)/shard_map/gather | solution.py:122
  407.1 16.7 %exponential_select_fusion = f32[4096,2,2]{2,1,0:T(2,128)S(1)} fusion(f32[4096,2,2]{2,1,0:T(2,128)} %gather_fusion.4, pred[4096]{0:T(1024)(128)(4,1)S(1)} %broadcast_compare_fusion, f32[4096,2,2]{2,1,0:T(2,128)} %bitcast.90), kind=kLoop, calls=%fused_computation.24 | loop fusion | flops 65536 | bytes 200704 | tf_op jit(solution)/shard_map/jit(_where)/select_n | solution.py:122
  423.8 4.9 fusion.50
  428.7 2.2 copy.101
  430.9 2.9 copy.100
  433.8 9.8 %copy.122 = bf16[4096,1,256]{0,2,1:T(8,128)(2,1)} copy(bf16[4096,1,256]{2,1,0:T(2,128)(2,1)} %get-tuple-element.356) | data formatting | bytes 4194304
  443.5 2.2 copy.104
  445.8 4.0 fusion.14
  449.8 4.0 fusion.17
  454.6 5.2 copy.99
  460.9 18.5 %all-gather.1 = f32[1024,2,2]{0,2,1:T(2,128)S(1)} all-gather(f32[128,2,2]{0,2,1:T(2,128)S(1)} %fusion.12), channel_id=3, replica_groups=mesh['req'=8,'tp'=4] {'req'}, dimensions={0}, use_global_device_ids=true | all-gather | bytes 18432 | tf_op jit(solution)/shard_map/all_gather | solution.py:17
  479.4 16.9 %all-gather = f32[1024,2,2]{0,2,1:T(2,128)S(1)} all-gather(f32[128,2,2]{0,2,1:T(2,128)S(1)} %pad_maximum_fusion.6), channel_id=2, replica_groups=mesh['req'=8,'tp'=4] {'req'}, dimensions={0}, use_global_device_ids=true | all-gather | bytes 18432 | tf_op jit(solution)/shard_map/all_gather | solution.py:17
  496.3 1.5 fusion.44
  498.3 1.5 convert_convert_fusion
  499.9 2.9 all-gather.5.cloned.1.call-done
  504.0 17.0 %while.43 = (s32[]{:T(128)}, f32[128,2,2]{0,2,1:T(2,128)S(1)}, f32[128,2,2]{0,2,1:T(2,128)S(1)}, f32[128,2,2,128]{3,2,1,0:T(2,128)S(1)}, f32[8,128,2,2]{1,0,3,2:...) while((s32[]{:T(128)}, f32[128,2,2]{0,2,1:T(2,128)S(1)}, ...), condition=%wide.region_7.8_spmd, body=%wide.region_6.7_spmd.sunk | while | flops 199685 | bytes 1347735 | solution.py:22
  522.7 30.0 %all-reduce.4.cloned.1.call-done = f32[16,2048]{1,0:T(8,128)} async-done(((f32[16,2048]{1,0:T(8,128)}), f32[16,2048]{1,0:T(8,128)}) %all-reduce.4.cloned.1.call-update) | async-done | bytes 131088 | tf_op jit(solution)/shard_map/psum | solution.py:161
  554.7 2.8 fusion.55
  557.6 5.4 fusion.21
  563.6 30.9 %all-reduce.6.cloned.1.call-done = f32[16,2048]{1,0:T(8,128)} async-done(((f32[16,2048]{1,0:T(8,128)}), f32[16,2048]{1,0:T(8,128)}) %all-reduce.6.cloned.1.call-update) | async-done | bytes 131088 | tf_op jit(solution)/shard_map/psum | solution.py:167
  594.5 1.6 fusion.32
  (151 shorter events, 30.5 us)
Async XLA Ops:
  7.2 514.4 %copy-start = (bf16[512,2048]{1,0:T(8,128)(2,1)S(1)}, bf16[512,2048]{1,0:T(8,128)(2,1)}, u32[]{:S(2)}) copy-start(bf16[512,2048]{1,0:T(8,128)(2,1)} %param.29) | copy-start | bytes 6291460
  7.2 495.6 %all-gather.5.cloned.1.call-start = ((), (), s32[]{:S(2)}) async-start(), calls=%async_computation.2 | async-start | bytes 2359296 | tf_op jit(solution)/shard_map/all_gather | solution.py:17
  258.7 0.7 copy-start.1
  331.2 10.1 %copy-start.6 = (s32[4096]{0:T(1024)S(1)}, s32[4096]{0:T(1024)}, u32[]{:S(2)}) copy-start(s32[4096]{0:T(1024)} %param.23) | copy-start | bytes 49156
  352.2 14.5 %copy-start.3 = (f32[4096,2,1,2]{3,2,1,0:T(1,128)}, f32[4096,2,1,2]{3,2,1,0:T(1,128)S(1)}, u32[]{:S(2)}) copy-start(f32[4096,2,1,2]{3,2,1,0:T(1,128)S(1)} %fusion.53) | copy-start | bytes 196612
  423.8 4.9 copy-start.2
  449.8 46.5 %copy-start.4 = (bf16[16,2048]{1,0:T(8,128)(2,1)S(1)}, bf16[16,2048]{1,0:T(8,128)(2,1)}, u32[]{:S(2)}) copy-start(bf16[16,2048]{1,0:T(8,128)(2,1)} %param.19) | copy-start | bytes 196612
  454.5 98.1 %all-reduce.4.cloned.1.call-start = ((), (), s32[]{:S(2)}) async-start(), calls=%async_computation | async-start | bytes 262144 | tf_op jit(solution)/shard_map/psum | solution.py:161
  504.0 18.7 %copy-start.7 = (bf16[2048]{0:T(1024)(128)(2,1)S(1)}, bf16[2048]{0:T(1024)(128)(2,1)}, u32[]{:S(2)}) copy-start(bf16[2048]{0:T(1024)(128)(2,1)} %param.30) | copy-start | bytes 12292
  522.6 71.9 %all-reduce.6.cloned.1.call-start = ((), (), s32[]{:S(2)}) async-start(), calls=%async_computation.1 | async-start | bytes 262144 | tf_op jit(solution)/shard_map/psum | solution.py:167
  557.6 37.0 %copy-start.5 = (f32[16,2048]{1,0:T(8,128)S(1)}, f32[16,2048]{1,0:T(8,128)}, u32[]{:S(2)}) copy-start(f32[16,2048]{1,0:T(8,128)} %all-reduce.4.cloned.1.call-done) | copy-start | bytes 393220
Sparse Core Ops, SparseCore 0:
  454.7 48.1 all-gather.4
  522.8 29.8 all-reduce.3
  563.1 31.4 all-reduce.5
where the time goes:
time: 605 us; the launch traced here: 603 us
  local copies, waits for them, and re-layouts  357 us (59%)
  blocking collectives  78.4 us (13%)
  waiting for transfers between devices  63.9 us (11%)
  other arithmetic  53.1 us (9%)
  matrix products  34.4 us (6%)
  between operations  14.8 us (2%)
    gather x8, local copies, waits for them, and re-layouts, per_device(): place = jnp.searchsorted(ends, slot_ids, side='right')  198 us
    all_gather x2, blocking collectives, joined(): gathered = jax.tree.map(lambda a: lax.all_gather(a, axis), part)  35.3 us
    all_gather x1, blocking collectives, per_device(): lax.all_gather(query.reshape(count, q_local * head_dim), 'req', axis=0, t...  32.3 us
    psum x1, waiting for transfers between devices, per_device(): hidden_out = mid + lax.psum(down_part, 'tp')  30.9 us
    psum x1, waiting for transfers between devices, per_device(): mid = rows + lax.psum(partial_attn, 'tp')  30 us
    gather x1, local copies, waits for them, and re-layouts, per_device(): weights = jnp.where(live, jnp.exp(scores - peak[owner]), 0.0)  28.6 us
    gather x1, local copies, waits for them, and re-layouts, per_device(): owner = pool_order[place]  24.7 us
    unnamed x23, local copies, waits for them, and re-layouts  22.9 us
  transfers between devices with their start and end apart: 3, of which 3 were waited for; matrix products, arithmetic and copies ran while one was open for 2% of the time, Pallas kernels for 0%

commit v1 on v0

v1 whole, which is shorter than its diff:
```python
import math

import jax
import jax.numpy as jnp
from jax import lax
from jax.experimental import pallas as pl
from jax.experimental.pallas import tpu as pltpu
from jax.sharding import PartitionSpec as P

HEAD_DIM = 128
ROPE_BASE = 1000000.0
EPS = 1e-05
FLOOR = -1e30
LOWEST = -1e29
LOG2E = 1.4426950408889634
TILE = 256
SUB = 128
WIN = 8
F32 = jnp.float32
BF16 = jnp.bfloat16
VMEM = pltpu.VMEM


def mm(a, b, dims=((1,), (0,))):
    return lax.dot_general(a, b, (dims, ((), ())), preferred_element_type=F32)


def norm_rows(rows, gain):
    mean_sq = jnp.mean(rows * rows, axis=-1, keepdims=True)
    return (rows * lax.rsqrt(mean_sq + EPS) * gain.astype(F32)).astype(BF16)


def project_kernel(tokens_ref, gain_ref, cos_ref, sin_ref, len_ref, wq_ref, wk_ref, wv_ref, msg_ref, kv_ref):
    normed = norm_rows(tokens_ref[...].astype(F32), gain_ref[...])
    cosine = cos_ref[...]
    sine = sin_ref[...]

    def rope(x):
        return x * cosine + pltpu.roll(x, HEAD_DIM // 2, 1) * sine

    q = mm(normed, wq_ref[...])
    width = q.shape[1]
    for low in range(0, width, HEAD_DIM):
        msg_ref[:, low : low + HEAD_DIM] = rope(q[:, low : low + HEAD_DIM]).astype(BF16)
    msg_ref[:, width:] = len_ref[...]
    k = mm(normed, wk_ref[...])
    half = k.shape[1]
    for low in range(0, half, HEAD_DIM):
        kv_ref[:, low : low + HEAD_DIM] = rope(k[:, low : low + HEAD_DIM])
    kv_ref[:, half:] = mm(normed, wv_ref[...])


def attend_kernel(
    base_ref, msg_ref, order_ref, live_ref, cache_ref, out_ref,
    queries, starts, ends, slots, top, total, summed, ranks, ranks_s, sem,
):
    reqs = msg_ref.shape[0]
    width = msg_ref.shape[1] - HEAD_DIM
    heads = width // HEAD_DIM
    kv_heads = slots.shape[0]
    group = heads // kv_heads
    per_slot = 2 * kv_heads
    tiles = cache_ref.shape[0] // (per_slot * TILE)
    span = TILE * per_slot
    sub_lanes = SUB * per_slot
    factor = LOG2E / math.sqrt(HEAD_DIM)
    base = base_ref[0].astype(F32)

    row = lax.broadcasted_iota(jnp.int32, (reqs, reqs), 0)
    col = lax.broadcasted_iota(jnp.int32, (reqs, reqs), 1)
    place = (order_ref[...] == row).astype(F32).astype(BF16)
    msg = msg_ref[...]
    sorted_msg = mm(place, msg, ((0,), (0,)))
    for h in range(heads):
        queries[h, 0:reqs, :] = sorted_msg[:, h * HEAD_DIM : (h + 1) * HEAD_DIM]
        queries[h, reqs:, :] = jnp.zeros((WIN, HEAD_DIM), F32)
    parts = sorted_msg[:, width:].astype(BF16)
    lane = lax.broadcasted_iota(jnp.int32, (reqs, HEAD_DIM), 1)
    high_half = lane < HEAD_DIM // 2

    def joined(counts):
        turned = pltpu.roll(counts, HEAD_DIM // 2, 1)
        return jnp.where(high_half, 128.0 * counts + turned, counts + 128.0 * turned)

    upto = joined(mm((col <= row).astype(F32).astype(BF16), parts)) - base
    before = joined(mm((col < row).astype(F32).astype(BF16), parts)) - base
    far = jnp.full((WIN, HEAD_DIM), 1e9, F32)
    ends[0:reqs, :] = upto
    ends[reqs:, :] = far
    starts[0:reqs, :] = before
    starts[reqs:, :] = far
    edge = (lane * TILE).astype(F32)
    first = jnp.sum((upto <= edge).astype(F32), axis=0, keepdims=True)
    last = jnp.sum((upto <= edge + (TILE - 1)).astype(F32), axis=0, keepdims=True)
    ranks[0:1, :] = first.astype(jnp.int32)
    ranks[1:2, :] = last.astype(jnp.int32)
    copy = pltpu.make_async_copy(ranks, ranks_s, sem)
    copy.start()

    blocks = live_ref.shape[0]
    out_lane = lax.broadcasted_iota(jnp.int32, (SUB, sub_lanes), 1)
    in_row = lax.broadcasted_iota(jnp.int32, (SUB, sub_lanes), 0)
    widen = (out_lane // per_slot == in_row).astype(F32).astype(BF16)
    alive = mm((live_ref[...] == 1).astype(F32).astype(BF16), widen) > 0.5
    lane_b = lax.broadcasted_iota(jnp.int32, (blocks, sub_lanes), 1)
    row_b = lax.broadcasted_iota(jnp.int32, (blocks, sub_lanes), 0)
    slot = (row_b * SUB + lane_b // per_slot).astype(F32)
    for c in range(kv_heads):
        slots[c, :, :] = jnp.where(alive & (lane_b % per_slot == 2 * c), slot, -1e9)

    top[...] = jnp.full(top.shape, LOWEST, F32)
    total[...] = jnp.zeros(total.shape, F32)
    summed[...] = jnp.zeros(summed.shape, F32)
    copy.wait()

    def part(tile, rank):
        q = jnp.concatenate(
            [queries[h, pl.ds(rank, WIN), :] for h in range(heads)], axis=0
        ).astype(BF16)
        low = starts[pl.ds(rank, WIN), :][:, 0:1]
        high = ends[pl.ds(rank, WIN), :][:, 0:1]
        chunk = cache_ref[pl.ds(tile * span, span), :]
        scores = mm(q, chunk, ((1,), (1,)))
        masks = []
        for c in range(kv_heads):
            at = jnp.concatenate(
                [slots[c, pl.ds(tile * (TILE // SUB) + i, 1), :] for i in range(TILE // SUB)], axis=1
            )
            masks.append((at >= low) & (at < high))
        masked = jnp.concatenate(
            [
                jnp.where(masks[h // group], scores[h * WIN : (h + 1) * WIN, :] * factor, FLOOR)
                for h in range(heads)
            ],
            axis=0,
        )
        peak = jnp.maximum(jnp.max(masked, axis=1, keepdims=True), LOWEST)
        weight = jnp.exp2(masked - peak)
        count = jnp.sum(weight, axis=1, keepdims=True)
        moved = jnp.concatenate(
            [pltpu.roll(weight[:, i : i + HEAD_DIM], 1, 1) for i in range(0, span, HEAD_DIM)], axis=1
        ).astype(BF16)
        return peak, count, mm(moved, chunk)

    def merge(rank, found):
        peak, count, value = found
        for h in range(heads):
            at = (h, pl.ds(rank, WIN), slice(None))
            rows = slice(h * WIN, (h + 1) * WIN)
            old = top[at]
            new = jnp.maximum(old, peak[rows, :])
            left = jnp.exp2(old - new)
            right = jnp.exp2(peak[rows, :] - new)
            top[at] = new
            total[at] = total[at] * left + count[rows, :] * right
            summed[at] = summed[at] * left + value[rows, :] * right

    for low in range(0, tiles, 4):
        some = range(low, min(low + 4, tiles))
        found = [part(t, ranks_s[0, t]) for t in some]
        for t, got in zip(some, found):
            merge(ranks_s[0, t], got)

    def more(t, carry):
        begin = ranks_s[0, t]

        def again(i, inner):
            rank = begin + (i + 1) * WIN
            merge(rank, part(t, rank))
            return inner

        return lax.fori_loop(0, (ranks_s[1, t] - begin) // WIN, again, carry)

    lax.fori_loop(0, tiles, more, 0)

    columns = []
    extra = jnp.zeros((reqs, HEAD_DIM), F32)
    for h in range(heads):
        sums = total[h, 0:reqs, :]
        some = sums > 0.0
        safe = jnp.where(some, sums, 1.0)
        columns.append((summed[h, 0:reqs, :] / safe).astype(BF16))
        rest = jnp.where(some, top[h, 0:reqs, :] + jnp.log2(safe), LOWEST)
        for piece in range(3):
            coded = rest.astype(BF16).astype(F32)
            extra = jnp.where(lane == piece * heads + h, coded, extra)
            rest = rest - coded
    both = jnp.concatenate(columns + [extra.astype(BF16)], axis=1)
    out_ref[...] = mm(place, both).astype(BF16)


def output_kernel(parts_ref, msg_ref, kv_ref, w_ref, out_ref):
    sources, count, wide = parts_ref.shape
    width = wide - HEAD_DIM
    heads = width // HEAD_DIM
    half = kv_ref.shape[1] // 2
    group = heads // (half // HEAD_DIM)
    factor = LOG2E / math.sqrt(HEAD_DIM)
    levels = []
    for r in range(sources):
        e = parts_ref[r, :, width:].astype(F32)
        levels.append(
            e + (pltpu.roll(e, HEAD_DIM - heads, 1) + pltpu.roll(e, HEAD_DIM - 2 * heads, 1))
        )
    context = []
    for h in range(heads):
        at = slice(h * HEAD_DIM, (h + 1) * HEAD_DIM)
        low = (h // group) * HEAD_DIM
        key = kv_ref[:, low : low + HEAD_DIM].astype(BF16).astype(F32)
        value = kv_ref[:, half + low : half + low + HEAD_DIM].astype(BF16).astype(F32)
        own = jnp.sum(msg_ref[:, at].astype(F32) * key, axis=1, keepdims=True) * factor
        cols = [level[:, h : h + 1] for level in levels]
        peak = own
        for c in cols:
            peak = jnp.maximum(peak, c)
        weight = jnp.exp2(own - peak)
        denom = weight
        numer = weight * value
        for r in range(sources):
            weight = jnp.exp2(cols[r] - peak)
            denom = denom + weight
            numer = numer + weight * parts_ref[r, :, at].astype(F32)
        context.append((numer / denom).astype(BF16))
    out_ref[...] = mm(jnp.concatenate(context, axis=1), w_ref[...]).astype(BF16)


def feed_kernel(tokens_ref, here_ref, there_ref, gain_ref, wg_ref, wu_ref, wd_ref, part_ref, mid_ref):
    mid = tokens_ref[...].astype(F32) + (here_ref[...].astype(F32) + there_ref[...].astype(F32))
    mid_ref[...] = mid
    normed = norm_rows(mid, gain_ref[...])
    gate = mm(normed, wg_ref[...])
    upper = mm(normed, wu_ref[...])
    act = (gate / (1.0 + jnp.exp(-gate)) * upper).astype(BF16)
    part_ref[...] = mm(act, wd_ref[...]).astype(BF16)


def swap(x, axis, distance):
    return lax.ppermute(x, axis, [(i, i ^ distance) for i in range(lax.axis_size(axis))])


def pair_sum(x):
    size = lax.axis_size("tp")
    distance = 1
    while distance * 2 < size:
        x = (x.astype(F32) + swap(x, "tp", distance).astype(F32)).astype(BF16)
        distance *= 2
    return x, swap(x, "tp", distance)


def per_device(
    tokens, lengths, pool_order, positions, slot_mask, kv_cache, attn_gain,
    w_query, w_key, w_value, w_out, ffn_gain, w_gate, w_up, w_down,
):
    count, model = tokens.shape
    nreq = lax.axis_size("req")
    reqs = count * nreq
    slot_count = kv_cache.shape[0]
    width = w_query.shape[1]
    half = w_key.shape[1]
    kv_heads = half // HEAD_DIM
    wide = width + HEAD_DIM
    assert slot_count % TILE == 0 and slot_count // TILE <= HEAD_DIM

    index = jnp.arange(HEAD_DIM, dtype=jnp.int32)
    pair = (index % (HEAD_DIM // 2)).astype(F32)
    freq = ROPE_BASE ** (-(pair * 2.0) / HEAD_DIM)
    angle = positions.astype(F32)[:, None] * freq[None, :]
    cosine = jnp.cos(angle)
    sine = jnp.where(index < HEAD_DIM // 2, -1.0, 1.0)[None, :] * jnp.sin(angle)
    coded = jnp.where(
        index[None, :] < HEAD_DIM // 2, lengths[:, None] >> 7, lengths[:, None] & 127
    ).astype(BF16)

    msg, new_kv = pl.pallas_call(
        project_kernel,
        out_shape=(
            jax.ShapeDtypeStruct((count, wide), BF16),
            jax.ShapeDtypeStruct((count, 2 * half), F32),
        ),
        compiler_params=pltpu.CompilerParams(vmem_limit_bytes=16 << 20),
        name="project",
    )(tokens, attn_gain.reshape(1, model), cosine, sine, coded, w_query, w_key, w_value)

    everyone = lax.all_to_all(jnp.broadcast_to(msg, (nreq, count, wide)), "req", 0, 0)
    everyone = everyone.reshape(reqs, wide)

    cache = kv_cache.reshape(slot_count, 2, kv_heads, HEAD_DIM).transpose(0, 2, 1, 3)
    cache = cache.reshape(slot_count * 2 * kv_heads, HEAD_DIM)
    live = slot_mask.reshape(slot_count // SUB, SUB)
    base = (lax.axis_index("req") * slot_count).astype(jnp.int32).reshape(1)
    rows = reqs + WIN
    per_head = (width // HEAD_DIM, rows, HEAD_DIM)
    parts = pl.pallas_call(
        attend_kernel,
        out_shape=jax.ShapeDtypeStruct((reqs, wide), BF16),
        in_specs=[pl.BlockSpec(memory_space=pltpu.SMEM)] + [pl.BlockSpec(memory_space=VMEM)] * 4,
        out_specs=pl.BlockSpec(memory_space=VMEM),
        scratch_shapes=[
            VMEM(per_head, F32),
            VMEM((rows, HEAD_DIM), F32),
            VMEM((rows, HEAD_DIM), F32),
            VMEM((kv_heads, slot_count // SUB, SUB * 2 * kv_heads), F32),
            VMEM(per_head, F32),
            VMEM(per_head, F32),
            VMEM(per_head, F32),
            VMEM((8, HEAD_DIM), jnp.int32),
            pltpu.SMEM((8, HEAD_DIM), jnp.int32),
            pltpu.SemaphoreType.DMA,
        ],
        compiler_params=pltpu.CompilerParams(vmem_limit_bytes=24 << 20),
        name="attend",
    )(base, everyone, pool_order.reshape(1, reqs), live, cache)

    mine = lax.all_to_all(parts.reshape(nreq, count, wide), "req", 0, 0)

    partial_attn = pl.pallas_call(
        output_kernel,
        out_shape=jax.ShapeDtypeStruct((count, model), BF16),
        compiler_params=pltpu.CompilerParams(vmem_limit_bytes=16 << 20),
        name="output",
    )(mine, msg, new_kv, w_out)

    here, there = pair_sum(partial_attn)
    down_part, mid = pl.pallas_call(
        feed_kernel,
        out_shape=(
            jax.ShapeDtypeStruct((count, model), BF16),
            jax.ShapeDtypeStruct((count, model), F32),
        ),
        compiler_params=pltpu.CompilerParams(vmem_limit_bytes=20 << 20),
        name="feed",
    )(tokens, here, there, ffn_gain.reshape(1, model), w_gate, w_up, w_down)

    here, there = pair_sum(down_part)
    hidden_out = mid + (here.astype(F32) + there.astype(F32))
    return (hidden_out, new_kv.reshape(count, 2, half))


def solution(mesh):
    placed = (
        P("req", None),
        P("req"),
        P(),
        P("req"),
        P("req"),
        P("req", None, "tp"),
        P(),
        P(None, "tp"),
        P(None, "tp"),
        P(None, "tp"),
        P("tp", None),
        P(),
        P(None, "tp"),
        P(None, "tp"),
        P("tp", None),
    )
    return jax.shard_map(
        per_device,
        mesh=mesh,
        in_specs=placed,
        out_specs=(P("req", None), P("req", None, "tp")),
        check_vma=False,
    )
```

time: 605 us -> 64 us (0.11)
  local copies, waits for them, and re-layouts: 357 us -> 13.5 us
  blocking collectives: 78.4 us -> 10.2 us
  other arithmetic: 53.1 us -> 2.23 us
  waiting for transfers between devices: 63.9 us -> 15 us
  matrix products: 34.4 us -> 0 us
  between operations: 14.8 us -> 0.7 us
  Pallas kernels: 0 us -> 11.4 us
  starting transfers between devices: 0.12 us -> 10.4 us
    gather x12 -> x0, local copies, waits for them, and re-layouts: 269 us -> none  [the longest x8 198 us: per_device(): place = jnp.searchsorted(ends, slot_ids, side='right')]
    all_gather x3 -> x0, blocking collectives: 67.6 us -> none  [the longest x2 35.3 us: joined(): gathered = jax.tree.map(lambda a: lax.all_gather(a, axis), part)]
    psum x2 -> x0, waiting for transfers between devices: 60.9 us -> none  [the longest x1 30.9 us: per_device(): hidden_out = mid + lax.psum(down_part, 'tp')]
    dot_general x11 -> x0, matrix products: 34.4 us -> none  [the longest x1 10.9 us: per_device(): jnp.einsum('skgd,skd->skg', picked, keys, preferred_element_type=jnp.floa...]
    select_n x20 -> x0, other arithmetic: 32 us -> none  [the longest x1 16.7 us: per_device(): weights = jnp.where(live, jnp.exp(scores - peak[owner]), 0.0)]
    slice x3 -> x0, local copies, waits for them, and re-layouts: 19.5 us -> none  [the longest x1 10.1 us: per_device(): values = kv_cache[:, 1, :].reshape(slot_count, kv_local, head_dim)]
    unnamed x23 -> x26, local copies, waits for them, and re-layouts: 22.9 us -> 11.5 us
    pallas_call x0 -> x4, Pallas kernels: none -> 11.4 us  [the longest x1 8.08 us: per_device(): pl.pallas_call(attend_kernel, out_shape=jax.ShapeDtypeStruct((reqs, wide)...]
  transfers between devices with their start and end apart: 3 -> 5, of which waited for: 3 -> 5; matrix products, arithmetic and copies ran while one was open for 2% -> 1% of each run, Pallas kernels for 0% -> 0%
where the time goes in v1:
time: 64 us; the launch traced here: 63.3 us
  waiting for transfers between devices  15 us (23%)
  local copies, waits for them, and re-layouts  13.5 us (21%)
  Pallas kernels  11.4 us (18%)
  starting transfers between devices  10.4 us (16%)
  blocking collectives  10.2 us (16%)
  other arithmetic  2.23 us (3%)
  between operations  0.7 us (1%)
    unnamed x26, local copies, waits for them, and re-layouts  11.5 us
    all_to_all x1, blocking collectives, per_device(): mine = lax.all_to_all(parts.reshape(nreq, count, wide), 'req', 0, 0)  10.2 us
    pallas_call x1, Pallas kernels, per_device(): pl.pallas_call(attend_kernel, out_shape=jax.ShapeDtypeStruct((reqs, wide)...  8.08 us
    all_to_all x1, waiting for transfers between devices, per_device(): lax.all_to_all(jnp.broadcast_to(msg, (nreq, count, wide)), 'req', 0, 0)  7.56 us
    ppermute x4, waiting for transfers between devices, swap(): lax.ppermute(x, axis, [(i, i ^ distance) for i in range(lax.axis_size(axi...  7.43 us
    all_to_all x1, starting transfers between devices, per_device(): lax.all_to_all(jnp.broadcast_to(msg, (nreq, count, wide)), 'req', 0, 0)  7.28 us
    ppermute x4, starting transfers between devices, swap(): lax.ppermute(x, axis, [(i, i ^ distance) for i in range(lax.axis_size(axi...  3.11 us
    pallas_call x1, Pallas kernels, per_device(): pl.pallas_call(feed_kernel, out_shape=(jax.ShapeDtypeStruct((count, model...  1.85 us
  transfers between devices with their start and end apart: 5, of which 5 were waited for; matrix products, arithmetic and copies ran while one was open for 1% of the time, Pallas kernels for 0%

profile of v1, /device:TPU:0, one launch (start us, length us, event | category | flops | bytes accessed | tf_op | source)
XLA Modules:
  0.0 63.3 jit_solution(3461214565212541558)
XLA Ops:
  0.6 0.0 copy-start.11
  0.6 0.0 copy-start.10
  0.7 0.7 %convert_element_type.37 = f32[16]{0:T(128)S(1)} convert(s32[16]{0:T(128)} %param.18) | non-fusion elementwise | flops 16 | bytes 128 | tf_op jit(solution)/shard_map/convert_element_type | solution.py:267
  1.3 0.7 %broadcast_shift-right-arithmetic_fusion = (s32[16]{0:T(128)S(1)}, s32[16]{0:T(128)S(1)}) fusion(s32[16]{0:T(128)} %param.16), kind=kLoop, calls=%fused_computation.15 | loop fusion | flops 32 | bytes 192 | tf_op jit(solution)/shard_map/shift_right_arithmetic | solution.py:271
  2.0 0.7 %reshape.62.gain_ref = bf16[1,2048]{1,0:T(2,128)(2,1)S(1)} reshape(bf16[2048]{0:T(1024)(128)(2,1)} %param.21) | data formatting | bytes 8192 | tf_op jit(solution)/shard_map/reshape | solution.py:282
  2.7 0.1 fusion
  2.8 0.1 select_convert_fusion.len_ref
  2.9 0.0 copy-start.4
  2.9 1.6 %copy-done.4 = bf16[2048,512]{1,0:T(8,128)(2,1)S(1)} copy-done((bf16[2048,512]{1,0:T(8,128)(2,1)S(1)}, bf16[2048,512]{1,0:T(8,128)(2,1)}, u32[]{:S(2)}) %copy-start.4) | copy-done | bytes 2097176
  4.5 0.0 copy-start.6
  4.5 1.2 %copy-done.6 = bf16[2048,256]{1,0:T(8,128)(2,1)S(1)} copy-done((bf16[2048,256]{1,0:T(8,128)(2,1)S(1)}, bf16[2048,256]{1,0:T(8,128)(2,1)}, u32[]{:S(2)}) %copy-start.6) | copy-done | bytes 1048600
  5.7 0.0 copy-start.7
  5.7 1.2 %copy-done.7 = bf16[2048,256]{1,0:T(8,128)(2,1)S(1)} copy-done((bf16[2048,256]{1,0:T(8,128)(2,1)S(1)}, bf16[2048,256]{1,0:T(8,128)(2,1)}, u32[]{:S(2)}) %copy-start.7) | copy-done | bytes 1048600
  6.9 0.0 copy-start.8
  6.9 0.8 %copy-done.8 = bf16[16,2048]{1,0:T(8,128)(2,1)S(1)} copy-done((bf16[16,2048]{1,0:T(8,128)(2,1)S(1)}, bf16[16,2048]{1,0:T(8,128)(2,1)}, u32[]{:S(2)}) %copy-start.8) | copy-done | bytes 65560
  7.8 0.0 copy-start.5
  7.8 0.8 %project.1 = (bf16[16,640]{1,0:T(8,128)(2,1)S(1)}, f32[16,512]{1,0:T(8,128)S(1)}) custom-call(bf16[16,2048]{1,0:T(8,128)(2,1)S(1)} %copy-done.8, bf16[1,2048]{1,0:T(2,128)(2,1)S(1)} %reshape.62.gain_ref, f32[16,128]{1,0:T(8,128)S(1)} %get-tuple-element.11.cos_ref, f32[16,128]{1,0:T(8,128)S(1)} %get-tuple-element.10.sin_ref, ...), custom_call_target="tpu_custom_call" | custom-call | tf_op jit(solution)/shard_map/project/pallas_call | solution.py:274
  8.6 0.0 copy-start.12
  8.6 0.0 copy-start.9
  8.6 0.7 %broadcast_in_dim.46 = bf16[8,16,640]{2,1,0:T(8,128)(2,1)} broadcast(bf16[16,640]{1,0:T(8,128)(2,1)S(1)} %get-tuple-element.6.msg_ref), dimensions={1,2} | broadcast | bytes 184320 | tf_op jit(solution)/shard_map/broadcast_in_dim | solution.py:284
  9.2 7.3 %all-to-all-start = ((bf16[8,16,640]{2,1,0:T(8,128)(2,1)}), bf16[8,16,640]{2,1,0:T(8,128)(2,1)S(1)}, u32[]{:S(2)}, u32[]{:S(2)}) async-start(bf16[8,16,640]{2,1,0:T(8,128)(2,1)} %broadcast_in_dim.46), calls=%async_computation | async-start | bytes 327680 | tf_op jit(solution)/shard_map/all_to_all | solution.py:284
  16.5 7.6 %all-to-all-done = bf16[8,16,640]{2,1,0:T(8,128)(2,1)S(1)} async-done(((bf16[8,16,640]{2,1,0:T(8,128)(2,1)}), bf16[8,16,640]{2,1,0:T(8,128)(2,1)S(1)}, u32[]{:S(2)}, u32[]{:S(2)}) %all-to-all-start) | async-done | bytes 163872 | tf_op jit(solution)/shard_map/all_to_all | solution.py:284
  24.1 0.0 copy-done.11
  24.1 0.0 copy-done.10
  24.1 0.0 copy-start
  24.1 2.2 %copy-done = bf16[4096,2,256]{2,1,0:T(2,128)(2,1)S(1)} copy-done((bf16[4096,2,256]{2,1,0:T(2,128)(2,1)S(1)}, bf16[4096,2,256]{2,1,0:T(2,128)(2,1)}, u32[]{:S(2)}) %copy-start) | copy-done | bytes 4194328
  26.3 0.0 copy-start.1
  26.3 8.1 %attend.1 = bf16[128,640]{1,0:T(8,128)(2,1)S(1)} custom-call(s32[1]{0:T(128)} %bitcast.base_ref, bf16[128,640]{1,0:T(8,128)(2,1)S(1)} %bitcast.11, s32[1,128]{1,0:T(1,128)S(1)} %bitcast.14, s32[32,128]{1,0:T(8,128)S(1)} %bitcast.13, bf16[16384,128]{1,0:T(8,128)(2,1)S(1)} %bitcast.10), custom_call_target="tpu_custom_call" | custom-call | tf_op jit(solution)/shard_map/attend/pallas_call | solution.py:293
  34.4 10.2 %all_to_all.10.parts_ref = bf16[8,16,640]{2,1,0:T(8,128)(2,1)S(1)} all-to-all(bf16[8,16,640]{2,1,0:T(8,128)(2,1)S(1)} %bitcast.12), channel_id=1, replica_groups=mesh['req'=8,'tp'=4] {'req'}, dimensions={0} | all-to-all | bytes 327680 | tf_op jit(solution)/shard_map/all_to_all | solution.py:314
  44.6 0.0 copy-done.5
  44.6 0.6 %output.1 = bf16[16,2048]{1,0:T(8,128)(2,1)S(1)} custom-call(bf16[8,16,640]{2,1,0:T(8,128)(2,1)S(1)} %all_to_all.10.parts_ref, bf16[16,640]{1,0:T(8,128)(2,1)S(1)} %get-tuple-element.6.msg_ref, f32[16,512]{1,0:T(8,128)S(1)} %get-tuple-element.7.kv_ref, bf16[512,2048]{1,0:T(8,128)(2,1)S(1)} %copy-done.5), custom_call_target="tpu_custom_call" | custom-call | tf_op jit(solution)/shard_map/output/pallas_call | solution.py:316
  45.2 0.0 collective-permute-start
  45.2 1.3 %collective-permute-done = bf16[16,2048]{1,0:T(8,128)(2,1)S(1)} collective-permute-done((bf16[16,2048]{1,0:T(8,128)(2,1)S(1)}, bf16[16,2048]{1,0:T(8,128)(2,1)S(1)}, u32[]{:S(2)}, u32[]{:S(2)}) %collective-permute-start) | collective-permute-done | bytes 65568 | tf_op jit(solution)/shard_map/ppermute | solution.py:238
  46.5 1.6 %collective-permute-start.1 = (bf16[16,2048]{1,0:T(8,128)(2,1)S(1)}, bf16[16,2048]{1,0:T(8,128)(2,1)S(1)}, u32[]{:S(2)}, u32[]{:S(2)}) collective-permute-start(bf16[16,2048]{1,0:T(8,128)(2,1)S(1)} %add_convert_fusion.1.here_ref), channel_id=1, source_target_pairs={{0,2},{1,3},{2,0},{3,1},{4,6},{5,7},{6,4},{7,5},{8,10},{9,11},{10,... | collective-permute-start | bytes 196616 | tf_op jit(solution)/shard_map/ppermute | solution.py:238
  48.0 0.0 copy-done.12
  48.1 2.8 %collective-permute-done.1.there_ref = bf16[16,2048]{1,0:T(8,128)(2,1)S(1)} collective-permute-done((bf16[16,2048]{1,0:T(8,128)(2,1)S(1)}, bf16[16,2048]{1,0:T(8,128)(2,1)S(1)}, u32[]{:S(2)}, u32[]{:S(2)}) %collective-permute-start.1) | collective-permute-done | bytes 65568 | tf_op jit(solution)/shard_map/ppermute | solution.py:238
  50.8 0.0 copy-done.9
  50.8 0.0 copy-done.1
  50.8 0.0 copy-start.2
  50.8 2.2 %copy-done.2 = bf16[2048,1024]{1,0:T(8,128)(2,1)S(1)} copy-done((bf16[2048,1024]{1,0:T(8,128)(2,1)S(1)}, bf16[2048,1024]{1,0:T(8,128)(2,1)}, u32[]{:S(2)}) %copy-start.2) | copy-done | bytes 4194328
  53.0 2.2 %copy-done.3 = bf16[1024,2048]{1,0:T(8,128)(2,1)S(1)} copy-done((bf16[1024,2048]{1,0:T(8,128)(2,1)S(1)}, bf16[1024,2048]{1,0:T(8,128)(2,1)}, u32[]{:S(2)}) %copy-start.3) | copy-done | bytes 4194328
  55.2 1.8 %feed.1 = (bf16[16,2048]{1,0:T(8,128)(2,1)S(1)}, f32[16,2048]{1,0:T(8,128)S(1)}) custom-call(bf16[16,2048]{1,0:T(8,128)(2,1)S(1)} %copy-done.9, bf16[16,2048]{1,0:T(8,128)(2,1)S(1)} %add_convert_fusion.1.here_ref, bf16[16,2048]{1,0:T(8,128)(2,1)S(1)} %collective-permute-done.1.there_ref, bf16[1,2048]{1,0:T(2,128)(2,1)S(1)} %reshape.69.gain_ref, ...), custom_call_target="tpu_custom_call" | custom-call | tf_op jit(solution)/shard_map/feed/pallas_call | solution.py:324
  57.0 0.0 collective-permute-start.2
  57.1 1.3 %collective-permute-done.2 = bf16[16,2048]{1,0:T(8,128)(2,1)S(1)} collective-permute-done((bf16[16,2048]{1,0:T(8,128)(2,1)S(1)}, bf16[16,2048]{1,0:T(8,128)(2,1)S(1)}, u32[]{:S(2)}, u32[]{:S(2)}) %collective-permute-start.2) | collective-permute-done | bytes 65568 | tf_op jit(solution)/shard_map/ppermute | solution.py:238
  58.3 1.6 %collective-permute-start.3 = (bf16[16,2048]{1,0:T(8,128)(2,1)S(1)}, bf16[16,2048]{1,0:T(8,128)(2,1)S(1)}, u32[]{:S(2)}, u32[]{:S(2)}) collective-permute-start(bf16[16,2048]{1,0:T(8,128)(2,1)S(1)} %add_convert_fusion), channel_id=1, source_target_pairs={{0,2},{1,3},{2,0},{3,1},{4,6},{5,7},{6,4},{7,5},{8,10},{9,11},{10,... | collective-permute-start | bytes 196616 | tf_op jit(solution)/shard_map/ppermute | solution.py:238
  59.9 0.6 %reshape.70 = f32[16,2,256]{2,1,0:T(2,128)} reshape(f32[16,512]{1,0:T(8,128)S(1)} %get-tuple-element.7.kv_ref) | data formatting | bytes 65536 | tf_op jit(solution)/shard_map/reshape | solution.py:336
  60.5 2.1 %collective-permute-done.3 = bf16[16,2048]{1,0:T(8,128)(2,1)S(1)} collective-permute-done((bf16[16,2048]{1,0:T(8,128)(2,1)S(1)}, bf16[16,2048]{1,0:T(8,128)(2,1)S(1)}, u32[]{:S(2)}, u32[]{:S(2)}) %collective-permute-start.3) | collective-permute-done | bytes 65568 | tf_op jit(solution)/shard_map/ppermute | solution.py:238
  62.7 0.7 %add_add_fusion = f32[16,2048]{1,0:T(8,128)} fusion(f32[16,2048]{1,0:T(8,128)S(1)} %get-tuple-element.8, bf16[16,2048]{1,0:T(8,128)(2,1)S(1)} %collective-permute-done.3, bf16[16,2048]{1,0:T(8,128)(2,1)S(1)} %add_convert_fusion), kind=kLoop, calls=%fused_computation | loop fusion | flops 131072 | bytes 393216 | tf_op jit(solution)/shard_map/add | solution.py:335
  (6 shorter events, 0.1 us)
Async XLA Ops:
  0.6 23.5 %copy-start.11 = (s32[128]{0:T(128)S(1)}, s32[128]{0:T(128)}, u32[]{:S(2)}) copy-start(s32[128]{0:T(128)} %param.17) | copy-start | bytes 1540
  0.6 23.5 %copy-start.10 = (s32[4096]{0:T(1024)S(1)}, s32[4096]{0:T(1024)}, u32[]{:S(2)}) copy-start(s32[4096]{0:T(1024)} %param.19) | copy-start | bytes 49156
  2.9 1.6 %copy-start.4 = (bf16[2048,512]{1,0:T(8,128)(2,1)S(1)}, bf16[2048,512]{1,0:T(8,128)(2,1)}, u32[]{:S(2)}) copy-start(bf16[2048,512]{1,0:T(8,128)(2,1)} %wq_ref.1) | copy-start | bytes 6291460
  4.5 1.2 %copy-start.6 = (bf16[2048,256]{1,0:T(8,128)(2,1)S(1)}, bf16[2048,256]{1,0:T(8,128)(2,1)}, u32[]{:S(2)}) copy-start(bf16[2048,256]{1,0:T(8,128)(2,1)} %wk_ref.1) | copy-start | bytes 3145732
  5.7 1.2 %copy-start.7 = (bf16[2048,256]{1,0:T(8,128)(2,1)S(1)}, bf16[2048,256]{1,0:T(8,128)(2,1)}, u32[]{:S(2)}) copy-start(bf16[2048,256]{1,0:T(8,128)(2,1)} %wv_ref.1) | copy-start | bytes 3145732
  6.9 0.8 %copy-start.8 = (bf16[16,2048]{1,0:T(8,128)(2,1)S(1)}, bf16[16,2048]{1,0:T(8,128)(2,1)}, u32[]{:S(2)}) copy-start(bf16[16,2048]{1,0:T(8,128)(2,1)} %tokens_ref.3) | copy-start | bytes 196612
  7.8 36.8 %copy-start.5 = (bf16[512,2048]{1,0:T(8,128)(2,1)S(1)}, bf16[512,2048]{1,0:T(8,128)(2,1)}, u32[]{:S(2)}) copy-start(bf16[512,2048]{1,0:T(8,128)(2,1)} %w_ref.1) | copy-start | bytes 6291460
  8.6 39.5 %copy-start.12 = (bf16[2048]{0:T(1024)(128)(2,1)S(1)}, bf16[2048]{0:T(1024)(128)(2,1)}, u32[]{:S(2)}) copy-start(bf16[2048]{0:T(1024)(128)(2,1)} %param.26) | copy-start | bytes 12292
  8.6 42.2 %copy-start.9 = (bf16[16,2048]{1,0:T(8,128)(2,1)S(1)}, bf16[16,2048]{1,0:T(8,128)(2,1)}, u32[]{:S(2)}) copy-start(bf16[16,2048]{1,0:T(8,128)(2,1)} %tokens_ref.3) | copy-start | bytes 196612
  9.2 14.8 %all-to-all-start = ((bf16[8,16,640]{2,1,0:T(8,128)(2,1)}), bf16[8,16,640]{2,1,0:T(8,128)(2,1)S(1)}, u32[]{:S(2)}, u32[]{:S(2)}) async-start(bf16[8,16,640]{2,1,0:T(8,128)(2,1)} %broadcast_in_dim.46), calls=%async_computation | async-start | bytes 327680 | tf_op jit(solution)/shard_map/all_to_all | solution.py:284
  24.1 2.2 %copy-start = (bf16[4096,2,256]{2,1,0:T(2,128)(2,1)S(1)}, bf16[4096,2,256]{2,1,0:T(2,128)(2,1)}, u32[]{:S(2)}) copy-start(bf16[4096,2,256]{2,1,0:T(2,128)(2,1)} %param.20) | copy-start | bytes 12582916
  26.3 24.5 %copy-start.1 = (bf16[2048,1024]{1,0:T(8,128)(2,1)S(1)}, bf16[2048,1024]{1,0:T(8,128)(2,1)}, u32[]{:S(2)}) copy-start(bf16[2048,1024]{1,0:T(8,128)(2,1)} %wg_ref.1) | copy-start | bytes 12582916
  45.2 1.3 %collective-permute-start = (bf16[16,2048]{1,0:T(8,128)(2,1)S(1)}, bf16[16,2048]{1,0:T(8,128)(2,1)S(1)}, u32[]{:S(2)}, u32[]{:S(2)}) collective-permute-start(bf16[16,2048]{1,0:T(8,128)(2,1)S(1)} %output.1), channel_id=1, source_target_pairs={{0,1},{1,0},{2,3},{3,2},{4,5},{5,4},{6,7},{7,6},{8,9},{9,8},{10,11... | collective-permute-start | bytes 196616 | tf_op jit(solution)/shard_map/ppermute | solution.py:238
  46.5 4.3 %collective-permute-start.1 = (bf16[16,2048]{1,0:T(8,128)(2,1)S(1)}, bf16[16,2048]{1,0:T(8,128)(2,1)S(1)}, u32[]{:S(2)}, u32[]{:S(2)}) collective-permute-start(bf16[16,2048]{1,0:T(8,128)(2,1)S(1)} %add_convert_fusion.1.here_ref), channel_id=1, source_target_pairs={{0,2},{1,3},{2,0},{3,1},{4,6},{5,7},{6,4},{7,5},{8,10},{9,11},{10,... | collective-permute-start | bytes 196616 | tf_op jit(solution)/shard_map/ppermute | solution.py:238
  50.8 2.2 %copy-start.2 = (bf16[2048,1024]{1,0:T(8,128)(2,1)S(1)}, bf16[2048,1024]{1,0:T(8,128)(2,1)}, u32[]{:S(2)}) copy-start(bf16[2048,1024]{1,0:T(8,128)(2,1)} %wu_ref.1) | copy-start | bytes 12582916
  53.0 2.2 %copy-start.3 = (bf16[1024,2048]{1,0:T(8,128)(2,1)S(1)}, bf16[1024,2048]{1,0:T(8,128)(2,1)}, u32[]{:S(2)}) copy-start(bf16[1024,2048]{1,0:T(8,128)(2,1)} %wd_ref.1) | copy-start | bytes 12582916
  57.0 1.3 %collective-permute-start.2 = (bf16[16,2048]{1,0:T(8,128)(2,1)S(1)}, bf16[16,2048]{1,0:T(8,128)(2,1)S(1)}, u32[]{:S(2)}, u32[]{:S(2)}) collective-permute-start(bf16[16,2048]{1,0:T(8,128)(2,1)S(1)} %get-tuple-element.9), channel_id=1, source_target_pairs={{0,1},{1,0},{2,3},{3,2},{4,5},{5,4},{6,7},{7,6},{8,9},{9,8},{10,11... | collective-permute-start | bytes 196616 | tf_op jit(solution)/shard_map/ppermute | solution.py:238
  58.3 4.3 %collective-permute-start.3 = (bf16[16,2048]{1,0:T(8,128)(2,1)S(1)}, bf16[16,2048]{1,0:T(8,128)(2,1)S(1)}, u32[]{:S(2)}, u32[]{:S(2)}) collective-permute-start(bf16[16,2048]{1,0:T(8,128)(2,1)S(1)} %add_convert_fusion), channel_id=1, source_target_pairs={{0,2},{1,3},{2,0},{3,1},{4,6},{5,7},{6,4},{7,5},{8,10},{9,11},{10,... | collective-permute-start | bytes 196616 | tf_op jit(solution)/shard_map/ppermute | solution.py:238

commit v2 on v1

v2 whole, which is shorter than its diff:
```python
import math

import jax
import jax.numpy as jnp
import numpy as np
from jax import lax
from jax.experimental import pallas as pl
from jax.experimental.pallas import tpu as pltpu
from jax.sharding import PartitionSpec as P

HEAD_DIM = 128
ROPE_BASE = 1000000.0
EPS = 1e-05
FLOOR = -1e30
LOWEST = -1e29
LOG2E = 1.4426950408889634
TILE = 256
SUB = 128
WIN = 8
PIECES = 4
SLAB = 1024
F32 = jnp.float32
BF16 = jnp.bfloat16
VMEM = pltpu.VMEM


def mm(a, b, dims=((1,), (0,))):
    return lax.dot_general(a, b, (dims, ((), ())), preferred_element_type=F32)


def norm_rows(rows, gain_ref):
    mean_sq = jnp.mean(rows * rows, axis=-1, keepdims=True)
    scaled = rows * lax.rsqrt(mean_sq + EPS)
    gain = gain_ref[...].astype(F32)
    blocks = [
        scaled[:, i * HEAD_DIM : (i + 1) * HEAD_DIM] * gain[i : i + 1, :] for i in range(gain.shape[0])
    ]
    return jnp.concatenate(blocks, axis=1).astype(BF16)


def column(row_ref, count):
    shape = (count, count)
    diagonal = lax.broadcasted_iota(jnp.int32, shape, 0) == lax.broadcasted_iota(jnp.int32, shape, 1)
    values = jnp.broadcast_to(row_ref[...].astype(F32), shape)
    return jnp.sum(jnp.where(diagonal, values, 0.0), axis=1, keepdims=True)


def fetch(pairs, sems):
    copies = [pltpu.make_async_copy(src, dst, sems.at[i]) for i, (src, dst) in enumerate(pairs)]
    for copy in copies:
        copy.start()
    return copies


def project_kernel(
    tokens_hbm, gain_hbm, place_hbm, len_hbm, freq_hbm, wq_hbm,
    msg_ref, normed_ref, cos_ref, sin_ref,
    tokens, gain, place, lens, freq, wq, sems,
):
    sources, count, wide = msg_ref.shape
    width = wide - HEAD_DIM
    rows = wq.shape[0] // PIECES
    small = [(tokens_hbm, tokens), (gain_hbm, gain), (place_hbm, place), (len_hbm, lens), (freq_hbm, freq)]
    slabs = [pl.ds(i * rows, rows) for i in range(PIECES)]
    copies = fetch(small + [(wq_hbm.at[at, :], wq.at[at, :]) for at in slabs], sems)
    for copy in copies[: len(small)]:
        copy.wait()
    normed = norm_rows(tokens[...].astype(F32), gain)
    normed_ref[...] = normed
    lane = lax.broadcasted_iota(jnp.int32, (count, HEAD_DIM), 1)
    angle = column(place, count) * freq[...]
    cosine = jnp.cos(angle)
    sine = jnp.where(lane < HEAD_DIM // 2, -1.0, 1.0) * jnp.sin(angle)
    cos_ref[...] = cosine
    sin_ref[...] = sine
    length = column(lens, count)
    high = jnp.floor(length * (1.0 / 128.0))
    coded = jnp.where(lane < HEAD_DIM // 2, high, length - 128.0 * high).astype(BF16)
    q = jnp.zeros((count, width), F32)
    for copy, at in zip(copies[len(small) :], slabs):
        copy.wait()
        q = q + mm(normed[:, at.start : at.start + rows], wq[at, :])
    parts = []
    for low in range(0, width, HEAD_DIM):
        x = q[:, low : low + HEAD_DIM]
        parts.append((x * cosine + pltpu.roll(x, HEAD_DIM // 2, 1) * sine).astype(BF16))
    msg = jnp.concatenate(parts + [coded], axis=1)
    for r in range(sources):
        msg_ref[r, :, :] = msg


def prepare_kernel(
    normed_ref, cos_ref, sin_ref, wk_hbm, wv_hbm, cache_hbm, wo_hbm,
    kv_ref, key_ref, value_ref, wo_ref,
    wk, wv, cache, wide, sems,
):
    half = wk.shape[1]
    slabs = cache.shape[0] // SLAB
    per_slot = 2 * half // HEAD_DIM
    spots = [pl.ds(i * SLAB, SLAB) for i in range(slabs)]
    wanted = [(cache_hbm.at[at, :], cache.at[at, :]) for at in spots]
    copies = fetch(wanted + [(wk_hbm, wk), (wv_hbm, wv), (wo_hbm, wo_ref)], sems)
    slots = SLAB // per_slot
    for i, at in enumerate(spots):
        copies[i].wait()
        wide[i % 2, :, :] = cache[at, :].astype(F32)
        for j in range(per_slot):
            rows = wide[i % 2, pl.ds(j, slots, stride=per_slot), :].astype(BF16)
            to = value_ref if j % 2 else key_ref
            to[i * slots : (i + 1) * slots, (j // 2) * HEAD_DIM : (j // 2 + 1) * HEAD_DIM] = rows
    normed = normed_ref[...]
    cosine = cos_ref[...]
    sine = sin_ref[...]
    copies[slabs].wait()
    k = mm(normed, wk[...])
    for low in range(0, half, HEAD_DIM):
        x = k[:, low : low + HEAD_DIM]
        kv_ref[:, low : low + HEAD_DIM] = x * cosine + pltpu.roll(x, HEAD_DIM // 2, 1) * sine
    copies[slabs + 1].wait()
    kv_ref[:, half:] = mm(normed, wv[...])
    copies[slabs + 2].wait()


def attend_kernel(
    base_ref, msg_ref, order_ref, live_ref, key_ref, value_ref, wg_hbm, wu_hbm,
    out_ref, wg_ref, wu_ref,
    queries, starts, ends, top, total, summed, held, weights, ranks, ranks_s, sem, load_sems,
):
    loads = fetch([(wg_hbm, wg_ref), (wu_hbm, wu_ref)], load_sems)
    reqs = msg_ref.shape[0]
    width = msg_ref.shape[1] - HEAD_DIM
    heads = width // HEAD_DIM
    group = heads // (key_ref.shape[1] // HEAD_DIM)
    tiles = key_ref.shape[0] // TILE
    factor = LOG2E / math.sqrt(HEAD_DIM)
    base = base_ref[0].astype(F32)

    row = lax.broadcasted_iota(jnp.int32, (reqs, reqs), 0)
    col = lax.broadcasted_iota(jnp.int32, (reqs, reqs), 1)
    place = (order_ref[...] == row).astype(F32).astype(BF16)
    parts = mm(place, msg_ref[:, width:], ((0,), (0,))).astype(BF16)
    lane = lax.broadcasted_iota(jnp.int32, (reqs, HEAD_DIM), 1)
    high_half = lane < HEAD_DIM // 2

    def joined(counts):
        turned = pltpu.roll(counts, HEAD_DIM // 2, 1)
        return jnp.where(high_half, 128.0 * counts + turned, counts + 128.0 * turned)

    upto = joined(mm((col <= row).astype(F32).astype(BF16), parts)) - base
    edge = (lane * TILE).astype(F32)
    first = jnp.sum((upto <= edge).astype(F32), axis=0, keepdims=True)
    last = jnp.sum((upto <= edge + (TILE - 1)).astype(F32), axis=0, keepdims=True)
    ranks[0:1, :] = first.astype(jnp.int32)
    ranks[1:2, :] = last.astype(jnp.int32)
    copy = pltpu.make_async_copy(ranks, ranks_s, sem)
    copy.start()
    far = jnp.full((WIN, HEAD_DIM), 1e9, F32)
    ends[0:reqs, :] = upto
    ends[reqs:, :] = far
    starts[0:reqs, :] = upto - joined(parts.astype(F32))
    starts[reqs:, :] = far
    sorted_q = mm(place, msg_ref[:, :width], ((0,), (0,)))
    for h in range(heads):
        queries[h, 0:reqs, :] = sorted_q[:, h * HEAD_DIM : (h + 1) * HEAD_DIM]
        queries[h, reqs:, :] = jnp.zeros((WIN, HEAD_DIM), F32)
    top[...] = jnp.full(top.shape, LOWEST, F32)
    total[...] = jnp.zeros(total.shape, F32)
    summed[...] = jnp.zeros(summed.shape, F32)
    copy.wait()

    def spot(h, rank):
        return (h, pl.ds(rank, WIN), slice(None))

    def of_head(x, h):
        return x[h * WIN : (h + 1) * WIN, :]

    def masked_scores(tile, rank):
        none = jnp.zeros((WIN, HEAD_DIM), BF16)
        lines = []
        for h in range(heads):
            q = queries[spot(h, rank)].astype(BF16)
            lines.append(
                jnp.concatenate([q if c == h // group else none for c in range(heads // group)], axis=1)
            )
        keys = key_ref[pl.ds(tile * TILE, TILE), :]
        scores = mm(jnp.concatenate(lines, axis=0), keys, ((1,), (1,))) * factor
        low = starts[pl.ds(rank, WIN), :]
        high = ends[pl.ds(rank, WIN), :]
        masks = []
        for i in range(TILE // SUB):
            block = tile * (TILE // SUB) + i
            at = (lax.broadcasted_iota(jnp.int32, (1, SUB), 1) + block * SUB).astype(F32)
            at = jnp.where(live_ref[pl.ds(block, 1), :] == 1, at, -1e9)
            masks.append((at >= low) & (at < high))
        mask = jnp.concatenate(masks, axis=1)
        return jnp.concatenate([jnp.where(mask, of_head(scores, h), FLOOR) for h in range(heads)], axis=0)

    def values_of(tile, weight):
        value = mm(weight, value_ref[pl.ds(tile * TILE, TILE), :])
        return [
            of_head(value, h)[:, (h // group) * HEAD_DIM : (h // group + 1) * HEAD_DIM] for h in range(heads)
        ]

    begins = [ranks_s[0, t] for t in range(tiles)]
    for t in range(tiles):
        held[t, :, :] = masked_scores(t, begins[t])
    peaks = [jnp.max(held[t, :, :], axis=1, keepdims=True) for t in range(tiles)]
    for t in range(tiles):
        for h in range(heads):
            at = spot(h, begins[t])
            top[at] = jnp.maximum(top[at], of_head(peaks[t], h))
    counts = []
    for t in range(tiles):
        peak = jnp.concatenate([top[spot(h, begins[t])] for h in range(heads)], axis=0)
        weight = jnp.exp2(held[t, :, :] - jnp.concatenate([peak] * (TILE // HEAD_DIM), axis=1))
        weights[t, :, :] = weight.astype(BF16)
        counts.append(jnp.sum(weight, axis=1, keepdims=True))
    found = [values_of(t, weights[t, :, :]) for t in range(tiles)]
    for t in range(tiles):
        for h in range(heads):
            at = spot(h, begins[t])
            total[at] = total[at] + of_head(counts[t], h)
            summed[at] = summed[at] + found[t][h]

    def more(t, carry):
        begin = ranks_s[0, t]

        def again(i, inner):
            rank = begin + (i + 1) * WIN
            masked = masked_scores(t, rank)
            peak = jnp.maximum(jnp.max(masked, axis=1, keepdims=True), LOWEST)
            weight = jnp.exp2(masked - peak)
            count = jnp.sum(weight, axis=1, keepdims=True)
            value = values_of(t, weight.astype(BF16))
            for h in range(heads):
                at = spot(h, rank)
                old = top[at]
                new = jnp.maximum(old, of_head(peak, h))
                left = jnp.exp2(old - new)
                right = jnp.exp2(of_head(peak, h) - new)
                top[at] = new
                total[at] = total[at] * left + of_head(count, h) * right
                summed[at] = summed[at] * left + value[h] * right
            return inner

        return lax.fori_loop(0, (ranks_s[1, t] - begin) // WIN, again, carry)

    lax.fori_loop(0, tiles, more, 0)

    columns = []
    extra = jnp.zeros((reqs, HEAD_DIM), F32)
    for h in range(heads):
        sums = total[h, 0:reqs, :]
        some = sums > 0.0
        safe = jnp.where(some, sums, 1.0)
        columns.append((summed[h, 0:reqs, :] / safe).astype(BF16))
        rest = jnp.where(some, top[h, 0:reqs, :] + jnp.log2(safe), LOWEST)
        for piece in range(3):
            coded = rest.astype(BF16).astype(F32)
            extra = jnp.where(lane == piece * heads + h, coded, extra)
            rest = rest - coded
    both = jnp.concatenate(columns + [extra.astype(BF16)], axis=1)
    out_ref[...] = mm(place, both).astype(BF16)
    for load in loads:
        load.wait()


def load_kernel(after_hbm, w_hbm, w_ref, sem):
    copy = pltpu.make_async_copy(w_hbm, w_ref, sem)
    copy.start()
    copy.wait()


def output_kernel(parts_ref, msg_ref, kv_ref, w_ref, out_ref):
    sources, count, wide = parts_ref.shape
    width = wide - HEAD_DIM
    heads = width // HEAD_DIM
    half = kv_ref.shape[1] // 2
    group = heads // (half // HEAD_DIM)
    factor = LOG2E / math.sqrt(HEAD_DIM)
    levels = []
    for r in range(sources):
        e = parts_ref[r, :, width:].astype(F32)
        levels.append(
            e + (pltpu.roll(e, HEAD_DIM - heads, 1) + pltpu.roll(e, HEAD_DIM - 2 * heads, 1))
        )
    context = []
    for h in range(heads):
        at = slice(h * HEAD_DIM, (h + 1) * HEAD_DIM)
        low = (h // group) * HEAD_DIM
        key = kv_ref[:, low : low + HEAD_DIM].astype(BF16).astype(F32)
        value = kv_ref[:, half + low : half + low + HEAD_DIM].astype(BF16).astype(F32)
        own = jnp.sum(msg_ref[0, :, at].astype(F32) * key, axis=1, keepdims=True) * factor
        cols = [level[:, h : h + 1] for level in levels]
        peak = own
        for c in cols:
            peak = jnp.maximum(peak, c)
        weight = jnp.exp2(own - peak)
        denom = weight
        numer = weight * value
        for r in range(sources):
            weight = jnp.exp2(cols[r] - peak)
            denom = denom + weight
            numer = numer + weight * parts_ref[r, :, at].astype(F32)
        context.append((numer / denom).astype(BF16))
    out_ref[...] = mm(jnp.concatenate(context, axis=1), w_ref[...]).astype(BF16)


def feed_kernel(tokens_ref, here_ref, there_ref, gain_ref, wg_ref, wu_ref, wd_ref, part_ref, mid_ref):
    mid = tokens_ref[...].astype(F32) + (here_ref[...].astype(F32) + there_ref[...].astype(F32))
    mid_ref[...] = mid
    normed = norm_rows(mid, gain_ref)
    gate = mm(normed, wg_ref[...])
    upper = mm(normed, wu_ref[...])
    act = (gate / (1.0 + jnp.exp(-gate)) * upper).astype(BF16)
    part_ref[...] = mm(act, wd_ref[...]).astype(BF16)


def swap(x, axis, distance):
    return lax.ppermute(x, axis, [(i, i ^ distance) for i in range(lax.axis_size(axis))])


def pair_sum(x):
    size = lax.axis_size("tp")
    distance = 1
    while distance * 2 < size:
        x = (x.astype(F32) + swap(x, "tp", distance).astype(F32)).astype(BF16)
        distance *= 2
    return x, swap(x, "tp", distance)


def in_hbm(x):
    return pltpu.with_memory_space_constraint(x, pltpu.HBM)


def in_vmem(x):
    return pltpu.with_memory_space_constraint(x, VMEM)


def per_device(
    tokens, lengths, pool_order, positions, slot_mask, kv_cache, attn_gain,
    w_query, w_key, w_value, w_out, ffn_gain, w_gate, w_up, w_down,
):
    count, model = tokens.shape
    nreq = lax.axis_size("req")
    reqs = count * nreq
    slot_count = kv_cache.shape[0]
    width = w_query.shape[1]
    half = w_key.shape[1]
    kv_heads = half // HEAD_DIM
    wide = width + HEAD_DIM
    assert slot_count % TILE == 0 and slot_count // TILE <= HEAD_DIM

    hbm_spec = pl.BlockSpec(memory_space=pltpu.HBM)
    vmem_spec = pl.BlockSpec(memory_space=VMEM)
    pair = np.arange(HEAD_DIM) % (HEAD_DIM // 2)
    freq = jnp.asarray((ROPE_BASE ** (-(pair * 2.0) / HEAD_DIM)).astype(np.float32)).reshape(1, HEAD_DIM)
    gain_shape = (model // HEAD_DIM, HEAD_DIM)

    msg, normed, cosine, sine = pl.pallas_call(
        project_kernel,
        out_shape=(
            jax.ShapeDtypeStruct((nreq, count, wide), BF16),
            VMEM((count, model), BF16),
            VMEM((count, HEAD_DIM), F32),
            VMEM((count, HEAD_DIM), F32),
        ),
        in_specs=[hbm_spec] * 6,
        out_specs=[vmem_spec] * 4,
        scratch_shapes=[
            VMEM((count, model), BF16),
            VMEM(gain_shape, BF16),
            VMEM((1, count), jnp.int32),
            VMEM((1, count), jnp.int32),
            VMEM((1, HEAD_DIM), F32),
            VMEM((model, width), BF16),
            pltpu.SemaphoreType.DMA((5 + PIECES,)),
        ],
        compiler_params=pltpu.CompilerParams(vmem_limit_bytes=4 << 20),
        cost_estimate=pl.CostEstimate(flops=2 * count * model * width, bytes_accessed=3 * model * width, transcendentals=0),
        name="project",
    )(
        in_hbm(tokens),
        in_hbm(attn_gain.reshape(gain_shape)),
        in_hbm(positions.reshape(1, count)),
        in_hbm(lengths.reshape(1, count)),
        in_hbm(freq),
        in_hbm(w_query),
    )

    everyone = lax.all_to_all(msg, "req", 0, 0).reshape(reqs, wide)

    cache = kv_cache.reshape(slot_count, 2, kv_heads, HEAD_DIM).transpose(0, 2, 1, 3)
    cache = cache.reshape(slot_count * 2 * kv_heads, HEAD_DIM)
    new_kv, keys, values, near_out = pl.pallas_call(
        prepare_kernel,
        out_shape=(
            VMEM((count, 2 * half), F32),
            VMEM((slot_count, half), BF16),
            VMEM((slot_count, half), BF16),
            VMEM(w_out.shape, BF16),
        ),
        in_specs=[vmem_spec] * 3 + [hbm_spec] * 4,
        out_specs=[vmem_spec] * 4,
        scratch_shapes=[
            VMEM((model, half), BF16),
            VMEM((model, half), BF16),
            VMEM(cache.shape, BF16),
            VMEM((2, SLAB, HEAD_DIM), F32),
            pltpu.SemaphoreType.DMA((cache.shape[0] // SLAB + 3,)),
        ],
        compiler_params=pltpu.CompilerParams(vmem_limit_bytes=9 << 20),
        cost_estimate=pl.CostEstimate(flops=4 * count * model * half, bytes_accessed=3 * cache.size, transcendentals=0),
        name="prepare",
    )(normed, cosine, sine, in_hbm(w_key), in_hbm(w_value), in_hbm(cache), in_hbm(w_out))

    live = slot_mask.reshape(slot_count // SUB, SUB)
    base = (lax.axis_index("req") * slot_count).astype(jnp.int32).reshape(1)
    rows = reqs + WIN
    heads = width // HEAD_DIM
    tiles = slot_count // TILE
    per_head = (heads, rows, HEAD_DIM)
    parts, near_gate, near_up = pl.pallas_call(
        attend_kernel,
        out_shape=(
            jax.ShapeDtypeStruct((reqs, wide), BF16),
            VMEM(w_gate.shape, BF16),
            VMEM(w_up.shape, BF16),
        ),
        in_specs=[pl.BlockSpec(memory_space=pltpu.SMEM)] + [vmem_spec] * 5 + [hbm_spec] * 2,
        out_specs=[vmem_spec] * 3,
        scratch_shapes=[
            VMEM(per_head, F32),
            VMEM((rows, HEAD_DIM), F32),
            VMEM((rows, HEAD_DIM), F32),
            VMEM(per_head, F32),
            VMEM(per_head, F32),
            VMEM(per_head, F32),
            VMEM((tiles, heads * WIN, TILE), F32),
            VMEM((tiles, heads * WIN, TILE), BF16),
            VMEM((8, HEAD_DIM), jnp.int32),
            pltpu.SMEM((8, HEAD_DIM), jnp.int32),
            pltpu.SemaphoreType.DMA,
            pltpu.SemaphoreType.DMA((2,)),
        ],
        compiler_params=pltpu.CompilerParams(vmem_limit_bytes=(2 + reqs // 32) << 20),
        cost_estimate=pl.CostEstimate(flops=1 << 30, bytes_accessed=8 << 20, transcendentals=0),
        name="attend",
    )(base, everyone, pool_order.reshape(1, reqs), live, keys, values, in_hbm(w_gate), in_hbm(w_up))

    mine = lax.all_to_all(parts.reshape(nreq, count, wide), "req", 0, 0)

    partial_attn = pl.pallas_call(
        output_kernel,
        out_shape=jax.ShapeDtypeStruct((count, model), BF16),
        compiler_params=pltpu.CompilerParams(vmem_limit_bytes=4 << 20),
        name="output",
    )(mine, msg, new_kv, near_out)

    here, there = pair_sum(partial_attn)
    near_down = pl.pallas_call(
        load_kernel,
        out_shape=VMEM(w_down.shape, BF16),
        in_specs=[pl.BlockSpec(memory_space=pl.ANY), hbm_spec],
        out_specs=vmem_spec,
        scratch_shapes=[pltpu.SemaphoreType.DMA],
        compiler_params=pltpu.CompilerParams(vmem_limit_bytes=1 << 20),
        cost_estimate=pl.CostEstimate(flops=0, bytes_accessed=2 * w_down.size, transcendentals=0),
        name="load",
    )(here, in_hbm(w_down))
    down_part, mid = pl.pallas_call(
        feed_kernel,
        out_shape=(
            jax.ShapeDtypeStruct((count, model), BF16),
            jax.ShapeDtypeStruct((count, model), F32),
        ),
        compiler_params=pltpu.CompilerParams(vmem_limit_bytes=6 << 20),
        name="feed",
    )(tokens, here, there, ffn_gain.reshape(gain_shape), near_gate, near_up, near_down)

    here, there = pair_sum(down_part)
    hidden_out = mid + (here.astype(F32) + there.astype(F32))
    return (hidden_out, new_kv.reshape(count, 2, half))


def solution(mesh):
    placed = (
        P("req", None),
        P("req"),
        P(),
        P("req"),
        P("req"),
        P("req", None, "tp"),
        P(),
        P(None, "tp"),
        P(None, "tp"),
        P(None, "tp"),
        P("tp", None),
        P(),
        P(None, "tp"),
        P(None, "tp"),
        P("tp", None),
    )
    return jax.shard_map(
        per_device,
        mesh=mesh,
        in_specs=placed,
        out_specs=(P("req", None), P("req", None, "tp")),
        check_vma=False,
    )
```

time: 64 us -> 51.2 us (0.80)
  local copies, waits for them, and re-layouts: 13.5 us -> 4.91 us
  waiting for transfers between devices: 15 us -> 6.42 us
  Pallas kernels: 11.4 us -> 15.5 us
  blocking collectives: 10.2 us -> 12.2 us
  other arithmetic: 2.23 us -> 0.71 us
    unnamed x26 -> x16, local copies, waits for them, and re-layouts: 11.5 us -> 4.28 us
    all_to_all x1, waiting for transfers between devices: 7.56 us -> 1.19 us  [per_device(): everyone = lax.all_to_all(msg, 'req', 0, 0).reshape(reqs, wide)]
    pallas_call x2 -> x4, Pallas kernels: 8.87 us -> 12.1 us  [the longest x1 3.68 us: per_device(): pl.pallas_call(prepare_kernel, out_shape=(VMEM((count, 2 * half), F32), V...]
    ppermute x4, waiting for transfers between devices: 7.43 us -> 5.22 us  [swap(): lax.ppermute(x, axis, [(i, i ^ distance) for i in range(lax.axis_size(axi...]
    all_to_all x1, blocking collectives: 10.2 us -> 12.2 us  [per_device(): mine = lax.all_to_all(parts.reshape(nreq, count, wide), 'req', 0, 0)]
    pallas_call x1, Pallas kernels: 0.64 us -> 1.55 us  [per_device(): pl.pallas_call(output_kernel, out_shape=jax.ShapeDtypeStruct((count, mode...]
    convert_element_type x2 -> x0, other arithmetic: 0.73 us -> none  [the longest x1 0.66 us: per_device(): angle = positions.astype(F32)[:, None] * freq[None, :]]
    reshape x2 -> x0, local copies, waits for them, and re-layouts: 0.7 us -> none  [the longest x1 0.69 us: per_device(): attn_gain.reshape(1, model)]
  transfers between devices with their start and end apart: 5 -> 5, of which waited for: 5 -> 5; matrix products, arithmetic and copies ran while one was open for 1% -> 1% of each run, Pallas kernels for 0% -> 12%
where the time goes in v2:
time: 51.2 us; the launch traced here: 50.9 us
  Pallas kernels  15.5 us (30%)
  blocking collectives  12.2 us (24%)
  starting transfers between devices  10.4 us (20%)
  waiting for transfers between devices  6.42 us (13%)
  local copies, waits for them, and re-layouts  4.91 us (10%)
  between operations  0.72 us (1%)
  other arithmetic  0.71 us (1%)
    all_to_all x1, blocking collectives, per_device(): mine = lax.all_to_all(parts.reshape(nreq, count, wide), 'req', 0, 0)  12.2 us
    all_to_all x1, starting transfers between devices, per_device(): everyone = lax.all_to_all(msg, 'req', 0, 0).reshape(reqs, wide)  7.29 us
    ppermute x4, waiting for transfers between devices, swap(): lax.ppermute(x, axis, [(i, i ^ distance) for i in range(lax.axis_size(axi...  5.22 us
    unnamed x16, local copies, waits for them, and re-layouts  4.28 us
    pallas_call x1, Pallas kernels, per_device(): pl.pallas_call(prepare_kernel, out_shape=(VMEM((count, 2 * half), F32), V...  3.68 us
    pallas_call x1, Pallas kernels, per_device(): pl.pallas_call(attend_kernel, out_shape=(jax.ShapeDtypeStruct((reqs, wide...  3.64 us
    ppermute x4, starting transfers between devices, swap(): lax.ppermute(x, axis, [(i, i ^ distance) for i in range(lax.axis_size(axi...  3.12 us
    pallas_call x1, Pallas kernels, per_device(): pl.pallas_call(project_kernel, out_shape=(jax.ShapeDtypeStruct((nreq, cou...  2.63 us
  transfers between devices with their start and end apart: 5, of which 5 were waited for; matrix products, arithmetic and copies ran while one was open for 1% of the time, Pallas kernels for 12%

profile of v2, /device:TPU:0, one launch (start us, length us, event | category | flops | bytes accessed | tf_op | source)
XLA Modules:
  0.0 50.9 jit_solution(4995521126104374220)
XLA Ops:
  0.6 2.6 %project.1 = (bf16[8,16,640]{2,1,0:T(8,128)(2,1)}, bf16[16,2048]{1,0:T(8,128)(2,1)S(1)}, f32[16,128]{1,0:T(8,128)S(1)}, f32[16,128]{1,0:T(8,128)S(1)}) custom-call(bf16[16,2048]{1,0:T(8,128)(2,1)} %tokens_ref.1, bf16[16,128]{1,0:T(8,128)(2,1)} %bitcast.20, s32[1,16]{1,0:T(1,128)} %bitcast.21, s32[1,16]{1,0:T(1,128)} %bitcast.22, ...), custom_call_target="tpu_custom_call" | custom-call | flops 33554432 | bytes 3145728 | tf_op jit(solution)/shard_map/project/pallas_call | solution.py:360
  3.3 7.3 %all-to-all-start = ((bf16[8,16,640]{2,1,0:T(8,128)(2,1)}), bf16[8,16,640]{2,1,0:T(8,128)(2,1)S(1)}, u32[]{:S(2)}, u32[]{:S(2)}) async-start(bf16[8,16,640]{2,1,0:T(8,128)(2,1)} %get-tuple-element.15.msg_ref), calls=%async_computation | async-start | bytes 327680 | tf_op jit(solution)/shard_map/all_to_all | solution.py:391
  10.6 0.0 copy-start.5
  10.6 0.0 copy-start.7
  10.6 3.7 %prepare.1 = (f32[16,512]{1,0:T(8,128)S(1)}, bf16[4096,256]{1,0:T(8,128)(2,1)S(1)}, bf16[4096,256]{1,0:T(8,128)(2,1)S(1)}, bf16[512,2048]{1,0:T(8,128)(2,1)S(1)}) custom-call(bf16[16,2048]{1,0:T(8,128)(2,1)S(1)} %get-tuple-element.16.normed_ref, f32[16,128]{1,0:T(8,128)S(1)} %get-tuple-element.17.cos_ref, f32[16,128]{1,0:T(8,128)S(1)} %get-tuple-element.18.sin_ref, ...), custom_call_target="tpu_custom_call" | custom-call | flops 33554432 | bytes 6291456 | tf_op jit(solution)/shard_map/prepare/pallas_call | solution.py:395
  14.3 0.0 copy-start
  14.3 1.3 %copy-done = bf16[4096,256]{1,0:T(8,128)(2,1)} copy-done((bf16[4096,256]{1,0:T(8,128)(2,1)}, bf16[4096,256]{1,0:T(8,128)(2,1)S(1)}, u32[]{:S(2)}) %copy-start) | copy-done | bytes 2097176
  15.6 0.0 copy-start.2
  15.6 1.3 %copy-done.2 = bf16[512,2048]{1,0:T(8,128)(2,1)} copy-done((bf16[512,2048]{1,0:T(8,128)(2,1)}, bf16[512,2048]{1,0:T(8,128)(2,1)S(1)}, u32[]{:S(2)}) %copy-start.2) | copy-done | bytes 2097176
  16.9 1.2 %all-to-all-done = bf16[8,16,640]{2,1,0:T(8,128)(2,1)S(1)} async-done(((bf16[8,16,640]{2,1,0:T(8,128)(2,1)}), bf16[8,16,640]{2,1,0:T(8,128)(2,1)S(1)}, u32[]{:S(2)}, u32[]{:S(2)}) %all-to-all-start) | async-done | bytes 163872 | tf_op jit(solution)/shard_map/all_to_all | solution.py:391
  18.1 0.0 copy-done.5
  18.1 0.0 copy-done.7
  18.1 0.0 copy-start.1
  18.1 1.6 %copy-done.1 = bf16[4096,256]{1,0:T(8,128)(2,1)S(1)} copy-done((bf16[4096,256]{1,0:T(8,128)(2,1)S(1)}, bf16[4096,256]{1,0:T(8,128)(2,1)}, u32[]{:S(2)}) %copy-start.1) | copy-done | bytes 2097176
  19.7 0.0 copy-start.3
  19.7 3.6 %attend.1 = (bf16[128,640]{1,0:T(8,128)(2,1)S(1)}, bf16[2048,1024]{1,0:T(8,128)(2,1)S(1)}, bf16[2048,1024]{1,0:T(8,128)(2,1)S(1)}) custom-call(s32[1]{0:T(128)} %bitcast.base_ref, bf16[128,640]{1,0:T(8,128)(2,1)S(1)} %bitcast.14, s32[1,128]{1,0:T(1,128)S(1)} %bitcast.18, s32[32,128]{1,0:T(8,128)S(1)} %bitcast.16, ...), custom_call_target="tpu_custom_call" | custom-call | flops 1073741824 | bytes 8388608 | tf_op jit(solution)/shard_map/attend/pallas_call | solution.py:423
  23.4 12.2 %all_to_all.10.parts_ref = bf16[8,16,640]{2,1,0:T(8,128)(2,1)S(1)} all-to-all(bf16[8,16,640]{2,1,0:T(8,128)(2,1)S(1)} %bitcast.15), channel_id=1, replica_groups=mesh['req'=8,'tp'=4] {'req'}, dimensions={0} | all-to-all | bytes 327680 | tf_op jit(solution)/shard_map/all_to_all | solution.py:451
  35.5 0.0 copy-done.3
  35.5 1.6 %output.1 = bf16[16,2048]{1,0:T(8,128)(2,1)S(1)} custom-call(bf16[8,16,640]{2,1,0:T(8,128)(2,1)S(1)} %all_to_all.10.parts_ref, bf16[8,16,640]{2,1,0:T(8,128)(2,1)} %get-tuple-element.15.msg_ref, f32[16,512]{1,0:T(8,128)S(1)} %get-tuple-element.22.kv_ref, bf16[512,2048]{1,0:T(8,128)(2,1)S(1)} %copy-done.3), custom_call_target="tpu_custom_call" | custom-call | tf_op jit(solution)/shard_map/output/pallas_call | solution.py:453
  37.1 0.0 collective-permute-start
  37.1 1.3 %collective-permute-done = bf16[16,2048]{1,0:T(8,128)(2,1)S(1)} collective-permute-done((bf16[16,2048]{1,0:T(8,128)(2,1)S(1)}, bf16[16,2048]{1,0:T(8,128)(2,1)S(1)}, u32[]{:S(2)}, u32[]{:S(2)}) %collective-permute-start) | collective-permute-done | bytes 65568 | tf_op jit(solution)/shard_map/ppermute | solution.py:320
  38.4 0.0 copy-start.4
  38.4 0.0 copy-start.6
  38.4 1.6 %collective-permute-start.1 = (bf16[16,2048]{1,0:T(8,128)(2,1)S(1)}, bf16[16,2048]{1,0:T(8,128)(2,1)S(1)}, u32[]{:S(2)}, u32[]{:S(2)}) collective-permute-start(bf16[16,2048]{1,0:T(8,128)(2,1)S(1)} %add_convert_fusion.1.after_hbm.here_ref), channel_id=1, source_target_pairs={{0,2},{1,3},{2,0},{3,1},{4,6},{5,7},{6,4},{7,5},{8,10},{9,11},{10,... | collective-permute-start | bytes 196616 | tf_op jit(solution)/shard_map/ppermute | solution.py:320
  40.0 2.2 %load.1.wd_ref = bf16[1024,2048]{1,0:T(8,128)(2,1)S(1)} custom-call(bf16[16,2048]{1,0:T(8,128)(2,1)S(1)} %add_convert_fusion.1.after_hbm.here_ref, bf16[1024,2048]{1,0:T(8,128)(2,1)} %w_hbm.1), custom_call_target="tpu_custom_call" | custom-call | bytes 4194304 | tf_op jit(solution)/shard_map/load/pallas_call | solution.py:461
  42.2 0.6 %collective-permute-done.1.there_ref = bf16[16,2048]{1,0:T(8,128)(2,1)S(1)} collective-permute-done((bf16[16,2048]{1,0:T(8,128)(2,1)S(1)}, bf16[16,2048]{1,0:T(8,128)(2,1)S(1)}, u32[]{:S(2)}, u32[]{:S(2)}) %collective-permute-start.1) | collective-permute-done | bytes 65568 | tf_op jit(solution)/shard_map/ppermute | solution.py:320
  42.7 0.0 copy-done.4
  42.7 0.0 copy-done.6
  42.7 1.8 %feed.1 = (bf16[16,2048]{1,0:T(8,128)(2,1)S(1)}, f32[16,2048]{1,0:T(8,128)S(1)}) custom-call(bf16[16,2048]{1,0:T(8,128)(2,1)S(1)} %copy-done.4, bf16[16,2048]{1,0:T(8,128)(2,1)S(1)} %add_convert_fusion.1.after_hbm.here_ref, bf16[16,2048]{1,0:T(8,128)(2,1)S(1)} %collective-permute-done.1.there_ref, bf16[16,128]{1,0:T(8,128)(2,1)S(1)} %bitcast.17, ...), custom_call_target="tpu_custom_call" | custom-call | tf_op jit(solution)/shard_map/feed/pallas_call | solution.py:471
  44.6 0.0 collective-permute-start.2
  44.6 1.3 %collective-permute-done.2 = bf16[16,2048]{1,0:T(8,128)(2,1)S(1)} collective-permute-done((bf16[16,2048]{1,0:T(8,128)(2,1)S(1)}, bf16[16,2048]{1,0:T(8,128)(2,1)S(1)}, u32[]{:S(2)}, u32[]{:S(2)}) %collective-permute-start.2) | collective-permute-done | bytes 65568 | tf_op jit(solution)/shard_map/ppermute | solution.py:320
  45.9 1.6 %collective-permute-start.3 = (bf16[16,2048]{1,0:T(8,128)(2,1)S(1)}, bf16[16,2048]{1,0:T(8,128)(2,1)S(1)}, u32[]{:S(2)}, u32[]{:S(2)}) collective-permute-start(bf16[16,2048]{1,0:T(8,128)(2,1)S(1)} %add_convert_fusion), channel_id=1, source_target_pairs={{0,2},{1,3},{2,0},{3,1},{4,6},{5,7},{6,4},{7,5},{8,10},{9,11},{10,... | collective-permute-start | bytes 196616 | tf_op jit(solution)/shard_map/ppermute | solution.py:320
  47.4 0.6 %reshape.55 = f32[16,2,256]{2,1,0:T(2,128)} reshape(f32[16,512]{1,0:T(8,128)S(1)} %get-tuple-element.22.kv_ref) | data formatting | bytes 65536 | tf_op jit(solution)/shard_map/reshape | solution.py:483
  48.1 2.1 %collective-permute-done.3 = bf16[16,2048]{1,0:T(8,128)(2,1)S(1)} collective-permute-done((bf16[16,2048]{1,0:T(8,128)(2,1)S(1)}, bf16[16,2048]{1,0:T(8,128)(2,1)S(1)}, u32[]{:S(2)}, u32[]{:S(2)}) %collective-permute-start.3) | collective-permute-done | bytes 65568 | tf_op jit(solution)/shard_map/ppermute | solution.py:320
  50.2 0.7 %add_add_fusion = f32[16,2048]{1,0:T(8,128)} fusion(f32[16,2048]{1,0:T(8,128)S(1)} %get-tuple-element.26, bf16[16,2048]{1,0:T(8,128)(2,1)S(1)} %collective-permute-done.3, bf16[16,2048]{1,0:T(8,128)(2,1)S(1)} %add_convert_fusion), kind=kLoop, calls=%fused_computation | loop fusion | flops 131072 | bytes 393216 | tf_op jit(solution)/shard_map/add | solution.py:482
  (2 shorter events, 0.0 us)
Async XLA Ops:
  3.3 14.9 %all-to-all-start = ((bf16[8,16,640]{2,1,0:T(8,128)(2,1)}), bf16[8,16,640]{2,1,0:T(8,128)(2,1)S(1)}, u32[]{:S(2)}, u32[]{:S(2)}) async-start(bf16[8,16,640]{2,1,0:T(8,128)(2,1)} %get-tuple-element.15.msg_ref), calls=%async_computation | async-start | bytes 327680 | tf_op jit(solution)/shard_map/all_to_all | solution.py:391
  10.6 7.6 %copy-start.5 = (s32[4096]{0:T(1024)S(1)}, s32[4096]{0:T(1024)}, u32[]{:S(2)}) copy-start(s32[4096]{0:T(1024)} %param.20) | copy-start | bytes 49156
  10.6 7.6 %copy-start.7 = (s32[128]{0:T(128)S(1)}, s32[128]{0:T(128)}, u32[]{:S(2)}) copy-start(s32[128]{0:T(128)} %param.18) | copy-start | bytes 1540
  14.3 1.3 %copy-start = (bf16[4096,256]{1,0:T(8,128)(2,1)}, bf16[4096,256]{1,0:T(8,128)(2,1)S(1)}, u32[]{:S(2)}) copy-start(bf16[4096,256]{1,0:T(8,128)(2,1)S(1)} %get-tuple-element.20.value_ref) | copy-start | bytes 6291460
  15.6 1.3 %copy-start.2 = (bf16[512,2048]{1,0:T(8,128)(2,1)}, bf16[512,2048]{1,0:T(8,128)(2,1)S(1)}, u32[]{:S(2)}) copy-start(bf16[512,2048]{1,0:T(8,128)(2,1)S(1)} %get-tuple-element.23.w_ref) | copy-start | bytes 6291460
  18.1 1.6 %copy-start.1 = (bf16[4096,256]{1,0:T(8,128)(2,1)S(1)}, bf16[4096,256]{1,0:T(8,128)(2,1)}, u32[]{:S(2)}) copy-start(bf16[4096,256]{1,0:T(8,128)(2,1)} %copy-done) | copy-start | bytes 6291460
  19.7 15.8 %copy-start.3 = (bf16[512,2048]{1,0:T(8,128)(2,1)S(1)}, bf16[512,2048]{1,0:T(8,128)(2,1)}, u32[]{:S(2)}) copy-start(bf16[512,2048]{1,0:T(8,128)(2,1)} %copy-done.2) | copy-start | bytes 6291460
  37.1 1.3 %collective-permute-start = (bf16[16,2048]{1,0:T(8,128)(2,1)S(1)}, bf16[16,2048]{1,0:T(8,128)(2,1)S(1)}, u32[]{:S(2)}, u32[]{:S(2)}) collective-permute-start(bf16[16,2048]{1,0:T(8,128)(2,1)S(1)} %output.1), channel_id=1, source_target_pairs={{0,1},{1,0},{2,3},{3,2},{4,5},{5,4},{6,7},{7,6},{8,9},{9,8},{10,11... | collective-permute-start | bytes 196616 | tf_op jit(solution)/shard_map/ppermute | solution.py:320
  38.4 4.4 %copy-start.4 = (bf16[16,2048]{1,0:T(8,128)(2,1)S(1)}, bf16[16,2048]{1,0:T(8,128)(2,1)}, u32[]{:S(2)}) copy-start(bf16[16,2048]{1,0:T(8,128)(2,1)} %tokens_ref.1) | copy-start | bytes 196612
  38.4 4.3 %copy-start.6 = (bf16[2048]{0:T(1024)(128)(2,1)S(1)}, bf16[2048]{0:T(1024)(128)(2,1)}, u32[]{:S(2)}) copy-start(bf16[2048]{0:T(1024)(128)(2,1)} %param.27) | copy-start | bytes 12292
  38.4 4.3 %collective-permute-start.1 = (bf16[16,2048]{1,0:T(8,128)(2,1)S(1)}, bf16[16,2048]{1,0:T(8,128)(2,1)S(1)}, u32[]{:S(2)}, u32[]{:S(2)}) collective-permute-start(bf16[16,2048]{1,0:T(8,128)(2,1)S(1)} %add_convert_fusion.1.after_hbm.here_ref), channel_id=1, source_target_pairs={{0,2},{1,3},{2,0},{3,1},{4,6},{5,7},{6,4},{7,5},{8,10},{9,11},{10,... | collective-permute-start | bytes 196616 | tf_op jit(solution)/shard_map/ppermute | solution.py:320
  44.6 1.3 %collective-permute-start.2 = (bf16[16,2048]{1,0:T(8,128)(2,1)S(1)}, bf16[16,2048]{1,0:T(8,128)(2,1)S(1)}, u32[]{:S(2)}, u32[]{:S(2)}) collective-permute-start(bf16[16,2048]{1,0:T(8,128)(2,1)S(1)} %get-tuple-element.27), channel_id=1, source_target_pairs={{0,1},{1,0},{2,3},{3,2},{4,5},{5,4},{6,7},{7,6},{8,9},{9,8},{10,11... | collective-permute-start | bytes 196616 | tf_op jit(solution)/shard_map/ppermute | solution.py:320
  45.9 4.3 %collective-permute-start.3 = (bf16[16,2048]{1,0:T(8,128)(2,1)S(1)}, bf16[16,2048]{1,0:T(8,128)(2,1)S(1)}, u32[]{:S(2)}, u32[]{:S(2)}) collective-permute-start(bf16[16,2048]{1,0:T(8,128)(2,1)S(1)} %add_convert_fusion), channel_id=1, source_target_pairs={{0,2},{1,3},{2,0},{3,1},{4,6},{5,7},{6,4},{7,5},{8,10},{9,11},{10,... | collective-permute-start | bytes 196616 | tf_op jit(solution)/shard_map/ppermute | solution.py:320

commit v3 on v2

--- a/solution.py
+++ b/solution.py
@@ -54,7 +54,7 @@
 
 def project_kernel(
     tokens_hbm, gain_hbm, place_hbm, len_hbm, freq_hbm, wq_hbm,
-    msg_ref, normed_ref, cos_ref, sin_ref,
+    msg_ref, mine_ref, normed_ref, cos_ref, sin_ref,
     tokens, gain, place, lens, freq, wq, sems,
 ):
     sources, count, wide = msg_ref.shape
@@ -85,48 +85,65 @@
         x = q[:, low : low + HEAD_DIM]
         parts.append((x * cosine + pltpu.roll(x, HEAD_DIM // 2, 1) * sine).astype(BF16))
     msg = jnp.concatenate(parts + [coded], axis=1)
+    mine_ref[...] = msg
     for r in range(sources):
         msg_ref[r, :, :] = msg
 
 
 def prepare_kernel(
-    normed_ref, cos_ref, sin_ref, wk_hbm, wv_hbm, cache_hbm, wo_hbm,
-    kv_ref, key_ref, value_ref, wo_ref,
-    wk, wv, cache, wide, sems,
+    normed_ref, cos_ref, sin_ref, wk_hbm, wv_hbm, cache_hbm,
+    kv_ref, key_ref, near_ref, far_hbm,
+    wk, wv, cache, wide, far, sems, out_sems,
 ):
     half = wk.shape[1]
     slabs = cache.shape[0] // SLAB
     per_slot = 2 * half // HEAD_DIM
     spots = [pl.ds(i * SLAB, SLAB) for i in range(slabs)]
     wanted = [(cache_hbm.at[at, :], cache.at[at, :]) for at in spots]
-    copies = fetch(wanted + [(wk_hbm, wk), (wv_hbm, wv), (wo_hbm, wo_ref)], sems)
+    copies = fetch([(wk_hbm, wk), (wv_hbm, wv)] + wanted, sems)
+    normed = normed_ref[...]
+    cosine = cos_ref[...]
+    sine = sin_ref[...]
+    copies.pop(0).wait()
+    k = mm(normed, wk[...])
+    for low in range(0, half, HEAD_DIM):
+        x = k[:, low : low + HEAD_DIM]
+        kv_ref[:, low : low + HEAD_DIM] = x * cosine + pltpu.roll(x, HEAD_DIM // 2, 1) * sine
+    copies.pop(0).wait()
+    kv_ref[:, half:] = mm(normed, wv[...])
     slots = SLAB // per_slot
+    outs = []
     for i, at in enumerate(spots):
         copies[i].wait()
         wide[i % 2, :, :] = cache[at, :].astype(F32)
         for j in range(per_slot):
             rows = wide[i % 2, pl.ds(j, slots, stride=per_slot), :].astype(BF16)
-            to = value_ref if j % 2 else key_ref
-            to[i * slots : (i + 1) * slots, (j // 2) * HEAD_DIM : (j // 2 + 1) * HEAD_DIM] = rows
-    normed = normed_ref[...]
-    cosine = cos_ref[...]
-    sine = sin_ref[...]
-    copies[slabs].wait()
-    k = mm(normed, wk[...])
-    for low in range(0, half, HEAD_DIM):
-        x = k[:, low : low + HEAD_DIM]
-        kv_ref[:, low : low + HEAD_DIM] = x * cosine + pltpu.roll(x, HEAD_DIM // 2, 1) * sine
-    copies[slabs + 1].wait()
-    kv_ref[:, half:] = mm(normed, wv[...])
-    copies[slabs + 2].wait()
+            to, first = key_ref, i * slots
+            if j % 2:
+                to, first = (far, first) if i < slabs // 2 else (near_ref, first - far.shape[0])
+            to[first : first + slots, (j // 2) * HEAD_DIM : (j // 2 + 1) * HEAD_DIM] = rows
+        if i < slabs // 2 and i % 4 == 3:
+            block = pl.ds((i - 3) * slots, 4 * slots)
+            outs.append(pltpu.make_async_copy(far.at[block, :], far_hbm.at[block, :], out_sems.at[i // 4]))
+            outs[-1].start()
+    for out in outs:
+        out.wait()
 
 
 def attend_kernel(
-    base_ref, msg_ref, order_ref, live_ref, key_ref, value_ref, wg_hbm, wu_hbm,
-    out_ref, wg_ref, wu_ref,
-    queries, starts, ends, top, total, summed, held, weights, ranks, ranks_s, sem, load_sems,
+    base_ref, msg_ref, order_ref, live_ref, key_ref, near_ref, far_hbm, wg_hbm,
+    out_ref, wg_ref,
+    queries, starts, ends, top, total, summed, held, weights, value_ref, ranks, ranks_s, sem, load_sems,
 ):
-    loads = fetch([(wg_hbm, wg_ref), (wu_hbm, wu_ref)], load_sems)
+    middle = far_hbm.shape[0]
+    loads = fetch(
+        [
+            (far_hbm, value_ref.at[pl.ds(0, middle), :]),
+            (near_ref, value_ref.at[pl.ds(middle, middle), :]),
+            (wg_hbm, wg_ref),
+        ],
+        load_sems,
+    )
     reqs = msg_ref.shape[0]
     width = msg_ref.shape[1] - HEAD_DIM
     heads = width // HEAD_DIM
@@ -215,6 +232,8 @@
         weight = jnp.exp2(held[t, :, :] - jnp.concatenate([peak] * (TILE // HEAD_DIM), axis=1))
         weights[t, :, :] = weight.astype(BF16)
         counts.append(jnp.sum(weight, axis=1, keepdims=True))
+    loads[0].wait()
+    loads[1].wait()
     found = [values_of(t, weights[t, :, :]) for t in range(tiles)]
     for t in range(tiles):
         for h in range(heads):
@@ -261,8 +280,7 @@
             rest = rest - coded
     both = jnp.concatenate(columns + [extra.astype(BF16)], axis=1)
     out_ref[...] = mm(place, both).astype(BF16)
-    for load in loads:
-        load.wait()
+    loads[2].wait()
 
 
 def load_kernel(after_hbm, w_hbm, w_ref, sem):
@@ -290,7 +308,7 @@
         low = (h // group) * HEAD_DIM
         key = kv_ref[:, low : low + HEAD_DIM].astype(BF16).astype(F32)
         value = kv_ref[:, half + low : half + low + HEAD_DIM].astype(BF16).astype(F32)
-        own = jnp.sum(msg_ref[0, :, at].astype(F32) * key, axis=1, keepdims=True) * factor
+        own = jnp.sum(msg_ref[:, at].astype(F32) * key, axis=1, keepdims=True) * factor
         cols = [level[:, h : h + 1] for level in levels]
         peak = own
         for c in cols:
@@ -357,16 +375,17 @@
     freq = jnp.asarray((ROPE_BASE ** (-(pair * 2.0) / HEAD_DIM)).astype(np.float32)).reshape(1, HEAD_DIM)
     gain_shape = (model // HEAD_DIM, HEAD_DIM)
 
-    msg, normed, cosine, sine = pl.pallas_call(
+    msg, mine, normed, cosine, sine = pl.pallas_call(
         project_kernel,
         out_shape=(
-            jax.ShapeDtypeStruct((nreq, count, wide), BF16),
+            VMEM((nreq, count, wide), BF16),
+            VMEM((count, wide), BF16),
             VMEM((count, model), BF16),
             VMEM((count, HEAD_DIM), F32),
             VMEM((count, HEAD_DIM), F32),
         ),
         in_specs=[hbm_spec] * 6,
-        out_specs=[vmem_spec] * 4,
+        out_specs=[vmem_spec] * 5,
         scratch_shapes=[
             VMEM((count, model), BF16),
             VMEM(gain_shape, BF16),
@@ -392,27 +411,29 @@
 
     cache = kv_cache.reshape(slot_count, 2, kv_heads, HEAD_DIM).transpose(0, 2, 1, 3)
     cache = cache.reshape(slot_count * 2 * kv_heads, HEAD_DIM)
-    new_kv, keys, values, near_out = pl.pallas_call(
+    new_kv, keys, near, far = pl.pallas_call(
         prepare_kernel,
         out_shape=(
             VMEM((count, 2 * half), F32),
             VMEM((slot_count, half), BF16),
-            VMEM((slot_count, half), BF16),
-            VMEM(w_out.shape, BF16),
+            VMEM((slot_count // 2, half), BF16),
+            pltpu.HBM((slot_count // 2, half), BF16),
         ),
-        in_specs=[vmem_spec] * 3 + [hbm_spec] * 4,
-        out_specs=[vmem_spec] * 4,
+        in_specs=[vmem_spec] * 3 + [hbm_spec] * 3,
+        out_specs=[vmem_spec, vmem_spec, vmem_spec, hbm_spec],
         scratch_shapes=[
             VMEM((model, half), BF16),
             VMEM((model, half), BF16),
             VMEM(cache.shape, BF16),
             VMEM((2, SLAB, HEAD_DIM), F32),
-            pltpu.SemaphoreType.DMA((cache.shape[0] // SLAB + 3,)),
+            VMEM((slot_count // 2, half), BF16),
+            pltpu.SemaphoreType.DMA((cache.shape[0] // SLAB + 2,)),
+            pltpu.SemaphoreType.DMA((cache.shape[0] // SLAB // 8,)),
         ],
-        compiler_params=pltpu.CompilerParams(vmem_limit_bytes=9 << 20),
+        compiler_params=pltpu.CompilerParams(vmem_limit_bytes=12 << 20),
         cost_estimate=pl.CostEstimate(flops=4 * count * model * half, bytes_accessed=3 * cache.size, transcendentals=0),
         name="prepare",
-    )(normed, cosine, sine, in_hbm(w_key), in_hbm(w_value), in_hbm(cache), in_hbm(w_out))
+    )(normed, cosine, sine, in_hbm(w_key), in_hbm(w_value), in_hbm(cache))
 
     live = slot_mask.reshape(slot_count // SUB, SUB)
     base = (lax.axis_index("req") * slot_count).astype(jnp.int32).reshape(1)
@@ -420,15 +441,14 @@
     heads = width // HEAD_DIM
     tiles = slot_count // TILE
     per_head = (heads, rows, HEAD_DIM)
-    parts, near_gate, near_up = pl.pallas_call(
+    parts, near_gate = pl.pallas_call(
         attend_kernel,
         out_shape=(
             jax.ShapeDtypeStruct((reqs, wide), BF16),
             VMEM(w_gate.shape, BF16),
-            VMEM(w_up.shape, BF16),
         ),
         in_specs=[pl.BlockSpec(memory_space=pltpu.SMEM)] + [vmem_spec] * 5 + [hbm_spec] * 2,
-        out_specs=[vmem_spec] * 3,
+        out_specs=[vmem_spec] * 2,
         scratch_shapes=[
             VMEM(per_head, F32),
             VMEM((rows, HEAD_DIM), F32),
@@ -438,24 +458,25 @@
             VMEM(per_head, F32),
             VMEM((tiles, heads * WIN, TILE), F32),
             VMEM((tiles, heads * WIN, TILE), BF16),
+            VMEM((slot_count, half), BF16),
             VMEM((8, HEAD_DIM), jnp.int32),
             pltpu.SMEM((8, HEAD_DIM), jnp.int32),
             pltpu.SemaphoreType.DMA,
-            pltpu.SemaphoreType.DMA((2,)),
+            pltpu.SemaphoreType.DMA((3,)),
         ],
-        compiler_params=pltpu.CompilerParams(vmem_limit_bytes=(2 + reqs // 32) << 20),
+        compiler_params=pltpu.CompilerParams(vmem_limit_bytes=(4 + reqs // 32) << 20),
         cost_estimate=pl.CostEstimate(flops=1 << 30, bytes_accessed=8 << 20, transcendentals=0),
         name="attend",
-    )(base, everyone, pool_order.reshape(1, reqs), live, keys, values, in_hbm(w_gate), in_hbm(w_up))
-
-    mine = lax.all_to_all(parts.reshape(nreq, count, wide), "req", 0, 0)
+    )(base, everyone, pool_order.reshape(1, reqs), live, keys, near, in_hbm(far), in_hbm(w_gate))
+
+    found = lax.all_to_all(parts.reshape(nreq, count, wide), "req", 0, 0)
 
     partial_attn = pl.pallas_call(
         output_kernel,
         out_shape=jax.ShapeDtypeStruct((count, model), BF16),
         compiler_params=pltpu.CompilerParams(vmem_limit_bytes=4 << 20),
         name="output",
-    )(mine, msg, new_kv, near_out)
+    )(found, mine, new_kv, w_out)
 
     here, there = pair_sum(partial_attn)
     near_down = pl.pallas_call(
@@ -476,7 +497,7 @@
         ),
         compiler_params=pltpu.CompilerParams(vmem_limit_bytes=6 << 20),
         name="feed",
-    )(tokens, here, there, ffn_gain.reshape(gain_shape), near_gate, near_up, near_down)
+    )(tokens, here, there, ffn_gain.reshape(gain_shape), near_gate, w_up, near_down)
 
     here, there = pair_sum(down_part)
     hidden_out = mid + (here.astype(F32) + there.astype(F32))

time: 51.2 us -> 46.4 us (0.906)
  local copies, waits for them, and re-layouts: 4.91 us -> 0.67 us
  waiting for transfers between devices: 6.42 us -> 9.08 us
  blocking collectives: 12.2 us -> 10.2 us
  Pallas kernels: 15.5 us -> 14.3 us
    unnamed x16 -> x12, local copies, waits for them, and re-layouts: 4.28 us -> 0.03 us
    all_to_all x1, waiting for transfers between devices: 1.19 us -> 3.85 us  [per_device(): everyone = lax.all_to_all(msg, 'req', 0, 0).reshape(reqs, wide)]
    all_to_all x1, blocking collectives: 12.2 us -> 10.2 us  [per_device(): found = lax.all_to_all(parts.reshape(nreq, count, wide), 'req', 0, 0)]
    pallas_call x1, Pallas kernels: 1.55 us -> 0.64 us  [per_device(): pl.pallas_call(output_kernel, out_shape=jax.ShapeDtypeStruct((count, mode...]
  transfers between devices with their start and end apart: 5 -> 5, of which waited for: 5 -> 5; matrix products, arithmetic and copies ran while one was open for 1% -> 1% of each run, Pallas kernels for 12% -> 13%
where the time goes in v3:
time: 46.4 us; the launch traced here: 46.1 us
  Pallas kernels  14.3 us (31%)
  starting transfers between devices  10.4 us (22%)
  blocking collectives  10.2 us (22%)
  waiting for transfers between devices  9.08 us (20%)
  between operations  0.72 us (2%)
  other arithmetic  0.71 us (2%)
  local copies, waits for them, and re-layouts  0.67 us (1%)
    all_to_all x1, blocking collectives, per_device(): found = lax.all_to_all(parts.reshape(nreq, count, wide), 'req', 0, 0)  10.2 us
    all_to_all x1, starting transfers between devices, per_device(): everyone = lax.all_to_all(msg, 'req', 0, 0).reshape(reqs, wide)  7.29 us
    ppermute x4, waiting for transfers between devices, swap(): lax.ppermute(x, axis, [(i, i ^ distance) for i in range(lax.axis_size(axi...  5.23 us
    all_to_all x1, waiting for transfers between devices, per_device(): everyone = lax.all_to_all(msg, 'req', 0, 0).reshape(reqs, wide)  3.85 us
    pallas_call x1, Pallas kernels, per_device(): pl.pallas_call(prepare_kernel, out_shape=(VMEM((count, 2 * half), F32), V...  3.7 us
    pallas_call x1, Pallas kernels, per_device(): pl.pallas_call(attend_kernel, out_shape=(jax.ShapeDtypeStruct((reqs, wide...  3.3 us
    ppermute x4, starting transfers between devices, swap(): lax.ppermute(x, axis, [(i, i ^ distance) for i in range(lax.axis_size(axi...  3.12 us
    pallas_call x1, Pallas kernels, per_device(): pl.pallas_call(project_kernel, out_shape=(VMEM((nreq, count, wide), BF16)...  2.63 us
  transfers between devices with their start and end apart: 5, of which 5 were waited for; matrix products, arithmetic and copies ran while one was open for 1% of the time, Pallas kernels for 13%

profile of v3, /device:TPU:0, one launch (start us, length us, event | category | flops | bytes accessed | tf_op | source)
XLA Modules:
  0.0 46.1 jit_solution(6273143540484512248)
XLA Ops:
  0.6 0.0 copy-start.3
  0.6 0.0 copy-start.5
  0.7 2.6 %project.1 = (bf16[8,16,640]{2,1,0:T(8,128)(2,1)}, bf16[16,640]{1,0:T(8,128)(2,1)S(1)}, bf16[16,2048]{1,0:T(8,128)(2,1)S(1)}, f32[16,128]{1,0:T(8,128)S(1)}, f32[16,128]{1,0:T(8,128)S(1)}) custom-call(bf16[16,2048]{1,0:T(8,128)(2,1)} %tokens_ref.1, bf16[16,128]{1,0:T(8,128)(2,1)} %bitcast.20, s32[1,16]{1,0:T(1,128)} %bitcast.21, s32[1,16]{1,0:T(1,128)} %bitcast.22, ...), custom_call_target="tpu_custom_call" | custom-call | flops 33554432 | bytes 3145728 | tf_op jit(solution)/shard_map/project/pallas_call | solution.py:378
  3.3 7.3 %all-to-all-start = ((bf16[8,16,640]{2,1,0:T(8,128)(2,1)}), bf16[8,16,640]{2,1,0:T(8,128)(2,1)S(1)}, u32[]{:S(2)}, u32[]{:S(2)}) async-start(bf16[8,16,640]{2,1,0:T(8,128)(2,1)} %get-tuple-element.15), calls=%async_computation | async-start | bytes 327680 | tf_op jit(solution)/shard_map/all_to_all | solution.py:410
  10.6 3.7 %prepare.1 = (f32[16,512]{1,0:T(8,128)S(1)}, bf16[4096,256]{1,0:T(8,128)(2,1)S(1)}, bf16[2048,256]{1,0:T(8,128)(2,1)S(1)}, bf16[2048,256]{1,0:T(8,128)(2,1)}) custom-call(bf16[16,2048]{1,0:T(8,128)(2,1)S(1)} %get-tuple-element.16.normed_ref, f32[16,128]{1,0:T(8,128)S(1)} %get-tuple-element.17.cos_ref, f32[16,128]{1,0:T(8,128)S(1)} %get-tuple-element.18.sin_ref, ...), custom_call_target="tpu_custom_call" | custom-call | flops 33554432 | bytes 6291456 | tf_op jit(solution)/shard_map/prepare/pallas_call | solution.py:414
  14.3 3.9 %all-to-all-done = bf16[8,16,640]{2,1,0:T(8,128)(2,1)S(1)} async-done(((bf16[8,16,640]{2,1,0:T(8,128)(2,1)}), bf16[8,16,640]{2,1,0:T(8,128)(2,1)S(1)}, u32[]{:S(2)}, u32[]{:S(2)}) %all-to-all-start) | async-done | bytes 163872 | tf_op jit(solution)/shard_map/all_to_all | solution.py:410
  18.1 0.0 copy-done.3
  18.2 0.0 copy-done.5
  18.2 0.0 copy-start.1
  18.2 3.3 %attend.1 = (bf16[128,640]{1,0:T(8,128)(2,1)S(1)}, bf16[2048,1024]{1,0:T(8,128)(2,1)S(1)}) custom-call(s32[1]{0:T(128)} %bitcast.base_ref, bf16[128,640]{1,0:T(8,128)(2,1)S(1)} %bitcast.14, s32[1,128]{1,0:T(1,128)S(1)} %bitcast.18, s32[32,128]{1,0:T(8,128)S(1)} %bitcast.16, bf16[4096,256]{1,0:T(8,128)(2,1)S(1)} %get-tuple-element.19.key_ref, ...), custom_call_target="tpu_custom_call" | custom-call | flops 1073741824 | bytes 8388608 | tf_op jit(solution)/shard_map/attend/pallas_call | solution.py:444
  21.5 10.2 %all_to_all.10.parts_ref = bf16[8,16,640]{2,1,0:T(8,128)(2,1)S(1)} all-to-all(bf16[8,16,640]{2,1,0:T(8,128)(2,1)S(1)} %bitcast.15), channel_id=1, replica_groups=mesh['req'=8,'tp'=4] {'req'}, dimensions={0} | all-to-all | bytes 327680 | tf_op jit(solution)/shard_map/all_to_all | solution.py:472
  31.7 0.0 copy-done.1
  31.7 0.6 %output.1 = bf16[16,2048]{1,0:T(8,128)(2,1)S(1)} custom-call(bf16[8,16,640]{2,1,0:T(8,128)(2,1)S(1)} %all_to_all.10.parts_ref, bf16[16,640]{1,0:T(8,128)(2,1)S(1)} %get-tuple-element.23.msg_ref, f32[16,512]{1,0:T(8,128)S(1)} %get-tuple-element.24.kv_ref, bf16[512,2048]{1,0:T(8,128)(2,1)S(1)} %copy-done.1), custom_call_target="tpu_custom_call" | custom-call | tf_op jit(solution)/shard_map/output/pallas_call | solution.py:474
  32.3 0.0 collective-permute-start
  32.3 1.3 %collective-permute-done = bf16[16,2048]{1,0:T(8,128)(2,1)S(1)} collective-permute-done((bf16[16,2048]{1,0:T(8,128)(2,1)S(1)}, bf16[16,2048]{1,0:T(8,128)(2,1)S(1)}, u32[]{:S(2)}, u32[]{:S(2)}) %collective-permute-start) | collective-permute-done | bytes 65568 | tf_op jit(solution)/shard_map/ppermute | solution.py:338
  33.6 0.0 copy-start
  33.6 0.0 copy-start.2
  33.6 0.0 copy-start.4
  33.6 1.6 %collective-permute-start.1 = (bf16[16,2048]{1,0:T(8,128)(2,1)S(1)}, bf16[16,2048]{1,0:T(8,128)(2,1)S(1)}, u32[]{:S(2)}, u32[]{:S(2)}) collective-permute-start(bf16[16,2048]{1,0:T(8,128)(2,1)S(1)} %add_convert_fusion.1.after_hbm.here_ref), channel_id=1, source_target_pairs={{0,2},{1,3},{2,0},{3,1},{4,6},{5,7},{6,4},{7,5},{8,10},{9,11},{10,... | collective-permute-start | bytes 196616 | tf_op jit(solution)/shard_map/ppermute | solution.py:338
  35.2 2.2 %load.1.wd_ref = bf16[1024,2048]{1,0:T(8,128)(2,1)S(1)} custom-call(bf16[16,2048]{1,0:T(8,128)(2,1)S(1)} %add_convert_fusion.1.after_hbm.here_ref, bf16[1024,2048]{1,0:T(8,128)(2,1)} %w_hbm.1), custom_call_target="tpu_custom_call" | custom-call | bytes 4194304 | tf_op jit(solution)/shard_map/load/pallas_call | solution.py:482
  37.4 0.6 %collective-permute-done.1.there_ref = bf16[16,2048]{1,0:T(8,128)(2,1)S(1)} collective-permute-done((bf16[16,2048]{1,0:T(8,128)(2,1)S(1)}, bf16[16,2048]{1,0:T(8,128)(2,1)S(1)}, u32[]{:S(2)}, u32[]{:S(2)}) %collective-permute-start.1) | collective-permute-done | bytes 65568 | tf_op jit(solution)/shard_map/ppermute | solution.py:338
  38.0 0.0 copy-done
  38.0 0.0 copy-done.2
  38.0 0.0 copy-done.4
  38.0 1.9 %feed.1 = (bf16[16,2048]{1,0:T(8,128)(2,1)S(1)}, f32[16,2048]{1,0:T(8,128)S(1)}) custom-call(bf16[16,2048]{1,0:T(8,128)(2,1)S(1)} %copy-done.2, bf16[16,2048]{1,0:T(8,128)(2,1)S(1)} %add_convert_fusion.1.after_hbm.here_ref, bf16[16,2048]{1,0:T(8,128)(2,1)S(1)} %collective-permute-done.1.there_ref, bf16[16,128]{1,0:T(8,128)(2,1)S(1)} %bitcast.17, ...), custom_call_target="tpu_custom_call" | custom-call | tf_op jit(solution)/shard_map/feed/pallas_call | solution.py:492
  39.8 0.0 collective-permute-start.2
  39.8 1.3 %collective-permute-done.2 = bf16[16,2048]{1,0:T(8,128)(2,1)S(1)} collective-permute-done((bf16[16,2048]{1,0:T(8,128)(2,1)S(1)}, bf16[16,2048]{1,0:T(8,128)(2,1)S(1)}, u32[]{:S(2)}, u32[]{:S(2)}) %collective-permute-start.2) | collective-permute-done | bytes 65568 | tf_op jit(solution)/shard_map/ppermute | solution.py:338
  41.1 1.6 %collective-permute-start.3 = (bf16[16,2048]{1,0:T(8,128)(2,1)S(1)}, bf16[16,2048]{1,0:T(8,128)(2,1)S(1)}, u32[]{:S(2)}, u32[]{:S(2)}) collective-permute-start(bf16[16,2048]{1,0:T(8,128)(2,1)S(1)} %add_convert_fusion), channel_id=1, source_target_pairs={{0,2},{1,3},{2,0},{3,1},{4,6},{5,7},{6,4},{7,5},{8,10},{9,11},{10,... | collective-permute-start | bytes 196616 | tf_op jit(solution)/shard_map/ppermute | solution.py:338
  42.7 0.6 %reshape.55 = f32[16,2,256]{2,1,0:T(2,128)} reshape(f32[16,512]{1,0:T(8,128)S(1)} %get-tuple-element.24.kv_ref) | data formatting | bytes 65536 | tf_op jit(solution)/shard_map/reshape | solution.py:504
  43.3 2.1 %collective-permute-done.3 = bf16[16,2048]{1,0:T(8,128)(2,1)S(1)} collective-permute-done((bf16[16,2048]{1,0:T(8,128)(2,1)S(1)}, bf16[16,2048]{1,0:T(8,128)(2,1)S(1)}, u32[]{:S(2)}, u32[]{:S(2)}) %collective-permute-start.3) | collective-permute-done | bytes 65568 | tf_op jit(solution)/shard_map/ppermute | solution.py:338
  45.4 0.7 %add_add_fusion = f32[16,2048]{1,0:T(8,128)} fusion(f32[16,2048]{1,0:T(8,128)S(1)} %get-tuple-element.26, bf16[16,2048]{1,0:T(8,128)(2,1)S(1)} %collective-permute-done.3, bf16[16,2048]{1,0:T(8,128)(2,1)S(1)} %add_convert_fusion), kind=kLoop, calls=%fused_computation | loop fusion | flops 131072 | bytes 393216 | tf_op jit(solution)/shard_map/add | solution.py:503
  (2 shorter events, 0.0 us)
Async XLA Ops:
  0.6 17.5 %copy-start.3 = (s32[4096]{0:T(1024)S(1)}, s32[4096]{0:T(1024)}, u32[]{:S(2)}) copy-start(s32[4096]{0:T(1024)} %param.20) | copy-start | bytes 49156
  0.6 17.5 %copy-start.5 = (s32[128]{0:T(128)S(1)}, s32[128]{0:T(128)}, u32[]{:S(2)}) copy-start(s32[128]{0:T(128)} %param.18) | copy-start | bytes 1540
  3.3 14.9 %all-to-all-start = ((bf16[8,16,640]{2,1,0:T(8,128)(2,1)}), bf16[8,16,640]{2,1,0:T(8,128)(2,1)S(1)}, u32[]{:S(2)}, u32[]{:S(2)}) async-start(bf16[8,16,640]{2,1,0:T(8,128)(2,1)} %get-tuple-element.15), calls=%async_computation | async-start | bytes 327680 | tf_op jit(solution)/shard_map/all_to_all | solution.py:410
  18.2 13.5 %copy-start.1 = (bf16[512,2048]{1,0:T(8,128)(2,1)S(1)}, bf16[512,2048]{1,0:T(8,128)(2,1)}, u32[]{:S(2)}) copy-start(bf16[512,2048]{1,0:T(8,128)(2,1)} %w_ref.1) | copy-start | bytes 6291460
  32.3 1.3 %collective-permute-start = (bf16[16,2048]{1,0:T(8,128)(2,1)S(1)}, bf16[16,2048]{1,0:T(8,128)(2,1)S(1)}, u32[]{:S(2)}, u32[]{:S(2)}) collective-permute-start(bf16[16,2048]{1,0:T(8,128)(2,1)S(1)} %output.1), channel_id=1, source_target_pairs={{0,1},{1,0},{2,3},{3,2},{4,5},{5,4},{6,7},{7,6},{8,9},{9,8},{10,11... | collective-permute-start | bytes 196616 | tf_op jit(solution)/shard_map/ppermute | solution.py:338
  33.6 4.4 %copy-start = (bf16[2048,1024]{1,0:T(8,128)(2,1)S(1)}, bf16[2048,1024]{1,0:T(8,128)(2,1)}, u32[]{:S(2)}) copy-start(bf16[2048,1024]{1,0:T(8,128)(2,1)} %wu_ref.1) | copy-start | bytes 12582916
  33.6 4.4 %copy-start.2 = (bf16[16,2048]{1,0:T(8,128)(2,1)S(1)}, bf16[16,2048]{1,0:T(8,128)(2,1)}, u32[]{:S(2)}) copy-start(bf16[16,2048]{1,0:T(8,128)(2,1)} %tokens_ref.1) | copy-start | bytes 196612
  33.6 4.4 %copy-start.4 = (bf16[2048]{0:T(1024)(128)(2,1)S(1)}, bf16[2048]{0:T(1024)(128)(2,1)}, u32[]{:S(2)}) copy-start(bf16[2048]{0:T(1024)(128)(2,1)} %param.27) | copy-start | bytes 12292
  33.6 4.3 %collective-permute-start.1 = (bf16[16,2048]{1,0:T(8,128)(2,1)S(1)}, bf16[16,2048]{1,0:T(8,128)(2,1)S(1)}, u32[]{:S(2)}, u32[]{:S(2)}) collective-permute-start(bf16[16,2048]{1,0:T(8,128)(2,1)S(1)} %add_convert_fusion.1.after_hbm.here_ref), channel_id=1, source_target_pairs={{0,2},{1,3},{2,0},{3,1},{4,6},{5,7},{6,4},{7,5},{8,10},{9,11},{10,... | collective-permute-start | bytes 196616 | tf_op jit(solution)/shard_map/ppermute | solution.py:338
  39.8 1.3 %collective-permute-start.2 = (bf16[16,2048]{1,0:T(8,128)(2,1)S(1)}, bf16[16,2048]{1,0:T(8,128)(2,1)S(1)}, u32[]{:S(2)}, u32[]{:S(2)}) collective-permute-start(bf16[16,2048]{1,0:T(8,128)(2,1)S(1)} %get-tuple-element.27), channel_id=1, source_target_pairs={{0,1},{1,0},{2,3},{3,2},{4,5},{5,4},{6,7},{7,6},{8,9},{9,8},{10,11... | collective-permute-start | bytes 196616 | tf_op jit(solution)/shard_map/ppermute | solution.py:338
  41.1 4.3 %collective-permute-start.3 = (bf16[16,2048]{1,0:T(8,128)(2,1)S(1)}, bf16[16,2048]{1,0:T(8,128)(2,1)S(1)}, u32[]{:S(2)}, u32[]{:S(2)}) collective-permute-start(bf16[16,2048]{1,0:T(8,128)(2,1)S(1)} %add_convert_fusion), channel_id=1, source_target_pairs={{0,2},{1,3},{2,0},{3,1},{4,6},{5,7},{6,4},{7,5},{8,10},{9,11},{10,... | collective-permute-start | bytes 196616 | tf_op jit(solution)/shard_map/ppermute | solution.py:338

commit v4 on v3

--- a/solution.py
+++ b/solution.py
@@ -53,14 +53,15 @@
 
 
 def project_kernel(
-    tokens_hbm, gain_hbm, place_hbm, len_hbm, freq_hbm, wq_hbm,
-    msg_ref, mine_ref, normed_ref, cos_ref, sin_ref,
-    tokens, gain, place, lens, freq, wq, sems,
+    tokens_hbm, gain_hbm, place_hbm, len_hbm, freq_hbm, order_hbm, wq_hbm,
+    msg_ref, mine_ref, normed_hbm, turn_hbm, sort_hbm, upto_hbm, back_hbm,
+    tokens, gain, place, lens, freq, order, wq, normed_ref, turn, sort_ref, upto_ref, back_ref, sems, out_sems,
 ):
     sources, count, wide = msg_ref.shape
     width = wide - HEAD_DIM
     rows = wq.shape[0] // PIECES
-    small = [(tokens_hbm, tokens), (gain_hbm, gain), (place_hbm, place), (len_hbm, lens), (freq_hbm, freq)]
+    small = [(tokens_hbm, tokens), (gain_hbm, gain), (place_hbm, place), (len_hbm, lens)]
+    small += [(freq_hbm, freq), (order_hbm, order)]
     slabs = [pl.ds(i * rows, rows) for i in range(PIECES)]
     copies = fetch(small + [(wq_hbm.at[at, :], wq.at[at, :]) for at in slabs], sems)
     for copy in copies[: len(small)]:
@@ -71,11 +72,21 @@
     angle = column(place, count) * freq[...]
     cosine = jnp.cos(angle)
     sine = jnp.where(lane < HEAD_DIM // 2, -1.0, 1.0) * jnp.sin(angle)
-    cos_ref[...] = cosine
-    sin_ref[...] = sine
+    turn[0:count, :] = cosine
+    turn[count:, :] = sine
     length = column(lens, count)
     high = jnp.floor(length * (1.0 / 128.0))
     coded = jnp.where(lane < HEAD_DIM // 2, high, length - 128.0 * high).astype(BF16)
+    reqs = order.shape[1]
+    row = lax.broadcasted_iota(jnp.int32, (reqs, reqs), 0)
+    col = lax.broadcasted_iota(jnp.int32, (reqs, reqs), 1)
+    sort = (column(order, reqs) == col.astype(F32)).astype(F32)
+    sort_ref[...] = sort.astype(BF16)
+    rank = jnp.sum(sort * row.astype(F32), axis=0, keepdims=True)
+    upto_ref[...] = (rank <= row.astype(F32)).astype(F32).astype(BF16)
+    back_ref[...] = (order[...] == row).astype(F32).astype(BF16)
+    early = [(normed_ref, normed_hbm), (turn, turn_hbm), (sort_ref, sort_hbm), (upto_ref, upto_hbm), (back_ref, back_hbm)]
+    outs = fetch(early, out_sems)
     q = jnp.zeros((count, width), F32)
     for copy, at in zip(copies[len(small) :], slabs):
         copy.wait()
@@ -88,23 +99,26 @@
     mine_ref[...] = msg
     for r in range(sources):
         msg_ref[r, :, :] = msg
+    for out in outs:
+        out.wait()
 
 
 def prepare_kernel(
-    normed_ref, cos_ref, sin_ref, wk_hbm, wv_hbm, cache_hbm,
+    normed_hbm, turn_hbm, wk_hbm, wv_hbm, cache_hbm,
     kv_ref, key_ref, near_ref, far_hbm,
-    wk, wv, cache, wide, far, sems, out_sems,
+    normed_ref, turn, wk, wv, cache, wide, far, sems, out_sems,
 ):
     half = wk.shape[1]
     slabs = cache.shape[0] // SLAB
     per_slot = 2 * half // HEAD_DIM
     spots = [pl.ds(i * SLAB, SLAB) for i in range(slabs)]
     wanted = [(cache_hbm.at[at, :], cache.at[at, :]) for at in spots]
-    copies = fetch([(wk_hbm, wk), (wv_hbm, wv)] + wanted, sems)
+    copies = fetch([(normed_hbm, normed_ref), (turn_hbm, turn), (wk_hbm, wk), (wv_hbm, wv)] + wanted, sems)
+    for _ in range(3):
+        copies.pop(0).wait()
     normed = normed_ref[...]
-    cosine = cos_ref[...]
-    sine = sin_ref[...]
-    copies.pop(0).wait()
+    cosine = turn[0 : turn.shape[0] // 2, :]
+    sine = turn[turn.shape[0] // 2 :, :]
     k = mm(normed, wk[...])
     for low in range(0, half, HEAD_DIM):
         x = k[:, low : low + HEAD_DIM]
@@ -131,8 +145,8 @@
 
 
 def attend_kernel(
-    base_ref, msg_ref, order_ref, live_ref, key_ref, near_ref, far_hbm, wg_hbm,
-    out_ref, wg_ref,
+    base_ref, msg_ref, sort_ref, upto_ref, back_ref, live_ref, key_ref, near_ref, far_hbm, later_hbm,
+    out_ref,
     queries, starts, ends, top, total, summed, held, weights, value_ref, ranks, ranks_s, sem, load_sems,
 ):
     middle = far_hbm.shape[0]
@@ -140,7 +154,6 @@
         [
             (far_hbm, value_ref.at[pl.ds(0, middle), :]),
             (near_ref, value_ref.at[pl.ds(middle, middle), :]),
-            (wg_hbm, wg_ref),
         ],
         load_sems,
     )
@@ -152,10 +165,6 @@
     factor = LOG2E / math.sqrt(HEAD_DIM)
     base = base_ref[0].astype(F32)
 
-    row = lax.broadcasted_iota(jnp.int32, (reqs, reqs), 0)
-    col = lax.broadcasted_iota(jnp.int32, (reqs, reqs), 1)
-    place = (order_ref[...] == row).astype(F32).astype(BF16)
-    parts = mm(place, msg_ref[:, width:], ((0,), (0,))).astype(BF16)
     lane = lax.broadcasted_iota(jnp.int32, (reqs, HEAD_DIM), 1)
     high_half = lane < HEAD_DIM // 2
 
@@ -163,27 +172,28 @@
         turned = pltpu.roll(counts, HEAD_DIM // 2, 1)
         return jnp.where(high_half, 128.0 * counts + turned, counts + 128.0 * turned)
 
-    upto = joined(mm((col <= row).astype(F32).astype(BF16), parts)) - base
+    upto = joined(mm(upto_ref[...], msg_ref[:, width:])) - base
     edge = (lane * TILE).astype(F32)
-    first = jnp.sum((upto <= edge).astype(F32), axis=0, keepdims=True)
-    last = jnp.sum((upto <= edge + (TILE - 1)).astype(F32), axis=0, keepdims=True)
-    ranks[0:1, :] = first.astype(jnp.int32)
-    ranks[1:2, :] = last.astype(jnp.int32)
+    first = jnp.sum((upto <= edge).astype(F32), axis=0, keepdims=True).astype(jnp.int32)
+    last = jnp.sum((upto <= edge + (TILE - 1)).astype(F32), axis=0, keepdims=True).astype(jnp.int32)
+    begins = [first[0, t] for t in range(tiles)]
+    widest = jnp.max(jnp.where(lane[0:1, :] < tiles, last - first, 0))
+    ranks[0:1, :] = first
+    ranks[1:2, :] = last
     copy = pltpu.make_async_copy(ranks, ranks_s, sem)
     copy.start()
+    sorted_msg = mm(sort_ref[...], msg_ref[...])
     far = jnp.full((WIN, HEAD_DIM), 1e9, F32)
     ends[0:reqs, :] = upto
     ends[reqs:, :] = far
-    starts[0:reqs, :] = upto - joined(parts.astype(F32))
+    starts[0:reqs, :] = upto - joined(sorted_msg[:, width:])
     starts[reqs:, :] = far
-    sorted_q = mm(place, msg_ref[:, :width], ((0,), (0,)))
     for h in range(heads):
-        queries[h, 0:reqs, :] = sorted_q[:, h * HEAD_DIM : (h + 1) * HEAD_DIM]
+        queries[h, 0:reqs, :] = sorted_msg[:, h * HEAD_DIM : (h + 1) * HEAD_DIM]
         queries[h, reqs:, :] = jnp.zeros((WIN, HEAD_DIM), F32)
     top[...] = jnp.full(top.shape, LOWEST, F32)
     total[...] = jnp.zeros(total.shape, F32)
     summed[...] = jnp.zeros(summed.shape, F32)
-    copy.wait()
 
     def spot(h, rank):
         return (h, pl.ds(rank, WIN), slice(None))
@@ -218,7 +228,6 @@
             of_head(value, h)[:, (h // group) * HEAD_DIM : (h // group + 1) * HEAD_DIM] for h in range(heads)
         ]
 
-    begins = [ranks_s[0, t] for t in range(tiles)]
     for t in range(tiles):
         held[t, :, :] = masked_scores(t, begins[t])
     peaks = [jnp.max(held[t, :, :], axis=1, keepdims=True) for t in range(tiles)]
@@ -264,7 +273,11 @@
 
         return lax.fori_loop(0, (ranks_s[1, t] - begin) // WIN, again, carry)
 
-    lax.fori_loop(0, tiles, more, 0)
+    copy.wait()
+
+    @pl.when(widest >= WIN)
+    def _():
+        lax.fori_loop(0, tiles, more, 0)
 
     columns = []
     extra = jnp.zeros((reqs, HEAD_DIM), F32)
@@ -279,17 +292,11 @@
             extra = jnp.where(lane == piece * heads + h, coded, extra)
             rest = rest - coded
     both = jnp.concatenate(columns + [extra.astype(BF16)], axis=1)
-    out_ref[...] = mm(place, both).astype(BF16)
-    loads[2].wait()
-
-
-def load_kernel(after_hbm, w_hbm, w_ref, sem):
-    copy = pltpu.make_async_copy(w_hbm, w_ref, sem)
-    copy.start()
-    copy.wait()
-
-
-def output_kernel(parts_ref, msg_ref, kv_ref, w_ref, out_ref):
+    out_ref[...] = mm(back_ref[...], both).astype(BF16)
+
+
+def output_kernel(parts_ref, msg_ref, kv_ref, w_ref, *rest):
+    out_ref = rest[-1]
     sources, count, wide = parts_ref.shape
     width = wide - HEAD_DIM
     heads = width // HEAD_DIM
@@ -375,27 +382,26 @@
     freq = jnp.asarray((ROPE_BASE ** (-(pair * 2.0) / HEAD_DIM)).astype(np.float32)).reshape(1, HEAD_DIM)
     gain_shape = (model // HEAD_DIM, HEAD_DIM)
 
-    msg, mine, normed, cosine, sine = pl.pallas_call(
+    sizes = [((count, model), BF16), ((2 * count, HEAD_DIM), F32)]
+    sizes += [((reqs, reqs), BF16)] * 3
+    msg, mine, normed, turn, sort, upto, back = pl.pallas_call(
         project_kernel,
-        out_shape=(
-            VMEM((nreq, count, wide), BF16),
-            VMEM((count, wide), BF16),
-            VMEM((count, model), BF16),
-            VMEM((count, HEAD_DIM), F32),
-            VMEM((count, HEAD_DIM), F32),
-        ),
-        in_specs=[hbm_spec] * 6,
-        out_specs=[vmem_spec] * 5,
+        out_shape=[jax.ShapeDtypeStruct((nreq, count, wide), BF16), VMEM((count, wide), BF16)]
+        + [pltpu.HBM(*size) for size in sizes],
+        in_specs=[hbm_spec] * 7,
+        out_specs=[vmem_spec] * 2 + [hbm_spec] * 5,
         scratch_shapes=[
             VMEM((count, model), BF16),
             VMEM(gain_shape, BF16),
             VMEM((1, count), jnp.int32),
             VMEM((1, count), jnp.int32),
             VMEM((1, HEAD_DIM), F32),
+            VMEM((1, reqs), jnp.int32),
             VMEM((model, width), BF16),
-            pltpu.SemaphoreType.DMA((5 + PIECES,)),
-        ],
-        compiler_params=pltpu.CompilerParams(vmem_limit_bytes=4 << 20),
+        ]
+        + [VMEM(*size) for size in sizes]
+        + [pltpu.SemaphoreType.DMA((6 + PIECES,)), pltpu.SemaphoreType.DMA((5,))],
+        compiler_params=pltpu.CompilerParams(vmem_limit_bytes=(4 + (reqs // 128) ** 2) << 20),
         cost_estimate=pl.CostEstimate(flops=2 * count * model * width, bytes_accessed=3 * model * width, transcendentals=0),
         name="project",
     )(
@@ -404,6 +410,7 @@
         in_hbm(positions.reshape(1, count)),
         in_hbm(lengths.reshape(1, count)),
         in_hbm(freq),
+        in_hbm(pool_order.reshape(1, reqs)),
         in_hbm(w_query),
     )
 
@@ -419,21 +426,23 @@
             VMEM((slot_count // 2, half), BF16),
             pltpu.HBM((slot_count // 2, half), BF16),
         ),
-        in_specs=[vmem_spec] * 3 + [hbm_spec] * 3,
+        in_specs=[hbm_spec] * 5,
         out_specs=[vmem_spec, vmem_spec, vmem_spec, hbm_spec],
         scratch_shapes=[
+            VMEM((count, model), BF16),
+            VMEM((2 * count, HEAD_DIM), F32),
             VMEM((model, half), BF16),
             VMEM((model, half), BF16),
             VMEM(cache.shape, BF16),
             VMEM((2, SLAB, HEAD_DIM), F32),
             VMEM((slot_count // 2, half), BF16),
-            pltpu.SemaphoreType.DMA((cache.shape[0] // SLAB + 2,)),
+            pltpu.SemaphoreType.DMA((cache.shape[0] // SLAB + 4,)),
             pltpu.SemaphoreType.DMA((cache.shape[0] // SLAB // 8,)),
         ],
         compiler_params=pltpu.CompilerParams(vmem_limit_bytes=12 << 20),
         cost_estimate=pl.CostEstimate(flops=4 * count * model * half, bytes_accessed=3 * cache.size, transcendentals=0),
         name="prepare",
-    )(normed, cosine, sine, in_hbm(w_key), in_hbm(w_value), in_hbm(cache))
+    )(in_hbm(normed), in_hbm(turn), in_hbm(w_key), in_hbm(w_value), in_hbm(cache))
 
     live = slot_mask.reshape(slot_count // SUB, SUB)
     base = (lax.axis_index("req") * slot_count).astype(jnp.int32).reshape(1)
@@ -441,14 +450,11 @@
     heads = width // HEAD_DIM
     tiles = slot_count // TILE
     per_head = (heads, rows, HEAD_DIM)
-    parts, near_gate = pl.pallas_call(
+    parts = pl.pallas_call(
         attend_kernel,
-        out_shape=(
-            jax.ShapeDtypeStruct((reqs, wide), BF16),
-            VMEM(w_gate.shape, BF16),
-        ),
-        in_specs=[pl.BlockSpec(memory_space=pltpu.SMEM)] + [vmem_spec] * 5 + [hbm_spec] * 2,
-        out_specs=[vmem_spec] * 2,
+        out_shape=jax.ShapeDtypeStruct((reqs, wide), BF16),
+        in_specs=[pl.BlockSpec(memory_space=pltpu.SMEM)] + [vmem_spec] * 7 + [hbm_spec] * 2,
+        out_specs=vmem_spec,
         scratch_shapes=[
             VMEM(per_head, F32),
             VMEM((rows, HEAD_DIM), F32),
@@ -462,33 +468,25 @@
             VMEM((8, HEAD_DIM), jnp.int32),
             pltpu.SMEM((8, HEAD_DIM), jnp.int32),
             pltpu.SemaphoreType.DMA,
-            pltpu.SemaphoreType.DMA((3,)),
+            pltpu.SemaphoreType.DMA((2,)),
         ],
         compiler_params=pltpu.CompilerParams(vmem_limit_bytes=(4 + reqs // 32) << 20),
         cost_estimate=pl.CostEstimate(flops=1 << 30, bytes_accessed=8 << 20, transcendentals=0),
         name="attend",
-    )(base, everyone, pool_order.reshape(1, reqs), live, keys, near, in_hbm(far), in_hbm(w_gate))
+    )(base, everyone, sort, upto, back, live, keys, near, in_hbm(far), in_hbm(w_gate))
 
     found = lax.all_to_all(parts.reshape(nreq, count, wide), "req", 0, 0)
 
     partial_attn = pl.pallas_call(
         output_kernel,
         out_shape=jax.ShapeDtypeStruct((count, model), BF16),
+        in_specs=[vmem_spec] * 4 + [hbm_spec] * 3,
+        out_specs=vmem_spec,
         compiler_params=pltpu.CompilerParams(vmem_limit_bytes=4 << 20),
         name="output",
-    )(found, mine, new_kv, w_out)
+    )(found, mine, new_kv, w_out, in_hbm(w_gate), in_hbm(w_up), in_hbm(w_down))
 
     here, there = pair_sum(partial_attn)
-    near_down = pl.pallas_call(
-        load_kernel,
-        out_shape=VMEM(w_down.shape, BF16),
-        in_specs=[pl.BlockSpec(memory_space=pl.ANY), hbm_spec],
-        out_specs=vmem_spec,
-        scratch_shapes=[pltpu.SemaphoreType.DMA],
-        compiler_params=pltpu.CompilerParams(vmem_limit_bytes=1 << 20),
-        cost_estimate=pl.CostEstimate(flops=0, bytes_accessed=2 * w_down.size, transcendentals=0),
-        name="load",
-    )(here, in_hbm(w_down))
     down_part, mid = pl.pallas_call(
         feed_kernel,
         out_shape=(
@@ -497,7 +495,7 @@
         ),
         compiler_params=pltpu.CompilerParams(vmem_limit_bytes=6 << 20),
         name="feed",
-    )(tokens, here, there, ffn_gain.reshape(gain_shape), near_gate, w_up, near_down)
+    )(tokens, here, there, ffn_gain.reshape(gain_shape), w_gate, w_up, w_down)
 
     here, there = pair_sum(down_part)
     hidden_out = mid + (here.astype(F32) + there.astype(F32))

time: 46.4 us -> 45.7 us (0.985)
  Pallas kernels: 14.3 us -> 11.2 us
  waiting for transfers between devices: 9.08 us -> 11.2 us
    pallas_call x3 -> x2, Pallas kernels: 8.13 us -> 4.96 us  [the longest x1 2.73 us: per_device(): pl.pallas_call(project_kernel, out_shape=[jax.ShapeDtypeStruct((nreq, cou...]
    ppermute x4, waiting for transfers between devices: 5.23 us -> 7.43 us  [swap(): lax.ppermute(x, axis, [(i, i ^ distance) for i in range(lax.axis_size(axi...]
  transfers between devices with their start and end apart: 5 -> 5, of which waited for: 5 -> 5; matrix products, arithmetic and copies ran while one was open for 1% -> 1% of each run, Pallas kernels for 13% -> 8%
where the time goes in v4:
time: 45.7 us; the launch traced here: 45.3 us
  Pallas kernels  11.2 us (25%)
  waiting for transfers between devices  11.2 us (25%)
  starting transfers between devices  10.5 us (23%)
  blocking collectives  10.2 us (22%)
  between operations  0.77 us (2%)
  other arithmetic  0.71 us (2%)
  local copies, waits for them, and re-layouts  0.68 us (1%)
    all_to_all x1, blocking collectives, per_device(): found = lax.all_to_all(parts.reshape(nreq, count, wide), 'req', 0, 0)  10.2 us
    ppermute x4, waiting for transfers between devices, swap(): lax.ppermute(x, axis, [(i, i ^ distance) for i in range(lax.axis_size(axi...  7.43 us
    all_to_all x1, starting transfers between devices, per_device(): everyone = lax.all_to_all(msg, 'req', 0, 0).reshape(reqs, wide)  7.42 us
    pallas_call x1, Pallas kernels, per_device(): pl.pallas_call(prepare_kernel, out_shape=(VMEM((count, 2 * half), F32), V...  3.78 us
    all_to_all x1, waiting for transfers between devices, per_device(): everyone = lax.all_to_all(msg, 'req', 0, 0).reshape(reqs, wide)  3.78 us
    ppermute x4, starting transfers between devices, swap(): lax.ppermute(x, axis, [(i, i ^ distance) for i in range(lax.axis_size(axi...  3.12 us
    pallas_call x1, Pallas kernels, per_device(): pl.pallas_call(project_kernel, out_shape=[jax.ShapeDtypeStruct((nreq, cou...  2.73 us
    pallas_call x1, Pallas kernels, per_device(): pl.pallas_call(attend_kernel, out_shape=jax.ShapeDtypeStruct((reqs, wide)...  2.24 us
  transfers between devices with their start and end apart: 5, of which 5 were waited for; matrix products, arithmetic and copies ran while one was open for 1% of the time, Pallas kernels for 8%

profile of v4, /device:TPU:0, one launch (start us, length us, event | category | flops | bytes accessed | tf_op | source)
XLA Modules:
  0.0 45.3 jit_solution(6092831232694204202)
XLA Ops:
  0.6 0.0 copy-start.8
  0.6 2.7 %project.1 = (bf16[8,16,640]{2,1,0:T(8,128)(2,1)}, bf16[16,640]{1,0:T(8,128)(2,1)S(1)}, bf16[16,2048]{1,0:T(8,128)(2,1)}, f32[32,128]{1,0:T(8,128)}, bf16[128,12...) custom-call(bf16[16,2048]{1,0:T(8,128)(2,1)} %tokens_ref.1, bf16[16,128]{1,0:T(8,128)(2,1)} %bitcast.19, ...), custom_call_target="tpu_custom_call" | custom-call | flops 33554432 | bytes 3145728 | tf_op jit(solution)/shard_map/project/pallas_call | solution.py:387
  3.4 0.0 copy-start.5
  3.4 0.0 copy-start.6
  3.4 0.0 copy-start.7
  3.4 7.4 %all-to-all-start = ((bf16[8,16,640]{2,1,0:T(8,128)(2,1)}), bf16[8,16,640]{2,1,0:T(8,128)(2,1)S(1)}, u32[]{:S(2)}, u32[]{:S(2)}) async-start(bf16[8,16,640]{2,1,0:T(8,128)(2,1)} %get-tuple-element.15), calls=%async_computation | async-start | bytes 327680 | tf_op jit(solution)/shard_map/all_to_all | solution.py:417
  10.8 3.8 %prepare.1 = (f32[16,512]{1,0:T(8,128)S(1)}, bf16[4096,256]{1,0:T(8,128)(2,1)S(1)}, bf16[2048,256]{1,0:T(8,128)(2,1)S(1)}, bf16[2048,256]{1,0:T(8,128)(2,1)}) custom-call(bf16[16,2048]{1,0:T(8,128)(2,1)} %get-tuple-element.19.normed_hbm, f32[32,128]{1,0:T(8,128)} %get-tuple-element.20.turn_hbm, bf16[2048,256]{1,0:T(8,128)(2,1)} %wk_hbm.1, ...), custom_call_target="tpu_custom_call" | custom-call | flops 33554432 | bytes 6291456 | tf_op jit(solution)/shard_map/prepare/pallas_call | solution.py:421
  14.6 3.8 %all-to-all-done = bf16[8,16,640]{2,1,0:T(8,128)(2,1)S(1)} async-done(((bf16[8,16,640]{2,1,0:T(8,128)(2,1)}), bf16[8,16,640]{2,1,0:T(8,128)(2,1)S(1)}, u32[]{:S(2)}, u32[]{:S(2)}) %all-to-all-start) | async-done | bytes 163872 | tf_op jit(solution)/shard_map/all_to_all | solution.py:417
  18.4 0.0 copy-done.8
  18.4 0.0 copy-done.5
  18.4 0.0 copy-done.6
  18.4 0.0 copy-done.7
  18.4 0.0 copy-start.3
  18.4 2.2 %attend.1 = bf16[128,640]{1,0:T(8,128)(2,1)S(1)} custom-call(s32[1]{0:T(128)} %bitcast.base_ref, bf16[128,640]{1,0:T(8,128)(2,1)S(1)} %bitcast.14, bf16[128,128]{1,0:T(8,128)(2,1)S(1)} %copy-done.5, bf16[128,128]{1,0:T(8,128)(2,1)S(1)} %copy-done.6, bf16[128,128]{1,0:T(8,128)(2,1)S(1)} %copy-done.7, s32[32,128]{1,0:T(8,128)S(1)} %bitcast.16, ...), custom_call_target="tpu_custom_call" | custom-call | flops 1073741824 | bytes 8388608 | tf_op jit(solution)/shard_map/attend/pallas_call | solution.py:453
  20.7 10.2 %all_to_all.10.parts_ref = bf16[8,16,640]{2,1,0:T(8,128)(2,1)S(1)} all-to-all(bf16[8,16,640]{2,1,0:T(8,128)(2,1)S(1)} %bitcast.15), channel_id=1, replica_groups=mesh['req'=8,'tp'=4] {'req'}, dimensions={0} | all-to-all | bytes 327680 | tf_op jit(solution)/shard_map/all_to_all | solution.py:478
  30.9 0.0 copy-done.3
  30.9 0.0 copy-start
  30.9 0.0 copy-start.1
  30.9 0.0 copy-start.2
  30.9 0.0 copy-start.4
  30.9 0.0 copy-start.9
  30.9 0.6 %output.1 = bf16[16,2048]{1,0:T(8,128)(2,1)S(1)} custom-call(bf16[8,16,640]{2,1,0:T(8,128)(2,1)S(1)} %all_to_all.10.parts_ref, bf16[16,640]{1,0:T(8,128)(2,1)S(1)} %get-tuple-element.24.msg_ref, f32[16,512]{1,0:T(8,128)S(1)} %get-tuple-element.25.kv_ref, bf16[512,2048]{1,0:T(8,128)(2,1)S(1)} %copy-done.3, bf16[2048,1024]{1,0:T(8,128)(2,1)} %wg_ref.1, ...), custom_call_target="tpu_custom_call" | custom-call | tf_op jit(solution)/shard_map/output/pallas_call | solution.py:480
  31.5 0.0 collective-permute-start
  31.6 1.3 %collective-permute-done = bf16[16,2048]{1,0:T(8,128)(2,1)S(1)} collective-permute-done((bf16[16,2048]{1,0:T(8,128)(2,1)S(1)}, bf16[16,2048]{1,0:T(8,128)(2,1)S(1)}, u32[]{:S(2)}, u32[]{:S(2)}) %collective-permute-start) | collective-permute-done | bytes 65568 | tf_op jit(solution)/shard_map/ppermute | solution.py:345
  32.8 1.6 %collective-permute-start.1 = (bf16[16,2048]{1,0:T(8,128)(2,1)S(1)}, bf16[16,2048]{1,0:T(8,128)(2,1)S(1)}, u32[]{:S(2)}, u32[]{:S(2)}) collective-permute-start(bf16[16,2048]{1,0:T(8,128)(2,1)S(1)} %add_convert_fusion.1.here_ref), channel_id=1, source_target_pairs={{0,2},{1,3},{2,0},{3,1},{4,6},{5,7},{6,4},{7,5},{8,10},{9,11},{10,... | collective-permute-start | bytes 196616 | tf_op jit(solution)/shard_map/ppermute | solution.py:345
  34.4 2.8 %collective-permute-done.1.there_ref = bf16[16,2048]{1,0:T(8,128)(2,1)S(1)} collective-permute-done((bf16[16,2048]{1,0:T(8,128)(2,1)S(1)}, bf16[16,2048]{1,0:T(8,128)(2,1)S(1)}, u32[]{:S(2)}, u32[]{:S(2)}) %collective-permute-start.1) | collective-permute-done | bytes 65568 | tf_op jit(solution)/shard_map/ppermute | solution.py:345
  37.2 0.0 copy-done
  37.2 0.0 copy-done.1
  37.2 0.0 copy-done.2
  37.2 0.0 copy-done.4
  37.2 0.0 copy-done.9
  37.2 1.9 %feed.1 = (bf16[16,2048]{1,0:T(8,128)(2,1)S(1)}, f32[16,2048]{1,0:T(8,128)S(1)}) custom-call(bf16[16,2048]{1,0:T(8,128)(2,1)S(1)} %copy-done.4, bf16[16,2048]{1,0:T(8,128)(2,1)S(1)} %add_convert_fusion.1.here_ref, bf16[16,2048]{1,0:T(8,128)(2,1)S(1)} %collective-permute-done.1.there_ref, bf16[16,128]{1,0:T(8,128)(2,1)S(1)} %bitcast.17, ...), custom_call_target="tpu_custom_call" | custom-call | tf_op jit(solution)/shard_map/feed/pallas_call | solution.py:490
  39.0 0.0 collective-permute-start.2
  39.1 1.3 %collective-permute-done.2 = bf16[16,2048]{1,0:T(8,128)(2,1)S(1)} collective-permute-done((bf16[16,2048]{1,0:T(8,128)(2,1)S(1)}, bf16[16,2048]{1,0:T(8,128)(2,1)S(1)}, u32[]{:S(2)}, u32[]{:S(2)}) %collective-permute-start.2) | collective-permute-done | bytes 65568 | tf_op jit(solution)/shard_map/ppermute | solution.py:345
  40.3 1.6 %collective-permute-start.3 = (bf16[16,2048]{1,0:T(8,128)(2,1)S(1)}, bf16[16,2048]{1,0:T(8,128)(2,1)S(1)}, u32[]{:S(2)}, u32[]{:S(2)}) collective-permute-start(bf16[16,2048]{1,0:T(8,128)(2,1)S(1)} %add_convert_fusion), channel_id=1, source_target_pairs={{0,2},{1,3},{2,0},{3,1},{4,6},{5,7},{6,4},{7,5},{8,10},{9,11},{10,... | collective-permute-start | bytes 196616 | tf_op jit(solution)/shard_map/ppermute | solution.py:345
  41.9 0.6 %reshape.55 = f32[16,2,256]{2,1,0:T(2,128)} reshape(f32[16,512]{1,0:T(8,128)S(1)} %get-tuple-element.25.kv_ref) | data formatting | bytes 65536 | tf_op jit(solution)/shard_map/reshape | solution.py:502
  42.5 2.1 %collective-permute-done.3 = bf16[16,2048]{1,0:T(8,128)(2,1)S(1)} collective-permute-done((bf16[16,2048]{1,0:T(8,128)(2,1)S(1)}, bf16[16,2048]{1,0:T(8,128)(2,1)S(1)}, u32[]{:S(2)}, u32[]{:S(2)}) %collective-permute-start.3) | collective-permute-done | bytes 65568 | tf_op jit(solution)/shard_map/ppermute | solution.py:345
  44.7 0.7 %add_add_fusion = f32[16,2048]{1,0:T(8,128)} fusion(f32[16,2048]{1,0:T(8,128)S(1)} %get-tuple-element.26, bf16[16,2048]{1,0:T(8,128)(2,1)S(1)} %collective-permute-done.3, bf16[16,2048]{1,0:T(8,128)(2,1)S(1)} %add_convert_fusion), kind=kLoop, calls=%fused_computation | loop fusion | flops 131072 | bytes 393216 | tf_op jit(solution)/shard_map/add | solution.py:501
  (2 shorter events, 0.0 us)
Async XLA Ops:
  0.6 17.8 %copy-start.8 = (s32[4096]{0:T(1024)S(1)}, s32[4096]{0:T(1024)}, u32[]{:S(2)}) copy-start(s32[4096]{0:T(1024)} %param.20) | copy-start | bytes 49156
  3.4 15.0 %copy-start.5 = (bf16[128,128]{1,0:T(8,128)(2,1)S(1)}, bf16[128,128]{1,0:T(8,128)(2,1)}, u32[]{:S(2)}) copy-start(bf16[128,128]{1,0:T(8,128)(2,1)} %get-tuple-element.16.sort_ref) | copy-start | bytes 98308
  3.4 15.0 %copy-start.6 = (bf16[128,128]{1,0:T(8,128)(2,1)S(1)}, bf16[128,128]{1,0:T(8,128)(2,1)}, u32[]{:S(2)}) copy-start(bf16[128,128]{1,0:T(8,128)(2,1)} %get-tuple-element.17.upto_ref) | copy-start | bytes 98308
  3.4 15.0 %copy-start.7 = (bf16[128,128]{1,0:T(8,128)(2,1)S(1)}, bf16[128,128]{1,0:T(8,128)(2,1)}, u32[]{:S(2)}) copy-start(bf16[128,128]{1,0:T(8,128)(2,1)} %get-tuple-element.18.back_ref) | copy-start | bytes 98308
  3.4 15.0 %all-to-all-start = ((bf16[8,16,640]{2,1,0:T(8,128)(2,1)}), bf16[8,16,640]{2,1,0:T(8,128)(2,1)S(1)}, u32[]{:S(2)}, u32[]{:S(2)}) async-start(bf16[8,16,640]{2,1,0:T(8,128)(2,1)} %get-tuple-element.15), calls=%async_computation | async-start | bytes 327680 | tf_op jit(solution)/shard_map/all_to_all | solution.py:417
  18.4 12.5 %copy-start.3 = (bf16[512,2048]{1,0:T(8,128)(2,1)S(1)}, bf16[512,2048]{1,0:T(8,128)(2,1)}, u32[]{:S(2)}) copy-start(bf16[512,2048]{1,0:T(8,128)(2,1)} %w_ref.1) | copy-start | bytes 6291460
  30.9 6.3 %copy-start = (bf16[2048,1024]{1,0:T(8,128)(2,1)S(1)}, bf16[2048,1024]{1,0:T(8,128)(2,1)}, u32[]{:S(2)}) copy-start(bf16[2048,1024]{1,0:T(8,128)(2,1)} %wg_ref.1) | copy-start | bytes 12582916
  30.9 6.3 %copy-start.1 = (bf16[2048,1024]{1,0:T(8,128)(2,1)S(1)}, bf16[2048,1024]{1,0:T(8,128)(2,1)}, u32[]{:S(2)}) copy-start(bf16[2048,1024]{1,0:T(8,128)(2,1)} %wu_ref.1) | copy-start | bytes 12582916
  30.9 6.3 %copy-start.2 = (bf16[1024,2048]{1,0:T(8,128)(2,1)S(1)}, bf16[1024,2048]{1,0:T(8,128)(2,1)}, u32[]{:S(2)}) copy-start(bf16[1024,2048]{1,0:T(8,128)(2,1)} %wd_ref.1) | copy-start | bytes 12582916
  30.9 6.3 %copy-start.4 = (bf16[16,2048]{1,0:T(8,128)(2,1)S(1)}, bf16[16,2048]{1,0:T(8,128)(2,1)}, u32[]{:S(2)}) copy-start(bf16[16,2048]{1,0:T(8,128)(2,1)} %tokens_ref.1) | copy-start | bytes 196612
  30.9 6.3 %copy-start.9 = (bf16[2048]{0:T(1024)(128)(2,1)S(1)}, bf16[2048]{0:T(1024)(128)(2,1)}, u32[]{:S(2)}) copy-start(bf16[2048]{0:T(1024)(128)(2,1)} %param.27) | copy-start | bytes 12292
  31.5 1.3 %collective-permute-start = (bf16[16,2048]{1,0:T(8,128)(2,1)S(1)}, bf16[16,2048]{1,0:T(8,128)(2,1)S(1)}, u32[]{:S(2)}, u32[]{:S(2)}) collective-permute-start(bf16[16,2048]{1,0:T(8,128)(2,1)S(1)} %output.1), channel_id=1, source_target_pairs={{0,1},{1,0},{2,3},{3,2},{4,5},{5,4},{6,7},{7,6},{8,9},{9,8},{10,11... | collective-permute-start | bytes 196616 | tf_op jit(solution)/shard_map/ppermute | solution.py:345
  32.8 4.3 %collective-permute-start.1 = (bf16[16,2048]{1,0:T(8,128)(2,1)S(1)}, bf16[16,2048]{1,0:T(8,128)(2,1)S(1)}, u32[]{:S(2)}, u32[]{:S(2)}) collective-permute-start(bf16[16,2048]{1,0:T(8,128)(2,1)S(1)} %add_convert_fusion.1.here_ref), channel_id=1, source_target_pairs={{0,2},{1,3},{2,0},{3,1},{4,6},{5,7},{6,4},{7,5},{8,10},{9,11},{10,... | collective-permute-start | bytes 196616 | tf_op jit(solution)/shard_map/ppermute | solution.py:345
  39.0 1.3 %collective-permute-start.2 = (bf16[16,2048]{1,0:T(8,128)(2,1)S(1)}, bf16[16,2048]{1,0:T(8,128)(2,1)S(1)}, u32[]{:S(2)}, u32[]{:S(2)}) collective-permute-start(bf16[16,2048]{1,0:T(8,128)(2,1)S(1)} %get-tuple-element.27), channel_id=1, source_target_pairs={{0,1},{1,0},{2,3},{3,2},{4,5},{5,4},{6,7},{7,6},{8,9},{9,8},{10,11... | collective-permute-start | bytes 196616 | tf_op jit(solution)/shard_map/ppermute | solution.py:345
  40.3 4.3 %collective-permute-start.3 = (bf16[16,2048]{1,0:T(8,128)(2,1)S(1)}, bf16[16,2048]{1,0:T(8,128)(2,1)S(1)}, u32[]{:S(2)}, u32[]{:S(2)}) collective-permute-start(bf16[16,2048]{1,0:T(8,128)(2,1)S(1)} %add_convert_fusion), channel_id=1, source_target_pairs={{0,2},{1,3},{2,0},{3,1},{4,6},{5,7},{6,4},{7,5},{8,10},{9,11},{10,... | collective-permute-start | bytes 196616 | tf_op jit(solution)/shard_map/ppermute | solution.py:345

commit v5 on v4

--- a/solution.py
+++ b/solution.py
@@ -175,21 +175,20 @@
     upto = joined(mm(upto_ref[...], msg_ref[:, width:])) - base
     edge = (lane * TILE).astype(F32)
     first = jnp.sum((upto <= edge).astype(F32), axis=0, keepdims=True).astype(jnp.int32)
-    last = jnp.sum((upto <= edge + (TILE - 1)).astype(F32), axis=0, keepdims=True).astype(jnp.int32)
-    begins = [first[0, t] for t in range(tiles)]
-    widest = jnp.max(jnp.where(lane[0:1, :] < tiles, last - first, 0))
+    begins = [first[0, t] for t in range(tiles + 1)]
+    widest = begins[1] - begins[0]
+    for t in range(1, tiles):
+        widest = jnp.maximum(widest, begins[t + 1] - begins[t])
     ranks[0:1, :] = first
-    ranks[1:2, :] = last
-    copy = pltpu.make_async_copy(ranks, ranks_s, sem)
-    copy.start()
-    sorted_msg = mm(sort_ref[...], msg_ref[...])
+    sorted_q = mm(sort_ref[...], msg_ref[:, :width])
     far = jnp.full((WIN, HEAD_DIM), 1e9, F32)
     ends[0:reqs, :] = upto
     ends[reqs:, :] = far
-    starts[0:reqs, :] = upto - joined(sorted_msg[:, width:])
+    row = lax.broadcasted_iota(jnp.int32, (reqs, HEAD_DIM), 0)
+    starts[0:reqs, :] = jnp.where(row == 0, -base, pltpu.roll(upto, 1, 0))
     starts[reqs:, :] = far
     for h in range(heads):
-        queries[h, 0:reqs, :] = sorted_msg[:, h * HEAD_DIM : (h + 1) * HEAD_DIM]
+        queries[h, 0:reqs, :] = sorted_q[:, h * HEAD_DIM : (h + 1) * HEAD_DIM]
         queries[h, reqs:, :] = jnp.zeros((WIN, HEAD_DIM), F32)
     top[...] = jnp.full(top.shape, LOWEST, F32)
     total[...] = jnp.zeros(total.shape, F32)
@@ -271,26 +270,30 @@
                 summed[at] = summed[at] * left + value[h] * right
             return inner
 
-        return lax.fori_loop(0, (ranks_s[1, t] - begin) // WIN, again, carry)
-
-    copy.wait()
+        return lax.fori_loop(0, (ranks_s[0, t + 1] - begin) // WIN, again, carry)
 
     @pl.when(widest >= WIN)
     def _():
+        copy = pltpu.make_async_copy(ranks, ranks_s, sem)
+        copy.start()
+        copy.wait()
         lax.fori_loop(0, tiles, more, 0)
 
     columns = []
+    sums = jnp.ones((reqs, HEAD_DIM), F32)
+    peaks = jnp.zeros((reqs, HEAD_DIM), F32)
+    for h in range(heads):
+        count = total[h, 0:reqs, :]
+        columns.append((summed[h, 0:reqs, :] / jnp.where(count > 0.0, count, 1.0)).astype(BF16))
+        sums = jnp.where(lane % heads == h, count, sums)
+        peaks = jnp.where(lane % heads == h, top[h, 0:reqs, :], peaks)
+    some = sums > 0.0
+    rest = jnp.where(some, peaks + jnp.log2(jnp.where(some, sums, 1.0)), LOWEST)
     extra = jnp.zeros((reqs, HEAD_DIM), F32)
-    for h in range(heads):
-        sums = total[h, 0:reqs, :]
-        some = sums > 0.0
-        safe = jnp.where(some, sums, 1.0)
-        columns.append((summed[h, 0:reqs, :] / safe).astype(BF16))
-        rest = jnp.where(some, top[h, 0:reqs, :] + jnp.log2(safe), LOWEST)
-        for piece in range(3):
-            coded = rest.astype(BF16).astype(F32)
-            extra = jnp.where(lane == piece * heads + h, coded, extra)
-            rest = rest - coded
+    for piece in range(3):
+        coded = rest.astype(BF16).astype(F32)
+        extra = jnp.where(lane // heads == piece, coded, extra)
+        rest = rest - coded
     both = jnp.concatenate(columns + [extra.astype(BF16)], axis=1)
     out_ref[...] = mm(back_ref[...], both).astype(BF16)
 
@@ -374,7 +377,7 @@
     half = w_key.shape[1]
     kv_heads = half // HEAD_DIM
     wide = width + HEAD_DIM
-    assert slot_count % TILE == 0 and slot_count // TILE <= HEAD_DIM
+    assert slot_count % TILE == 0 and slot_count // TILE < HEAD_DIM
 
     hbm_spec = pl.BlockSpec(memory_space=pltpu.HBM)
     vmem_spec = pl.BlockSpec(memory_space=VMEM)

time: 45.7 us -> 45.6 us (level)
  no operation moved by 1% of the time
where the time goes in v5:
time: 45.6 us; the launch traced here: 45.3 us
  waiting for transfers between devices  11.2 us (25%)
  Pallas kernels  11.1 us (24%)
  starting transfers between devices  10.5 us (23%)
  blocking collectives  10.2 us (22%)
  between operations  0.77 us (2%)
  other arithmetic  0.71 us (2%)
  local copies, waits for them, and re-layouts  0.68 us (1%)
    all_to_all x1, blocking collectives, per_device(): found = lax.all_to_all(parts.reshape(nreq, count, wide), 'req', 0, 0)  10.2 us
    ppermute x4, waiting for transfers between devices, swap(): lax.ppermute(x, axis, [(i, i ^ distance) for i in range(lax.axis_size(axi...  7.43 us
    all_to_all x1, starting transfers between devices, per_device(): everyone = lax.all_to_all(msg, 'req', 0, 0).reshape(reqs, wide)  7.42 us
    pallas_call x1, Pallas kernels, per_device(): pl.pallas_call(prepare_kernel, out_shape=(VMEM((count, 2 * half), F32), V...  3.78 us
    all_to_all x1, waiting for transfers between devices, per_device(): everyone = lax.all_to_all(msg, 'req', 0, 0).reshape(reqs, wide)  3.78 us
    ppermute x4, starting transfers between devices, swap(): lax.ppermute(x, axis, [(i, i ^ distance) for i in range(lax.axis_size(axi...  3.12 us
    pallas_call x1, Pallas kernels, per_device(): pl.pallas_call(project_kernel, out_shape=[jax.ShapeDtypeStruct((nreq, cou...  2.73 us
    pallas_call x1, Pallas kernels, per_device(): pl.pallas_call(attend_kernel, out_shape=jax.ShapeDtypeStruct((reqs, wide)...  2.15 us
  transfers between devices with their start and end apart: 5, of which 5 were waited for; matrix products, arithmetic and copies ran while one was open for 1% of the time, Pallas kernels for 8%

profile of v5, /device:TPU:0, one launch (start us, length us, event | category | flops | bytes accessed | tf_op | source)
XLA Modules:
  0.0 45.3 jit_solution(3599040227608831169)
XLA Ops:
  0.6 0.0 copy-start.8
  0.6 2.7 %project.1 = (bf16[8,16,640]{2,1,0:T(8,128)(2,1)}, bf16[16,640]{1,0:T(8,128)(2,1)S(1)}, bf16[16,2048]{1,0:T(8,128)(2,1)}, f32[32,128]{1,0:T(8,128)}, bf16[128,12...) custom-call(bf16[16,2048]{1,0:T(8,128)(2,1)} %tokens_ref.1, bf16[16,128]{1,0:T(8,128)(2,1)} %bitcast.19, ...), custom_call_target="tpu_custom_call" | custom-call | flops 33554432 | bytes 3145728 | tf_op jit(solution)/shard_map/project/pallas_call | solution.py:390
  3.4 0.0 copy-start.5
  3.4 0.0 copy-start.6
  3.4 0.0 copy-start.7
  3.4 7.4 %all-to-all-start = ((bf16[8,16,640]{2,1,0:T(8,128)(2,1)}), bf16[8,16,640]{2,1,0:T(8,128)(2,1)S(1)}, u32[]{:S(2)}, u32[]{:S(2)}) async-start(bf16[8,16,640]{2,1,0:T(8,128)(2,1)} %get-tuple-element.15), calls=%async_computation | async-start | bytes 327680 | tf_op jit(solution)/shard_map/all_to_all | solution.py:420
  10.8 3.8 %prepare.1 = (f32[16,512]{1,0:T(8,128)S(1)}, bf16[4096,256]{1,0:T(8,128)(2,1)S(1)}, bf16[2048,256]{1,0:T(8,128)(2,1)S(1)}, bf16[2048,256]{1,0:T(8,128)(2,1)}) custom-call(bf16[16,2048]{1,0:T(8,128)(2,1)} %get-tuple-element.19.normed_hbm, f32[32,128]{1,0:T(8,128)} %get-tuple-element.20.turn_hbm, bf16[2048,256]{1,0:T(8,128)(2,1)} %wk_hbm.1, ...), custom_call_target="tpu_custom_call" | custom-call | flops 33554432 | bytes 6291456 | tf_op jit(solution)/shard_map/prepare/pallas_call | solution.py:424
  14.6 3.8 %all-to-all-done = bf16[8,16,640]{2,1,0:T(8,128)(2,1)S(1)} async-done(((bf16[8,16,640]{2,1,0:T(8,128)(2,1)}), bf16[8,16,640]{2,1,0:T(8,128)(2,1)S(1)}, u32[]{:S(2)}, u32[]{:S(2)}) %all-to-all-start) | async-done | bytes 163872 | tf_op jit(solution)/shard_map/all_to_all | solution.py:420
  18.4 0.0 copy-done.8
  18.4 0.0 copy-done.5
  18.4 0.0 copy-done.6
  18.4 0.0 copy-done.7
  18.4 0.0 copy-start.3
  18.4 2.1 %attend.1 = bf16[128,640]{1,0:T(8,128)(2,1)S(1)} custom-call(s32[1]{0:T(128)} %bitcast.base_ref, bf16[128,640]{1,0:T(8,128)(2,1)S(1)} %bitcast.14, bf16[128,128]{1,0:T(8,128)(2,1)S(1)} %copy-done.5, bf16[128,128]{1,0:T(8,128)(2,1)S(1)} %copy-done.6, bf16[128,128]{1,0:T(8,128)(2,1)S(1)} %copy-done.7, s32[32,128]{1,0:T(8,128)S(1)} %bitcast.16, ...), custom_call_target="tpu_custom_call" | custom-call | flops 1073741824 | bytes 8388608 | tf_op jit(solution)/shard_map/attend/pallas_call | solution.py:456
  20.6 10.2 %all_to_all.10.parts_ref = bf16[8,16,640]{2,1,0:T(8,128)(2,1)S(1)} all-to-all(bf16[8,16,640]{2,1,0:T(8,128)(2,1)S(1)} %bitcast.15), channel_id=1, replica_groups=mesh['req'=8,'tp'=4] {'req'}, dimensions={0} | all-to-all | bytes 327680 | tf_op jit(solution)/shard_map/all_to_all | solution.py:481
  30.8 0.0 copy-done.3
  30.8 0.0 copy-start
  30.8 0.0 copy-start.1
  30.8 0.0 copy-start.2
  30.8 0.0 copy-start.4
  30.8 0.0 copy-start.9
  30.8 0.6 %output.1 = bf16[16,2048]{1,0:T(8,128)(2,1)S(1)} custom-call(bf16[8,16,640]{2,1,0:T(8,128)(2,1)S(1)} %all_to_all.10.parts_ref, bf16[16,640]{1,0:T(8,128)(2,1)S(1)} %get-tuple-element.24.msg_ref, f32[16,512]{1,0:T(8,128)S(1)} %get-tuple-element.25.kv_ref, bf16[512,2048]{1,0:T(8,128)(2,1)S(1)} %copy-done.3, bf16[2048,1024]{1,0:T(8,128)(2,1)} %wg_ref.1, ...), custom_call_target="tpu_custom_call" | custom-call | tf_op jit(solution)/shard_map/output/pallas_call | solution.py:483
  31.5 0.0 collective-permute-start
  31.5 1.3 %collective-permute-done = bf16[16,2048]{1,0:T(8,128)(2,1)S(1)} collective-permute-done((bf16[16,2048]{1,0:T(8,128)(2,1)S(1)}, bf16[16,2048]{1,0:T(8,128)(2,1)S(1)}, u32[]{:S(2)}, u32[]{:S(2)}) %collective-permute-start) | collective-permute-done | bytes 65568 | tf_op jit(solution)/shard_map/ppermute | solution.py:348
  32.7 1.6 %collective-permute-start.1 = (bf16[16,2048]{1,0:T(8,128)(2,1)S(1)}, bf16[16,2048]{1,0:T(8,128)(2,1)S(1)}, u32[]{:S(2)}, u32[]{:S(2)}) collective-permute-start(bf16[16,2048]{1,0:T(8,128)(2,1)S(1)} %add_convert_fusion.1.here_ref), channel_id=1, source_target_pairs={{0,2},{1,3},{2,0},{3,1},{4,6},{5,7},{6,4},{7,5},{8,10},{9,11},{10,... | collective-permute-start | bytes 196616 | tf_op jit(solution)/shard_map/ppermute | solution.py:348
  34.3 2.8 %collective-permute-done.1.there_ref = bf16[16,2048]{1,0:T(8,128)(2,1)S(1)} collective-permute-done((bf16[16,2048]{1,0:T(8,128)(2,1)S(1)}, bf16[16,2048]{1,0:T(8,128)(2,1)S(1)}, u32[]{:S(2)}, u32[]{:S(2)}) %collective-permute-start.1) | collective-permute-done | bytes 65568 | tf_op jit(solution)/shard_map/ppermute | solution.py:348
  37.1 0.0 copy-done
  37.1 0.0 copy-done.1
  37.1 0.0 copy-done.2
  37.1 0.0 copy-done.4
  37.1 0.0 copy-done.9
  37.1 1.9 %feed.1 = (bf16[16,2048]{1,0:T(8,128)(2,1)S(1)}, f32[16,2048]{1,0:T(8,128)S(1)}) custom-call(bf16[16,2048]{1,0:T(8,128)(2,1)S(1)} %copy-done.4, bf16[16,2048]{1,0:T(8,128)(2,1)S(1)} %add_convert_fusion.1.here_ref, bf16[16,2048]{1,0:T(8,128)(2,1)S(1)} %collective-permute-done.1.there_ref, bf16[16,128]{1,0:T(8,128)(2,1)S(1)} %bitcast.17, ...), custom_call_target="tpu_custom_call" | custom-call | tf_op jit(solution)/shard_map/feed/pallas_call | solution.py:493
  39.0 0.0 collective-permute-start.2
  39.0 1.3 %collective-permute-done.2 = bf16[16,2048]{1,0:T(8,128)(2,1)S(1)} collective-permute-done((bf16[16,2048]{1,0:T(8,128)(2,1)S(1)}, bf16[16,2048]{1,0:T(8,128)(2,1)S(1)}, u32[]{:S(2)}, u32[]{:S(2)}) %collective-permute-start.2) | collective-permute-done | bytes 65568 | tf_op jit(solution)/shard_map/ppermute | solution.py:348
  40.2 1.6 %collective-permute-start.3 = (bf16[16,2048]{1,0:T(8,128)(2,1)S(1)}, bf16[16,2048]{1,0:T(8,128)(2,1)S(1)}, u32[]{:S(2)}, u32[]{:S(2)}) collective-permute-start(bf16[16,2048]{1,0:T(8,128)(2,1)S(1)} %add_convert_fusion), channel_id=1, source_target_pairs={{0,2},{1,3},{2,0},{3,1},{4,6},{5,7},{6,4},{7,5},{8,10},{9,11},{10,... | collective-permute-start | bytes 196616 | tf_op jit(solution)/shard_map/ppermute | solution.py:348
  41.8 0.6 %reshape.55 = f32[16,2,256]{2,1,0:T(2,128)} reshape(f32[16,512]{1,0:T(8,128)S(1)} %get-tuple-element.25.kv_ref) | data formatting | bytes 65536 | tf_op jit(solution)/shard_map/reshape | solution.py:505
  42.4 2.1 %collective-permute-done.3 = bf16[16,2048]{1,0:T(8,128)(2,1)S(1)} collective-permute-done((bf16[16,2048]{1,0:T(8,128)(2,1)S(1)}, bf16[16,2048]{1,0:T(8,128)(2,1)S(1)}, u32[]{:S(2)}, u32[]{:S(2)}) %collective-permute-start.3) | collective-permute-done | bytes 65568 | tf_op jit(solution)/shard_map/ppermute | solution.py:348
  44.6 0.7 %add_add_fusion = f32[16,2048]{1,0:T(8,128)} fusion(f32[16,2048]{1,0:T(8,128)S(1)} %get-tuple-element.26, bf16[16,2048]{1,0:T(8,128)(2,1)S(1)} %collective-permute-done.3, bf16[16,2048]{1,0:T(8,128)(2,1)S(1)} %add_convert_fusion), kind=kLoop, calls=%fused_computation | loop fusion | flops 131072 | bytes 393216 | tf_op jit(solution)/shard_map/add | solution.py:504
  (2 shorter events, 0.0 us)
Async XLA Ops:
  0.6 17.8 %copy-start.8 = (s32[4096]{0:T(1024)S(1)}, s32[4096]{0:T(1024)}, u32[]{:S(2)}) copy-start(s32[4096]{0:T(1024)} %param.20) | copy-start | bytes 49156
  3.4 15.0 %copy-start.5 = (bf16[128,128]{1,0:T(8,128)(2,1)S(1)}, bf16[128,128]{1,0:T(8,128)(2,1)}, u32[]{:S(2)}) copy-start(bf16[128,128]{1,0:T(8,128)(2,1)} %get-tuple-element.16.sort_ref) | copy-start | bytes 98308
  3.4 15.0 %copy-start.6 = (bf16[128,128]{1,0:T(8,128)(2,1)S(1)}, bf16[128,128]{1,0:T(8,128)(2,1)}, u32[]{:S(2)}) copy-start(bf16[128,128]{1,0:T(8,128)(2,1)} %get-tuple-element.17.upto_ref) | copy-start | bytes 98308
  3.4 15.0 %copy-start.7 = (bf16[128,128]{1,0:T(8,128)(2,1)S(1)}, bf16[128,128]{1,0:T(8,128)(2,1)}, u32[]{:S(2)}) copy-start(bf16[128,128]{1,0:T(8,128)(2,1)} %get-tuple-element.18.back_ref) | copy-start | bytes 98308
  3.4 15.0 %all-to-all-start = ((bf16[8,16,640]{2,1,0:T(8,128)(2,1)}), bf16[8,16,640]{2,1,0:T(8,128)(2,1)S(1)}, u32[]{:S(2)}, u32[]{:S(2)}) async-start(bf16[8,16,640]{2,1,0:T(8,128)(2,1)} %get-tuple-element.15), calls=%async_computation | async-start | bytes 327680 | tf_op jit(solution)/shard_map/all_to_all | solution.py:420
  18.4 12.4 %copy-start.3 = (bf16[512,2048]{1,0:T(8,128)(2,1)S(1)}, bf16[512,2048]{1,0:T(8,128)(2,1)}, u32[]{:S(2)}) copy-start(bf16[512,2048]{1,0:T(8,128)(2,1)} %w_ref.1) | copy-start | bytes 6291460
  30.8 6.3 %copy-start = (bf16[2048,1024]{1,0:T(8,128)(2,1)S(1)}, bf16[2048,1024]{1,0:T(8,128)(2,1)}, u32[]{:S(2)}) copy-start(bf16[2048,1024]{1,0:T(8,128)(2,1)} %wg_ref.1) | copy-start | bytes 12582916
  30.8 6.3 %copy-start.1 = (bf16[2048,1024]{1,0:T(8,128)(2,1)S(1)}, bf16[2048,1024]{1,0:T(8,128)(2,1)}, u32[]{:S(2)}) copy-start(bf16[2048,1024]{1,0:T(8,128)(2,1)} %wu_ref.1) | copy-start | bytes 12582916
  30.8 6.3 %copy-start.2 = (bf16[1024,2048]{1,0:T(8,128)(2,1)S(1)}, bf16[1024,2048]{1,0:T(8,128)(2,1)}, u32[]{:S(2)}) copy-start(bf16[1024,2048]{1,0:T(8,128)(2,1)} %wd_ref.1) | copy-start | bytes 12582916
  30.8 6.3 %copy-start.4 = (bf16[16,2048]{1,0:T(8,128)(2,1)S(1)}, bf16[16,2048]{1,0:T(8,128)(2,1)}, u32[]{:S(2)}) copy-start(bf16[16,2048]{1,0:T(8,128)(2,1)} %tokens_ref.1) | copy-start | bytes 196612
  30.8 6.3 %copy-start.9 = (bf16[2048]{0:T(1024)(128)(2,1)S(1)}, bf16[2048]{0:T(1024)(128)(2,1)}, u32[]{:S(2)}) copy-start(bf16[2048]{0:T(1024)(128)(2,1)} %param.27) | copy-start | bytes 12292
  31.5 1.3 %collective-permute-start = (bf16[16,2048]{1,0:T(8,128)(2,1)S(1)}, bf16[16,2048]{1,0:T(8,128)(2,1)S(1)}, u32[]{:S(2)}, u32[]{:S(2)}) collective-permute-start(bf16[16,2048]{1,0:T(8,128)(2,1)S(1)} %output.1), channel_id=1, source_target_pairs={{0,1},{1,0},{2,3},{3,2},{4,5},{5,4},{6,7},{7,6},{8,9},{9,8},{10,11... | collective-permute-start | bytes 196616 | tf_op jit(solution)/shard_map/ppermute | solution.py:348
  32.7 4.3 %collective-permute-start.1 = (bf16[16,2048]{1,0:T(8,128)(2,1)S(1)}, bf16[16,2048]{1,0:T(8,128)(2,1)S(1)}, u32[]{:S(2)}, u32[]{:S(2)}) collective-permute-start(bf16[16,2048]{1,0:T(8,128)(2,1)S(1)} %add_convert_fusion.1.here_ref), channel_id=1, source_target_pairs={{0,2},{1,3},{2,0},{3,1},{4,6},{5,7},{6,4},{7,5},{8,10},{9,11},{10,... | collective-permute-start | bytes 196616 | tf_op jit(solution)/shard_map/ppermute | solution.py:348
  39.0 1.3 %collective-permute-start.2 = (bf16[16,2048]{1,0:T(8,128)(2,1)S(1)}, bf16[16,2048]{1,0:T(8,128)(2,1)S(1)}, u32[]{:S(2)}, u32[]{:S(2)}) collective-permute-start(bf16[16,2048]{1,0:T(8,128)(2,1)S(1)} %get-tuple-element.27), channel_id=1, source_target_pairs={{0,1},{1,0},{2,3},{3,2},{4,5},{5,4},{6,7},{7,6},{8,9},{9,8},{10,11... | collective-permute-start | bytes 196616 | tf_op jit(solution)/shard_map/ppermute | solution.py:348
  40.2 4.3 %collective-permute-start.3 = (bf16[16,2048]{1,0:T(8,128)(2,1)S(1)}, bf16[16,2048]{1,0:T(8,128)(2,1)S(1)}, u32[]{:S(2)}, u32[]{:S(2)}) collective-permute-start(bf16[16,2048]{1,0:T(8,128)(2,1)S(1)} %add_convert_fusion), channel_id=1, source_target_pairs={{0,2},{1,3},{2,0},{3,1},{4,6},{5,7},{6,4},{7,5},{8,10},{9,11},{10,... | collective-permute-start | bytes 196616 | tf_op jit(solution)/shard_map/ppermute | solution.py:348

commit v6 on v5

--- a/solution.py
+++ b/solution.py
@@ -351,9 +351,9 @@
 def pair_sum(x):
     size = lax.axis_size("tp")
     distance = 1
-    while distance * 2 < size:
+    while 2 * distance < size - 1:
         x = (x.astype(F32) + swap(x, "tp", distance).astype(F32)).astype(BF16)
-        distance *= 2
+        distance = 2 * distance + 1
     return x, swap(x, "tp", distance)
 
 

time: 45.6 us -> 45.2 us (level)
  no operation moved by 1% of the time
where the time goes in v6:
time: 45.2 us; the launch traced here: 44.8 us
  Pallas kernels  11.1 us (25%)
  waiting for transfers between devices  11.1 us (25%)
  starting transfers between devices  10.2 us (23%)
  blocking collectives  10.2 us (23%)
  between operations  0.77 us (2%)
  other arithmetic  0.71 us (2%)
  local copies, waits for them, and re-layouts  0.68 us (2%)
    all_to_all x1, blocking collectives, per_device(): found = lax.all_to_all(parts.reshape(nreq, count, wide), 'req', 0, 0)  10.2 us
    all_to_all x1, starting transfers between devices, per_device(): everyone = lax.all_to_all(msg, 'req', 0, 0).reshape(reqs, wide)  7.42 us
    ppermute x4, waiting for transfers between devices, swap(): lax.ppermute(x, axis, [(i, i ^ distance) for i in range(lax.axis_size(axi...  7.31 us
    pallas_call x1, Pallas kernels, per_device(): pl.pallas_call(prepare_kernel, out_shape=(VMEM((count, 2 * half), F32), V...  3.78 us
    all_to_all x1, waiting for transfers between devices, per_device(): everyone = lax.all_to_all(msg, 'req', 0, 0).reshape(reqs, wide)  3.78 us
    ppermute x4, starting transfers between devices, swap(): lax.ppermute(x, axis, [(i, i ^ distance) for i in range(lax.axis_size(axi...  2.81 us
    pallas_call x1, Pallas kernels, per_device(): pl.pallas_call(project_kernel, out_shape=[jax.ShapeDtypeStruct((nreq, cou...  2.73 us
    pallas_call x1, Pallas kernels, per_device(): pl.pallas_call(attend_kernel, out_shape=jax.ShapeDtypeStruct((reqs, wide)...  2.15 us
  transfers between devices with their start and end apart: 5, of which 5 were waited for; matrix products, arithmetic and copies ran while one was open for 1% of the time, Pallas kernels for 8%

profile of v6, /device:TPU:0, one launch (start us, length us, event | category | flops | bytes accessed | tf_op | source)
XLA Modules:
  0.0 44.8 jit_solution(13588380335355132918)
XLA Ops:
  0.6 0.0 copy-start.8
  0.6 2.7 %project.1 = (bf16[8,16,640]{2,1,0:T(8,128)(2,1)}, bf16[16,640]{1,0:T(8,128)(2,1)S(1)}, bf16[16,2048]{1,0:T(8,128)(2,1)}, f32[32,128]{1,0:T(8,128)}, bf16[128,12...) custom-call(bf16[16,2048]{1,0:T(8,128)(2,1)} %tokens_ref.1, bf16[16,128]{1,0:T(8,128)(2,1)} %bitcast.19, ...), custom_call_target="tpu_custom_call" | custom-call | flops 33554432 | bytes 3145728 | tf_op jit(solution)/shard_map/project/pallas_call | solution.py:390
  3.4 0.0 copy-start.5
  3.4 0.0 copy-start.6
  3.4 0.0 copy-start.7
  3.4 7.4 %all-to-all-start = ((bf16[8,16,640]{2,1,0:T(8,128)(2,1)}), bf16[8,16,640]{2,1,0:T(8,128)(2,1)S(1)}, u32[]{:S(2)}, u32[]{:S(2)}) async-start(bf16[8,16,640]{2,1,0:T(8,128)(2,1)} %get-tuple-element.15), calls=%async_computation | async-start | bytes 327680 | tf_op jit(solution)/shard_map/all_to_all | solution.py:420
  10.8 3.8 %prepare.1 = (f32[16,512]{1,0:T(8,128)S(1)}, bf16[4096,256]{1,0:T(8,128)(2,1)S(1)}, bf16[2048,256]{1,0:T(8,128)(2,1)S(1)}, bf16[2048,256]{1,0:T(8,128)(2,1)}) custom-call(bf16[16,2048]{1,0:T(8,128)(2,1)} %get-tuple-element.19.normed_hbm, f32[32,128]{1,0:T(8,128)} %get-tuple-element.20.turn_hbm, bf16[2048,256]{1,0:T(8,128)(2,1)} %wk_hbm.1, ...), custom_call_target="tpu_custom_call" | custom-call | flops 33554432 | bytes 6291456 | tf_op jit(solution)/shard_map/prepare/pallas_call | solution.py:424
  14.6 3.8 %all-to-all-done = bf16[8,16,640]{2,1,0:T(8,128)(2,1)S(1)} async-done(((bf16[8,16,640]{2,1,0:T(8,128)(2,1)}), bf16[8,16,640]{2,1,0:T(8,128)(2,1)S(1)}, u32[]{:S(2)}, u32[]{:S(2)}) %all-to-all-start) | async-done | bytes 163872 | tf_op jit(solution)/shard_map/all_to_all | solution.py:420
  18.4 0.0 copy-done.8
  18.4 0.0 copy-done.5
  18.4 0.0 copy-done.6
  18.4 0.0 copy-done.7
  18.4 0.0 copy-start.3
  18.4 2.1 %attend.1 = bf16[128,640]{1,0:T(8,128)(2,1)S(1)} custom-call(s32[1]{0:T(128)} %bitcast.base_ref, bf16[128,640]{1,0:T(8,128)(2,1)S(1)} %bitcast.14, bf16[128,128]{1,0:T(8,128)(2,1)S(1)} %copy-done.5, bf16[128,128]{1,0:T(8,128)(2,1)S(1)} %copy-done.6, bf16[128,128]{1,0:T(8,128)(2,1)S(1)} %copy-done.7, s32[32,128]{1,0:T(8,128)S(1)} %bitcast.16, ...), custom_call_target="tpu_custom_call" | custom-call | flops 1073741824 | bytes 8388608 | tf_op jit(solution)/shard_map/attend/pallas_call | solution.py:456
  20.6 10.2 %all_to_all.10.parts_ref = bf16[8,16,640]{2,1,0:T(8,128)(2,1)S(1)} all-to-all(bf16[8,16,640]{2,1,0:T(8,128)(2,1)S(1)} %bitcast.15), channel_id=1, replica_groups=mesh['req'=8,'tp'=4] {'req'}, dimensions={0} | all-to-all | bytes 327680 | tf_op jit(solution)/shard_map/all_to_all | solution.py:481
  30.8 0.0 copy-done.3
  30.8 0.0 copy-start
  30.8 0.0 copy-start.1
  30.8 0.0 copy-start.2
  30.8 0.0 copy-start.4
  30.8 0.0 copy-start.9
  30.8 0.6 %output.1 = bf16[16,2048]{1,0:T(8,128)(2,1)S(1)} custom-call(bf16[8,16,640]{2,1,0:T(8,128)(2,1)S(1)} %all_to_all.10.parts_ref, bf16[16,640]{1,0:T(8,128)(2,1)S(1)} %get-tuple-element.24.msg_ref, f32[16,512]{1,0:T(8,128)S(1)} %get-tuple-element.25.kv_ref, bf16[512,2048]{1,0:T(8,128)(2,1)S(1)} %copy-done.3, bf16[2048,1024]{1,0:T(8,128)(2,1)} %wg_ref.1, ...), custom_call_target="tpu_custom_call" | custom-call | tf_op jit(solution)/shard_map/output/pallas_call | solution.py:483
  31.5 0.0 collective-permute-start
  31.5 1.3 %collective-permute-done = bf16[16,2048]{1,0:T(8,128)(2,1)S(1)} collective-permute-done((bf16[16,2048]{1,0:T(8,128)(2,1)S(1)}, bf16[16,2048]{1,0:T(8,128)(2,1)S(1)}, u32[]{:S(2)}, u32[]{:S(2)}) %collective-permute-start) | collective-permute-done | bytes 65568 | tf_op jit(solution)/shard_map/ppermute | solution.py:348
  32.7 1.3 %collective-permute-start.1 = (bf16[16,2048]{1,0:T(8,128)(2,1)S(1)}, bf16[16,2048]{1,0:T(8,128)(2,1)S(1)}, u32[]{:S(2)}, u32[]{:S(2)}) collective-permute-start(bf16[16,2048]{1,0:T(8,128)(2,1)S(1)} %add_convert_fusion.1.here_ref), channel_id=1, source_target_pairs={{0,3},{1,2},{2,1},{3,0},{4,7},{5,6},{6,5},{7,4},{8,11},{9,10},{10,... | collective-permute-start | bytes 196616 | tf_op jit(solution)/shard_map/ppermute | solution.py:348
  34.1 2.8 %collective-permute-done.1.there_ref = bf16[16,2048]{1,0:T(8,128)(2,1)S(1)} collective-permute-done((bf16[16,2048]{1,0:T(8,128)(2,1)S(1)}, bf16[16,2048]{1,0:T(8,128)(2,1)S(1)}, u32[]{:S(2)}, u32[]{:S(2)}) %collective-permute-start.1) | collective-permute-done | bytes 65568 | tf_op jit(solution)/shard_map/ppermute | solution.py:348
  36.9 0.0 copy-done
  36.9 0.0 copy-done.1
  36.9 0.0 copy-done.2
  36.9 0.0 copy-done.4
  36.9 0.0 copy-done.9
  36.9 1.9 %feed.1 = (bf16[16,2048]{1,0:T(8,128)(2,1)S(1)}, f32[16,2048]{1,0:T(8,128)S(1)}) custom-call(bf16[16,2048]{1,0:T(8,128)(2,1)S(1)} %copy-done.4, bf16[16,2048]{1,0:T(8,128)(2,1)S(1)} %add_convert_fusion.1.here_ref, bf16[16,2048]{1,0:T(8,128)(2,1)S(1)} %collective-permute-done.1.there_ref, bf16[16,128]{1,0:T(8,128)(2,1)S(1)} %bitcast.17, ...), custom_call_target="tpu_custom_call" | custom-call | tf_op jit(solution)/shard_map/feed/pallas_call | solution.py:493
  38.8 0.2 collective-permute-start.2
  38.9 1.1 %collective-permute-done.2 = bf16[16,2048]{1,0:T(8,128)(2,1)S(1)} collective-permute-done((bf16[16,2048]{1,0:T(8,128)(2,1)S(1)}, bf16[16,2048]{1,0:T(8,128)(2,1)S(1)}, u32[]{:S(2)}, u32[]{:S(2)}) %collective-permute-start.2) | collective-permute-done | bytes 65568 | tf_op jit(solution)/shard_map/ppermute | solution.py:348
  40.0 1.3 %collective-permute-start.3 = (bf16[16,2048]{1,0:T(8,128)(2,1)S(1)}, bf16[16,2048]{1,0:T(8,128)(2,1)S(1)}, u32[]{:S(2)}, u32[]{:S(2)}) collective-permute-start(bf16[16,2048]{1,0:T(8,128)(2,1)S(1)} %add_convert_fusion), channel_id=1, source_target_pairs={{0,3},{1,2},{2,1},{3,0},{4,7},{5,6},{6,5},{7,4},{8,11},{9,10},{10,... | collective-permute-start | bytes 196616 | tf_op jit(solution)/shard_map/ppermute | solution.py:348
  41.4 0.6 %reshape.55 = f32[16,2,256]{2,1,0:T(2,128)} reshape(f32[16,512]{1,0:T(8,128)S(1)} %get-tuple-element.25.kv_ref) | data formatting | bytes 65536 | tf_op jit(solution)/shard_map/reshape | solution.py:505
  42.0 2.2 %collective-permute-done.3 = bf16[16,2048]{1,0:T(8,128)(2,1)S(1)} collective-permute-done((bf16[16,2048]{1,0:T(8,128)(2,1)S(1)}, bf16[16,2048]{1,0:T(8,128)(2,1)S(1)}, u32[]{:S(2)}, u32[]{:S(2)}) %collective-permute-start.3) | collective-permute-done | bytes 65568 | tf_op jit(solution)/shard_map/ppermute | solution.py:348
  44.2 0.7 %add_add_fusion = f32[16,2048]{1,0:T(8,128)} fusion(f32[16,2048]{1,0:T(8,128)S(1)} %get-tuple-element.26, bf16[16,2048]{1,0:T(8,128)(2,1)S(1)} %collective-permute-done.3, bf16[16,2048]{1,0:T(8,128)(2,1)S(1)} %add_convert_fusion), kind=kLoop, calls=%fused_computation | loop fusion | flops 131072 | bytes 393216 | tf_op jit(solution)/shard_map/add | solution.py:504
  (2 shorter events, 0.0 us)
Async XLA Ops:
  0.6 17.8 %copy-start.8 = (s32[4096]{0:T(1024)S(1)}, s32[4096]{0:T(1024)}, u32[]{:S(2)}) copy-start(s32[4096]{0:T(1024)} %param.20) | copy-start | bytes 49156
  3.4 15.0 %copy-start.5 = (bf16[128,128]{1,0:T(8,128)(2,1)S(1)}, bf16[128,128]{1,0:T(8,128)(2,1)}, u32[]{:S(2)}) copy-start(bf16[128,128]{1,0:T(8,128)(2,1)} %get-tuple-element.16.sort_ref) | copy-start | bytes 98308
  3.4 15.0 %copy-start.6 = (bf16[128,128]{1,0:T(8,128)(2,1)S(1)}, bf16[128,128]{1,0:T(8,128)(2,1)}, u32[]{:S(2)}) copy-start(bf16[128,128]{1,0:T(8,128)(2,1)} %get-tuple-element.17.upto_ref) | copy-start | bytes 98308
  3.4 15.0 %copy-start.7 = (bf16[128,128]{1,0:T(8,128)(2,1)S(1)}, bf16[128,128]{1,0:T(8,128)(2,1)}, u32[]{:S(2)}) copy-start(bf16[128,128]{1,0:T(8,128)(2,1)} %get-tuple-element.18.back_ref) | copy-start | bytes 98308
  3.4 15.0 %all-to-all-start = ((bf16[8,16,640]{2,1,0:T(8,128)(2,1)}), bf16[8,16,640]{2,1,0:T(8,128)(2,1)S(1)}, u32[]{:S(2)}, u32[]{:S(2)}) async-start(bf16[8,16,640]{2,1,0:T(8,128)(2,1)} %get-tuple-element.15), calls=%async_computation | async-start | bytes 327680 | tf_op jit(solution)/shard_map/all_to_all | solution.py:420
  18.4 12.4 %copy-start.3 = (bf16[512,2048]{1,0:T(8,128)(2,1)S(1)}, bf16[512,2048]{1,0:T(8,128)(2,1)}, u32[]{:S(2)}) copy-start(bf16[512,2048]{1,0:T(8,128)(2,1)} %w_ref.1) | copy-start | bytes 6291460
  30.8 6.1 %copy-start = (bf16[2048,1024]{1,0:T(8,128)(2,1)S(1)}, bf16[2048,1024]{1,0:T(8,128)(2,1)}, u32[]{:S(2)}) copy-start(bf16[2048,1024]{1,0:T(8,128)(2,1)} %wg_ref.1) | copy-start | bytes 12582916
  30.8 6.1 %copy-start.1 = (bf16[2048,1024]{1,0:T(8,128)(2,1)S(1)}, bf16[2048,1024]{1,0:T(8,128)(2,1)}, u32[]{:S(2)}) copy-start(bf16[2048,1024]{1,0:T(8,128)(2,1)} %wu_ref.1) | copy-start | bytes 12582916
  30.8 6.1 %copy-start.2 = (bf16[1024,2048]{1,0:T(8,128)(2,1)S(1)}, bf16[1024,2048]{1,0:T(8,128)(2,1)}, u32[]{:S(2)}) copy-start(bf16[1024,2048]{1,0:T(8,128)(2,1)} %wd_ref.1) | copy-start | bytes 12582916
  30.8 6.1 %copy-start.4 = (bf16[16,2048]{1,0:T(8,128)(2,1)S(1)}, bf16[16,2048]{1,0:T(8,128)(2,1)}, u32[]{:S(2)}) copy-start(bf16[16,2048]{1,0:T(8,128)(2,1)} %tokens_ref.1) | copy-start | bytes 196612
  30.8 6.1 %copy-start.9 = (bf16[2048]{0:T(1024)(128)(2,1)S(1)}, bf16[2048]{0:T(1024)(128)(2,1)}, u32[]{:S(2)}) copy-start(bf16[2048]{0:T(1024)(128)(2,1)} %param.27) | copy-start | bytes 12292
  31.5 1.3 %collective-permute-start = (bf16[16,2048]{1,0:T(8,128)(2,1)S(1)}, bf16[16,2048]{1,0:T(8,128)(2,1)S(1)}, u32[]{:S(2)}, u32[]{:S(2)}) collective-permute-start(bf16[16,2048]{1,0:T(8,128)(2,1)S(1)} %output.1), channel_id=1, source_target_pairs={{0,1},{1,0},{2,3},{3,2},{4,5},{5,4},{6,7},{7,6},{8,9},{9,8},{10,11... | collective-permute-start | bytes 196616 | tf_op jit(solution)/shard_map/ppermute | solution.py:348
  32.7 4.1 %collective-permute-start.1 = (bf16[16,2048]{1,0:T(8,128)(2,1)S(1)}, bf16[16,2048]{1,0:T(8,128)(2,1)S(1)}, u32[]{:S(2)}, u32[]{:S(2)}) collective-permute-start(bf16[16,2048]{1,0:T(8,128)(2,1)S(1)} %add_convert_fusion.1.here_ref), channel_id=1, source_target_pairs={{0,3},{1,2},{2,1},{3,0},{4,7},{5,6},{6,5},{7,4},{8,11},{9,10},{10,... | collective-permute-start | bytes 196616 | tf_op jit(solution)/shard_map/ppermute | solution.py:348
  38.8 1.3 %collective-permute-start.2 = (bf16[16,2048]{1,0:T(8,128)(2,1)S(1)}, bf16[16,2048]{1,0:T(8,128)(2,1)S(1)}, u32[]{:S(2)}, u32[]{:S(2)}) collective-permute-start(bf16[16,2048]{1,0:T(8,128)(2,1)S(1)} %get-tuple-element.27), channel_id=1, source_target_pairs={{0,1},{1,0},{2,3},{3,2},{4,5},{5,4},{6,7},{7,6},{8,9},{9,8},{10,11... | collective-permute-start | bytes 196616 | tf_op jit(solution)/shard_map/ppermute | solution.py:348
  40.0 4.1 %collective-permute-start.3 = (bf16[16,2048]{1,0:T(8,128)(2,1)S(1)}, bf16[16,2048]{1,0:T(8,128)(2,1)S(1)}, u32[]{:S(2)}, u32[]{:S(2)}) collective-permute-start(bf16[16,2048]{1,0:T(8,128)(2,1)S(1)} %add_convert_fusion), channel_id=1, source_target_pairs={{0,3},{1,2},{2,1},{3,0},{4,7},{5,6},{6,5},{7,4},{8,11},{9,10},{10,... | collective-permute-start | bytes 196616 | tf_op jit(solution)/shard_map/ppermute | solution.py:348

commit v7 on v6

--- a/solution.py
+++ b/solution.py
@@ -17,7 +17,7 @@
 TILE = 256
 SUB = 128
 WIN = 8
-PIECES = 4
+PIECES = 8
 SLAB = 1024
 F32 = jnp.float32
 BF16 = jnp.bfloat16

time: 45.2 us -> 45.2 us (level)
  no operation moved by 1% of the time
where the time goes in v7:
time: 45.2 us; the launch traced here: 44.8 us
  Pallas kernels  11.1 us (25%)
  waiting for transfers between devices  11.1 us (25%)
  starting transfers between devices  10.2 us (23%)
  blocking collectives  10.2 us (23%)
  between operations  0.77 us (2%)
  other arithmetic  0.71 us (2%)
  local copies, waits for them, and re-layouts  0.68 us (2%)
    all_to_all x1, blocking collectives, per_device(): found = lax.all_to_all(parts.reshape(nreq, count, wide), 'req', 0, 0)  10.2 us
    all_to_all x1, starting transfers between devices, per_device(): everyone = lax.all_to_all(msg, 'req', 0, 0).reshape(reqs, wide)  7.42 us
    ppermute x4, waiting for transfers between devices, swap(): lax.ppermute(x, axis, [(i, i ^ distance) for i in range(lax.axis_size(axi...  7.32 us
    pallas_call x1, Pallas kernels, per_device(): pl.pallas_call(prepare_kernel, out_shape=(VMEM((count, 2 * half), F32), V...  3.78 us
    all_to_all x1, waiting for transfers between devices, per_device(): everyone = lax.all_to_all(msg, 'req', 0, 0).reshape(reqs, wide)  3.78 us
    ppermute x4, starting transfers between devices, swap(): lax.ppermute(x, axis, [(i, i ^ distance) for i in range(lax.axis_size(axi...  2.81 us
    pallas_call x1, Pallas kernels, per_device(): pl.pallas_call(project_kernel, out_shape=[jax.ShapeDtypeStruct((nreq, cou...  2.72 us
    pallas_call x1, Pallas kernels, per_device(): pl.pallas_call(attend_kernel, out_shape=jax.ShapeDtypeStruct((reqs, wide)...  2.15 us
  transfers between devices with their start and end apart: 5, of which 5 were waited for; matrix products, arithmetic and copies ran while one was open for 1% of the time, Pallas kernels for 8%

profile of v7, /device:TPU:0, one launch (start us, length us, event | category | flops | bytes accessed | tf_op | source)
XLA Modules:
  0.0 44.8 jit_solution(11947532993269039011)
XLA Ops:
  0.6 0.0 copy-start.8
  0.6 2.7 %project.1 = (bf16[8,16,640]{2,1,0:T(8,128)(2,1)}, bf16[16,640]{1,0:T(8,128)(2,1)S(1)}, bf16[16,2048]{1,0:T(8,128)(2,1)}, f32[32,128]{1,0:T(8,128)}, bf16[128,12...) custom-call(bf16[16,2048]{1,0:T(8,128)(2,1)} %tokens_ref.1, bf16[16,128]{1,0:T(8,128)(2,1)} %bitcast.19, ...), custom_call_target="tpu_custom_call" | custom-call | flops 33554432 | bytes 3145728 | tf_op jit(solution)/shard_map/project/pallas_call | solution.py:390
  3.4 0.0 copy-start.5
  3.4 0.0 copy-start.6
  3.4 0.0 copy-start.7
  3.4 7.4 %all-to-all-start = ((bf16[8,16,640]{2,1,0:T(8,128)(2,1)}), bf16[8,16,640]{2,1,0:T(8,128)(2,1)S(1)}, u32[]{:S(2)}, u32[]{:S(2)}) async-start(bf16[8,16,640]{2,1,0:T(8,128)(2,1)} %get-tuple-element.15), calls=%async_computation | async-start | bytes 327680 | tf_op jit(solution)/shard_map/all_to_all | solution.py:420
  10.8 3.8 %prepare.1 = (f32[16,512]{1,0:T(8,128)S(1)}, bf16[4096,256]{1,0:T(8,128)(2,1)S(1)}, bf16[2048,256]{1,0:T(8,128)(2,1)S(1)}, bf16[2048,256]{1,0:T(8,128)(2,1)}) custom-call(bf16[16,2048]{1,0:T(8,128)(2,1)} %get-tuple-element.19.normed_hbm, f32[32,128]{1,0:T(8,128)} %get-tuple-element.20.turn_hbm, bf16[2048,256]{1,0:T(8,128)(2,1)} %wk_hbm.1, ...), custom_call_target="tpu_custom_call" | custom-call | flops 33554432 | bytes 6291456 | tf_op jit(solution)/shard_map/prepare/pallas_call | solution.py:424
  14.6 3.8 %all-to-all-done = bf16[8,16,640]{2,1,0:T(8,128)(2,1)S(1)} async-done(((bf16[8,16,640]{2,1,0:T(8,128)(2,1)}), bf16[8,16,640]{2,1,0:T(8,128)(2,1)S(1)}, u32[]{:S(2)}, u32[]{:S(2)}) %all-to-all-start) | async-done | bytes 163872 | tf_op jit(solution)/shard_map/all_to_all | solution.py:420
  18.4 0.0 copy-done.8
  18.4 0.0 copy-done.5
  18.4 0.0 copy-done.6
  18.4 0.0 copy-done.7
  18.4 0.0 copy-start.3
  18.4 2.1 %attend.1 = bf16[128,640]{1,0:T(8,128)(2,1)S(1)} custom-call(s32[1]{0:T(128)} %bitcast.base_ref, bf16[128,640]{1,0:T(8,128)(2,1)S(1)} %bitcast.14, bf16[128,128]{1,0:T(8,128)(2,1)S(1)} %copy-done.5, bf16[128,128]{1,0:T(8,128)(2,1)S(1)} %copy-done.6, bf16[128,128]{1,0:T(8,128)(2,1)S(1)} %copy-done.7, s32[32,128]{1,0:T(8,128)S(1)} %bitcast.16, ...), custom_call_target="tpu_custom_call" | custom-call | flops 1073741824 | bytes 8388608 | tf_op jit(solution)/shard_map/attend/pallas_call | solution.py:456
  20.6 10.2 %all_to_all.10.parts_ref = bf16[8,16,640]{2,1,0:T(8,128)(2,1)S(1)} all-to-all(bf16[8,16,640]{2,1,0:T(8,128)(2,1)S(1)} %bitcast.15), channel_id=1, replica_groups=mesh['req'=8,'tp'=4] {'req'}, dimensions={0} | all-to-all | bytes 327680 | tf_op jit(solution)/shard_map/all_to_all | solution.py:481
  30.8 0.0 copy-done.3
  30.8 0.0 copy-start
  30.8 0.0 copy-start.1
  30.8 0.0 copy-start.2
  30.8 0.0 copy-start.4
  30.8 0.0 copy-start.9
  30.8 0.6 %output.1 = bf16[16,2048]{1,0:T(8,128)(2,1)S(1)} custom-call(bf16[8,16,640]{2,1,0:T(8,128)(2,1)S(1)} %all_to_all.10.parts_ref, bf16[16,640]{1,0:T(8,128)(2,1)S(1)} %get-tuple-element.24.msg_ref, f32[16,512]{1,0:T(8,128)S(1)} %get-tuple-element.25.kv_ref, bf16[512,2048]{1,0:T(8,128)(2,1)S(1)} %copy-done.3, bf16[2048,1024]{1,0:T(8,128)(2,1)} %wg_ref.1, ...), custom_call_target="tpu_custom_call" | custom-call | tf_op jit(solution)/shard_map/output/pallas_call | solution.py:483
  31.5 0.0 collective-permute-start
  31.5 1.3 %collective-permute-done = bf16[16,2048]{1,0:T(8,128)(2,1)S(1)} collective-permute-done((bf16[16,2048]{1,0:T(8,128)(2,1)S(1)}, bf16[16,2048]{1,0:T(8,128)(2,1)S(1)}, u32[]{:S(2)}, u32[]{:S(2)}) %collective-permute-start) | collective-permute-done | bytes 65568 | tf_op jit(solution)/shard_map/ppermute | solution.py:348
  32.7 1.3 %collective-permute-start.1 = (bf16[16,2048]{1,0:T(8,128)(2,1)S(1)}, bf16[16,2048]{1,0:T(8,128)(2,1)S(1)}, u32[]{:S(2)}, u32[]{:S(2)}) collective-permute-start(bf16[16,2048]{1,0:T(8,128)(2,1)S(1)} %add_convert_fusion.1.here_ref), channel_id=1, source_target_pairs={{0,3},{1,2},{2,1},{3,0},{4,7},{5,6},{6,5},{7,4},{8,11},{9,10},{10,... | collective-permute-start | bytes 196616 | tf_op jit(solution)/shard_map/ppermute | solution.py:348
  34.1 2.8 %collective-permute-done.1.there_ref = bf16[16,2048]{1,0:T(8,128)(2,1)S(1)} collective-permute-done((bf16[16,2048]{1,0:T(8,128)(2,1)S(1)}, bf16[16,2048]{1,0:T(8,128)(2,1)S(1)}, u32[]{:S(2)}, u32[]{:S(2)}) %collective-permute-start.1) | collective-permute-done | bytes 65568 | tf_op jit(solution)/shard_map/ppermute | solution.py:348
  36.9 0.0 copy-done
  36.9 0.0 copy-done.1
  36.9 0.0 copy-done.2
  36.9 0.0 copy-done.4
  36.9 0.0 copy-done.9
  36.9 1.9 %feed.1 = (bf16[16,2048]{1,0:T(8,128)(2,1)S(1)}, f32[16,2048]{1,0:T(8,128)S(1)}) custom-call(bf16[16,2048]{1,0:T(8,128)(2,1)S(1)} %copy-done.4, bf16[16,2048]{1,0:T(8,128)(2,1)S(1)} %add_convert_fusion.1.here_ref, bf16[16,2048]{1,0:T(8,128)(2,1)S(1)} %collective-permute-done.1.there_ref, bf16[16,128]{1,0:T(8,128)(2,1)S(1)} %bitcast.17, ...), custom_call_target="tpu_custom_call" | custom-call | tf_op jit(solution)/shard_map/feed/pallas_call | solution.py:493
  38.7 0.2 collective-permute-start.2
  38.9 1.1 %collective-permute-done.2 = bf16[16,2048]{1,0:T(8,128)(2,1)S(1)} collective-permute-done((bf16[16,2048]{1,0:T(8,128)(2,1)S(1)}, bf16[16,2048]{1,0:T(8,128)(2,1)S(1)}, u32[]{:S(2)}, u32[]{:S(2)}) %collective-permute-start.2) | collective-permute-done | bytes 65568 | tf_op jit(solution)/shard_map/ppermute | solution.py:348
  40.0 1.3 %collective-permute-start.3 = (bf16[16,2048]{1,0:T(8,128)(2,1)S(1)}, bf16[16,2048]{1,0:T(8,128)(2,1)S(1)}, u32[]{:S(2)}, u32[]{:S(2)}) collective-permute-start(bf16[16,2048]{1,0:T(8,128)(2,1)S(1)} %add_convert_fusion), channel_id=1, source_target_pairs={{0,3},{1,2},{2,1},{3,0},{4,7},{5,6},{6,5},{7,4},{8,11},{9,10},{10,... | collective-permute-start | bytes 196616 | tf_op jit(solution)/shard_map/ppermute | solution.py:348
  41.3 0.6 %reshape.55 = f32[16,2,256]{2,1,0:T(2,128)} reshape(f32[16,512]{1,0:T(8,128)S(1)} %get-tuple-element.25.kv_ref) | data formatting | bytes 65536 | tf_op jit(solution)/shard_map/reshape | solution.py:505
  42.0 2.2 %collective-permute-done.3 = bf16[16,2048]{1,0:T(8,128)(2,1)S(1)} collective-permute-done((bf16[16,2048]{1,0:T(8,128)(2,1)S(1)}, bf16[16,2048]{1,0:T(8,128)(2,1)S(1)}, u32[]{:S(2)}, u32[]{:S(2)}) %collective-permute-start.3) | collective-permute-done | bytes 65568 | tf_op jit(solution)/shard_map/ppermute | solution.py:348
  44.1 0.7 %add_add_fusion = f32[16,2048]{1,0:T(8,128)} fusion(f32[16,2048]{1,0:T(8,128)S(1)} %get-tuple-element.26, bf16[16,2048]{1,0:T(8,128)(2,1)S(1)} %collective-permute-done.3, bf16[16,2048]{1,0:T(8,128)(2,1)S(1)} %add_convert_fusion), kind=kLoop, calls=%fused_computation | loop fusion | flops 131072 | bytes 393216 | tf_op jit(solution)/shard_map/add | solution.py:504
  (2 shorter events, 0.0 us)
Async XLA Ops:
  0.6 17.8 %copy-start.8 = (s32[4096]{0:T(1024)S(1)}, s32[4096]{0:T(1024)}, u32[]{:S(2)}) copy-start(s32[4096]{0:T(1024)} %param.20) | copy-start | bytes 49156
  3.4 15.0 %copy-start.5 = (bf16[128,128]{1,0:T(8,128)(2,1)S(1)}, bf16[128,128]{1,0:T(8,128)(2,1)}, u32[]{:S(2)}) copy-start(bf16[128,128]{1,0:T(8,128)(2,1)} %get-tuple-element.16.sort_ref) | copy-start | bytes 98308
  3.4 15.0 %copy-start.6 = (bf16[128,128]{1,0:T(8,128)(2,1)S(1)}, bf16[128,128]{1,0:T(8,128)(2,1)}, u32[]{:S(2)}) copy-start(bf16[128,128]{1,0:T(8,128)(2,1)} %get-tuple-element.17.upto_ref) | copy-start | bytes 98308
  3.4 15.0 %copy-start.7 = (bf16[128,128]{1,0:T(8,128)(2,1)S(1)}, bf16[128,128]{1,0:T(8,128)(2,1)}, u32[]{:S(2)}) copy-start(bf16[128,128]{1,0:T(8,128)(2,1)} %get-tuple-element.18.back_ref) | copy-start | bytes 98308
  3.4 15.0 %all-to-all-start = ((bf16[8,16,640]{2,1,0:T(8,128)(2,1)}), bf16[8,16,640]{2,1,0:T(8,128)(2,1)S(1)}, u32[]{:S(2)}, u32[]{:S(2)}) async-start(bf16[8,16,640]{2,1,0:T(8,128)(2,1)} %get-tuple-element.15), calls=%async_computation | async-start | bytes 327680 | tf_op jit(solution)/shard_map/all_to_all | solution.py:420
  18.4 12.4 %copy-start.3 = (bf16[512,2048]{1,0:T(8,128)(2,1)S(1)}, bf16[512,2048]{1,0:T(8,128)(2,1)}, u32[]{:S(2)}) copy-start(bf16[512,2048]{1,0:T(8,128)(2,1)} %w_ref.1) | copy-start | bytes 6291460
  30.8 6.1 %copy-start = (bf16[2048,1024]{1,0:T(8,128)(2,1)S(1)}, bf16[2048,1024]{1,0:T(8,128)(2,1)}, u32[]{:S(2)}) copy-start(bf16[2048,1024]{1,0:T(8,128)(2,1)} %wg_ref.1) | copy-start | bytes 12582916
  30.8 6.1 %copy-start.1 = (bf16[2048,1024]{1,0:T(8,128)(2,1)S(1)}, bf16[2048,1024]{1,0:T(8,128)(2,1)}, u32[]{:S(2)}) copy-start(bf16[2048,1024]{1,0:T(8,128)(2,1)} %wu_ref.1) | copy-start | bytes 12582916
  30.8 6.1 %copy-start.2 = (bf16[1024,2048]{1,0:T(8,128)(2,1)S(1)}, bf16[1024,2048]{1,0:T(8,128)(2,1)}, u32[]{:S(2)}) copy-start(bf16[1024,2048]{1,0:T(8,128)(2,1)} %wd_ref.1) | copy-start | bytes 12582916
  30.8 6.1 %copy-start.4 = (bf16[16,2048]{1,0:T(8,128)(2,1)S(1)}, bf16[16,2048]{1,0:T(8,128)(2,1)}, u32[]{:S(2)}) copy-start(bf16[16,2048]{1,0:T(8,128)(2,1)} %tokens_ref.1) | copy-start | bytes 196612
  30.8 6.1 %copy-start.9 = (bf16[2048]{0:T(1024)(128)(2,1)S(1)}, bf16[2048]{0:T(1024)(128)(2,1)}, u32[]{:S(2)}) copy-start(bf16[2048]{0:T(1024)(128)(2,1)} %param.27) | copy-start | bytes 12292
  31.5 1.3 %collective-permute-start = (bf16[16,2048]{1,0:T(8,128)(2,1)S(1)}, bf16[16,2048]{1,0:T(8,128)(2,1)S(1)}, u32[]{:S(2)}, u32[]{:S(2)}) collective-permute-start(bf16[16,2048]{1,0:T(8,128)(2,1)S(1)} %output.1), channel_id=1, source_target_pairs={{0,1},{1,0},{2,3},{3,2},{4,5},{5,4},{6,7},{7,6},{8,9},{9,8},{10,11... | collective-permute-start | bytes 196616 | tf_op jit(solution)/shard_map/ppermute | solution.py:348
  32.7 4.1 %collective-permute-start.1 = (bf16[16,2048]{1,0:T(8,128)(2,1)S(1)}, bf16[16,2048]{1,0:T(8,128)(2,1)S(1)}, u32[]{:S(2)}, u32[]{:S(2)}) collective-permute-start(bf16[16,2048]{1,0:T(8,128)(2,1)S(1)} %add_convert_fusion.1.here_ref), channel_id=1, source_target_pairs={{0,3},{1,2},{2,1},{3,0},{4,7},{5,6},{6,5},{7,4},{8,11},{9,10},{10,... | collective-permute-start | bytes 196616 | tf_op jit(solution)/shard_map/ppermute | solution.py:348
  38.7 1.3 %collective-permute-start.2 = (bf16[16,2048]{1,0:T(8,128)(2,1)S(1)}, bf16[16,2048]{1,0:T(8,128)(2,1)S(1)}, u32[]{:S(2)}, u32[]{:S(2)}) collective-permute-start(bf16[16,2048]{1,0:T(8,128)(2,1)S(1)} %get-tuple-element.27), channel_id=1, source_target_pairs={{0,1},{1,0},{2,3},{3,2},{4,5},{5,4},{6,7},{7,6},{8,9},{9,8},{10,11... | collective-permute-start | bytes 196616 | tf_op jit(solution)/shard_map/ppermute | solution.py:348
  40.0 4.1 %collective-permute-start.3 = (bf16[16,2048]{1,0:T(8,128)(2,1)S(1)}, bf16[16,2048]{1,0:T(8,128)(2,1)S(1)}, u32[]{:S(2)}, u32[]{:S(2)}) collective-permute-start(bf16[16,2048]{1,0:T(8,128)(2,1)S(1)} %add_convert_fusion), channel_id=1, source_target_pairs={{0,3},{1,2},{2,1},{3,0},{4,7},{5,6},{6,5},{7,4},{8,11},{9,10},{10,... | collective-permute-start | bytes 196616 | tf_op jit(solution)/shard_map/ppermute | solution.py:348

commit v8 on v7

--- a/solution.py
+++ b/solution.py
@@ -338,10 +338,12 @@
     mid = tokens_ref[...].astype(F32) + (here_ref[...].astype(F32) + there_ref[...].astype(F32))
     mid_ref[...] = mid
     normed = norm_rows(mid, gain_ref)
-    gate = mm(normed, wg_ref[...])
-    upper = mm(normed, wu_ref[...])
-    act = (gate / (1.0 + jnp.exp(-gate)) * upper).astype(BF16)
-    part_ref[...] = mm(act, wd_ref[...]).astype(BF16)
+    act = []
+    for low in range(0, wg_ref.shape[1], TILE):
+        gate = mm(normed, wg_ref[:, low : low + TILE])
+        upper = mm(normed, wu_ref[:, low : low + TILE])
+        act.append((gate / (1.0 + jnp.exp(-gate)) * upper).astype(BF16))
+    part_ref[...] = mm(jnp.concatenate(act, axis=1), wd_ref[...]).astype(BF16)
 
 
 def swap(x, axis, distance):

time: 45.2 us -> 45.1 us (level)
  no operation moved by 1% of the time
where the time goes in v8:
time: 45.1 us; the launch traced here: 44.8 us
  Pallas kernels  11.1 us (25%)
  waiting for transfers between devices  11.1 us (25%)
  starting transfers between devices  10.2 us (23%)
  blocking collectives  10.2 us (23%)
  between operations  0.77 us (2%)
  other arithmetic  0.71 us (2%)
  local copies, waits for them, and re-layouts  0.68 us (2%)
    all_to_all x1, blocking collectives, per_device(): found = lax.all_to_all(parts.reshape(nreq, count, wide), 'req', 0, 0)  10.2 us
    all_to_all x1, starting transfers between devices, per_device(): everyone = lax.all_to_all(msg, 'req', 0, 0).reshape(reqs, wide)  7.42 us
    ppermute x4, waiting for transfers between devices, swap(): lax.ppermute(x, axis, [(i, i ^ distance) for i in range(lax.axis_size(axi...  7.32 us
    pallas_call x1, Pallas kernels, per_device(): pl.pallas_call(prepare_kernel, out_shape=(VMEM((count, 2 * half), F32), V...  3.78 us
    all_to_all x1, waiting for transfers between devices, per_device(): everyone = lax.all_to_all(msg, 'req', 0, 0).reshape(reqs, wide)  3.78 us
    ppermute x4, starting transfers between devices, swap(): lax.ppermute(x, axis, [(i, i ^ distance) for i in range(lax.axis_size(axi...  2.81 us
    pallas_call x1, Pallas kernels, per_device(): pl.pallas_call(project_kernel, out_shape=[jax.ShapeDtypeStruct((nreq, cou...  2.72 us
    pallas_call x1, Pallas kernels, per_device(): pl.pallas_call(attend_kernel, out_shape=jax.ShapeDtypeStruct((reqs, wide)...  2.15 us
  transfers between devices with their start and end apart: 5, of which 5 were waited for; matrix products, arithmetic and copies ran while one was open for 1% of the time, Pallas kernels for 8%

profile of v8, /device:TPU:0, one launch (start us, length us, event | category | flops | bytes accessed | tf_op | source)
XLA Modules:
  0.0 44.8 jit_solution(10948866404630509966)
XLA Ops:
  0.6 0.0 copy-start.8
  0.6 2.7 %project.1 = (bf16[8,16,640]{2,1,0:T(8,128)(2,1)}, bf16[16,640]{1,0:T(8,128)(2,1)S(1)}, bf16[16,2048]{1,0:T(8,128)(2,1)}, f32[32,128]{1,0:T(8,128)}, bf16[128,12...) custom-call(bf16[16,2048]{1,0:T(8,128)(2,1)} %tokens_ref.1, bf16[16,128]{1,0:T(8,128)(2,1)} %bitcast.19, ...), custom_call_target="tpu_custom_call" | custom-call | flops 33554432 | bytes 3145728 | tf_op jit(solution)/shard_map/project/pallas_call | solution.py:392
  3.4 0.0 copy-start.5
  3.4 0.0 copy-start.6
  3.4 0.0 copy-start.7
  3.4 7.4 %all-to-all-start = ((bf16[8,16,640]{2,1,0:T(8,128)(2,1)}), bf16[8,16,640]{2,1,0:T(8,128)(2,1)S(1)}, u32[]{:S(2)}, u32[]{:S(2)}) async-start(bf16[8,16,640]{2,1,0:T(8,128)(2,1)} %get-tuple-element.15), calls=%async_computation | async-start | bytes 327680 | tf_op jit(solution)/shard_map/all_to_all | solution.py:422
  10.8 3.8 %prepare.1 = (f32[16,512]{1,0:T(8,128)S(1)}, bf16[4096,256]{1,0:T(8,128)(2,1)S(1)}, bf16[2048,256]{1,0:T(8,128)(2,1)S(1)}, bf16[2048,256]{1,0:T(8,128)(2,1)}) custom-call(bf16[16,2048]{1,0:T(8,128)(2,1)} %get-tuple-element.19.normed_hbm, f32[32,128]{1,0:T(8,128)} %get-tuple-element.20.turn_hbm, bf16[2048,256]{1,0:T(8,128)(2,1)} %wk_hbm.1, ...), custom_call_target="tpu_custom_call" | custom-call | flops 33554432 | bytes 6291456 | tf_op jit(solution)/shard_map/prepare/pallas_call | solution.py:426
  14.6 3.8 %all-to-all-done = bf16[8,16,640]{2,1,0:T(8,128)(2,1)S(1)} async-done(((bf16[8,16,640]{2,1,0:T(8,128)(2,1)}), bf16[8,16,640]{2,1,0:T(8,128)(2,1)S(1)}, u32[]{:S(2)}, u32[]{:S(2)}) %all-to-all-start) | async-done | bytes 163872 | tf_op jit(solution)/shard_map/all_to_all | solution.py:422
  18.4 0.0 copy-done.8
  18.4 0.0 copy-done.5
  18.4 0.0 copy-done.6
  18.4 0.0 copy-done.7
  18.4 0.0 copy-start.3
  18.4 2.2 %attend.1 = bf16[128,640]{1,0:T(8,128)(2,1)S(1)} custom-call(s32[1]{0:T(128)} %bitcast.base_ref, bf16[128,640]{1,0:T(8,128)(2,1)S(1)} %bitcast.14, bf16[128,128]{1,0:T(8,128)(2,1)S(1)} %copy-done.5, bf16[128,128]{1,0:T(8,128)(2,1)S(1)} %copy-done.6, bf16[128,128]{1,0:T(8,128)(2,1)S(1)} %copy-done.7, s32[32,128]{1,0:T(8,128)S(1)} %bitcast.16, ...), custom_call_target="tpu_custom_call" | custom-call | flops 1073741824 | bytes 8388608 | tf_op jit(solution)/shard_map/attend/pallas_call | solution.py:458
  20.6 10.2 %all_to_all.10.parts_ref = bf16[8,16,640]{2,1,0:T(8,128)(2,1)S(1)} all-to-all(bf16[8,16,640]{2,1,0:T(8,128)(2,1)S(1)} %bitcast.15), channel_id=1, replica_groups=mesh['req'=8,'tp'=4] {'req'}, dimensions={0} | all-to-all | bytes 327680 | tf_op jit(solution)/shard_map/all_to_all | solution.py:483
  30.8 0.0 copy-done.3
  30.8 0.0 copy-start
  30.8 0.0 copy-start.1
  30.8 0.0 copy-start.2
  30.8 0.0 copy-start.4
  30.8 0.0 copy-start.9
  30.8 0.6 %output.1 = bf16[16,2048]{1,0:T(8,128)(2,1)S(1)} custom-call(bf16[8,16,640]{2,1,0:T(8,128)(2,1)S(1)} %all_to_all.10.parts_ref, bf16[16,640]{1,0:T(8,128)(2,1)S(1)} %get-tuple-element.24.msg_ref, f32[16,512]{1,0:T(8,128)S(1)} %get-tuple-element.25.kv_ref, bf16[512,2048]{1,0:T(8,128)(2,1)S(1)} %copy-done.3, bf16[2048,1024]{1,0:T(8,128)(2,1)} %wg_ref.1, ...), custom_call_target="tpu_custom_call" | custom-call | tf_op jit(solution)/shard_map/output/pallas_call | solution.py:485
  31.5 0.0 collective-permute-start
  31.5 1.3 %collective-permute-done = bf16[16,2048]{1,0:T(8,128)(2,1)S(1)} collective-permute-done((bf16[16,2048]{1,0:T(8,128)(2,1)S(1)}, bf16[16,2048]{1,0:T(8,128)(2,1)S(1)}, u32[]{:S(2)}, u32[]{:S(2)}) %collective-permute-start) | collective-permute-done | bytes 65568 | tf_op jit(solution)/shard_map/ppermute | solution.py:350
  32.7 1.3 %collective-permute-start.1 = (bf16[16,2048]{1,0:T(8,128)(2,1)S(1)}, bf16[16,2048]{1,0:T(8,128)(2,1)S(1)}, u32[]{:S(2)}, u32[]{:S(2)}) collective-permute-start(bf16[16,2048]{1,0:T(8,128)(2,1)S(1)} %add_convert_fusion.1.here_ref), channel_id=1, source_target_pairs={{0,3},{1,2},{2,1},{3,0},{4,7},{5,6},{6,5},{7,4},{8,11},{9,10},{10,... | collective-permute-start | bytes 196616 | tf_op jit(solution)/shard_map/ppermute | solution.py:350
  34.1 2.8 %collective-permute-done.1.there_ref = bf16[16,2048]{1,0:T(8,128)(2,1)S(1)} collective-permute-done((bf16[16,2048]{1,0:T(8,128)(2,1)S(1)}, bf16[16,2048]{1,0:T(8,128)(2,1)S(1)}, u32[]{:S(2)}, u32[]{:S(2)}) %collective-permute-start.1) | collective-permute-done | bytes 65568 | tf_op jit(solution)/shard_map/ppermute | solution.py:350
  36.9 0.0 copy-done
  36.9 0.0 copy-done.1
  36.9 0.0 copy-done.2
  36.9 0.0 copy-done.4
  36.9 0.0 copy-done.9
  36.9 1.8 %feed.1 = (bf16[16,2048]{1,0:T(8,128)(2,1)S(1)}, f32[16,2048]{1,0:T(8,128)S(1)}) custom-call(bf16[16,2048]{1,0:T(8,128)(2,1)S(1)} %copy-done.4, bf16[16,2048]{1,0:T(8,128)(2,1)S(1)} %add_convert_fusion.1.here_ref, bf16[16,2048]{1,0:T(8,128)(2,1)S(1)} %collective-permute-done.1.there_ref, bf16[16,128]{1,0:T(8,128)(2,1)S(1)} %bitcast.17, ...), custom_call_target="tpu_custom_call" | custom-call | tf_op jit(solution)/shard_map/feed/pallas_call | solution.py:495
  38.7 0.2 collective-permute-start.2
  38.9 1.1 %collective-permute-done.2 = bf16[16,2048]{1,0:T(8,128)(2,1)S(1)} collective-permute-done((bf16[16,2048]{1,0:T(8,128)(2,1)S(1)}, bf16[16,2048]{1,0:T(8,128)(2,1)S(1)}, u32[]{:S(2)}, u32[]{:S(2)}) %collective-permute-start.2) | collective-permute-done | bytes 65568 | tf_op jit(solution)/shard_map/ppermute | solution.py:350
  40.0 1.3 %collective-permute-start.3 = (bf16[16,2048]{1,0:T(8,128)(2,1)S(1)}, bf16[16,2048]{1,0:T(8,128)(2,1)S(1)}, u32[]{:S(2)}, u32[]{:S(2)}) collective-permute-start(bf16[16,2048]{1,0:T(8,128)(2,1)S(1)} %add_convert_fusion), channel_id=1, source_target_pairs={{0,3},{1,2},{2,1},{3,0},{4,7},{5,6},{6,5},{7,4},{8,11},{9,10},{10,... | collective-permute-start | bytes 196616 | tf_op jit(solution)/shard_map/ppermute | solution.py:350
  41.3 0.6 %reshape.55 = f32[16,2,256]{2,1,0:T(2,128)} reshape(f32[16,512]{1,0:T(8,128)S(1)} %get-tuple-element.25.kv_ref) | data formatting | bytes 65536 | tf_op jit(solution)/shard_map/reshape | solution.py:507
  42.0 2.2 %collective-permute-done.3 = bf16[16,2048]{1,0:T(8,128)(2,1)S(1)} collective-permute-done((bf16[16,2048]{1,0:T(8,128)(2,1)S(1)}, bf16[16,2048]{1,0:T(8,128)(2,1)S(1)}, u32[]{:S(2)}, u32[]{:S(2)}) %collective-permute-start.3) | collective-permute-done | bytes 65568 | tf_op jit(solution)/shard_map/ppermute | solution.py:350
  44.1 0.7 %add_add_fusion = f32[16,2048]{1,0:T(8,128)} fusion(f32[16,2048]{1,0:T(8,128)S(1)} %get-tuple-element.26, bf16[16,2048]{1,0:T(8,128)(2,1)S(1)} %collective-permute-done.3, bf16[16,2048]{1,0:T(8,128)(2,1)S(1)} %add_convert_fusion), kind=kLoop, calls=%fused_computation | loop fusion | flops 131072 | bytes 393216 | tf_op jit(solution)/shard_map/add | solution.py:506
  (2 shorter events, 0.0 us)
Async XLA Ops:
  0.6 17.8 %copy-start.8 = (s32[4096]{0:T(1024)S(1)}, s32[4096]{0:T(1024)}, u32[]{:S(2)}) copy-start(s32[4096]{0:T(1024)} %param.20) | copy-start | bytes 49156
  3.4 15.0 %copy-start.5 = (bf16[128,128]{1,0:T(8,128)(2,1)S(1)}, bf16[128,128]{1,0:T(8,128)(2,1)}, u32[]{:S(2)}) copy-start(bf16[128,128]{1,0:T(8,128)(2,1)} %get-tuple-element.16.sort_ref) | copy-start | bytes 98308
  3.4 15.0 %copy-start.6 = (bf16[128,128]{1,0:T(8,128)(2,1)S(1)}, bf16[128,128]{1,0:T(8,128)(2,1)}, u32[]{:S(2)}) copy-start(bf16[128,128]{1,0:T(8,128)(2,1)} %get-tuple-element.17.upto_ref) | copy-start | bytes 98308
  3.4 15.0 %copy-start.7 = (bf16[128,128]{1,0:T(8,128)(2,1)S(1)}, bf16[128,128]{1,0:T(8,128)(2,1)}, u32[]{:S(2)}) copy-start(bf16[128,128]{1,0:T(8,128)(2,1)} %get-tuple-element.18.back_ref) | copy-start | bytes 98308
  3.4 15.0 %all-to-all-start = ((bf16[8,16,640]{2,1,0:T(8,128)(2,1)}), bf16[8,16,640]{2,1,0:T(8,128)(2,1)S(1)}, u32[]{:S(2)}, u32[]{:S(2)}) async-start(bf16[8,16,640]{2,1,0:T(8,128)(2,1)} %get-tuple-element.15), calls=%async_computation | async-start | bytes 327680 | tf_op jit(solution)/shard_map/all_to_all | solution.py:422
  18.4 12.4 %copy-start.3 = (bf16[512,2048]{1,0:T(8,128)(2,1)S(1)}, bf16[512,2048]{1,0:T(8,128)(2,1)}, u32[]{:S(2)}) copy-start(bf16[512,2048]{1,0:T(8,128)(2,1)} %w_ref.1) | copy-start | bytes 6291460
  30.8 6.1 %copy-start = (bf16[2048,1024]{1,0:T(8,128)(2,1)S(1)}, bf16[2048,1024]{1,0:T(8,128)(2,1)}, u32[]{:S(2)}) copy-start(bf16[2048,1024]{1,0:T(8,128)(2,1)} %wg_ref.1) | copy-start | bytes 12582916
  30.8 6.1 %copy-start.1 = (bf16[2048,1024]{1,0:T(8,128)(2,1)S(1)}, bf16[2048,1024]{1,0:T(8,128)(2,1)}, u32[]{:S(2)}) copy-start(bf16[2048,1024]{1,0:T(8,128)(2,1)} %wu_ref.1) | copy-start | bytes 12582916
  30.8 6.1 %copy-start.2 = (bf16[1024,2048]{1,0:T(8,128)(2,1)S(1)}, bf16[1024,2048]{1,0:T(8,128)(2,1)}, u32[]{:S(2)}) copy-start(bf16[1024,2048]{1,0:T(8,128)(2,1)} %wd_ref.1) | copy-start | bytes 12582916
  30.8 6.1 %copy-start.4 = (bf16[16,2048]{1,0:T(8,128)(2,1)S(1)}, bf16[16,2048]{1,0:T(8,128)(2,1)}, u32[]{:S(2)}) copy-start(bf16[16,2048]{1,0:T(8,128)(2,1)} %tokens_ref.1) | copy-start | bytes 196612
  30.8 6.1 %copy-start.9 = (bf16[2048]{0:T(1024)(128)(2,1)S(1)}, bf16[2048]{0:T(1024)(128)(2,1)}, u32[]{:S(2)}) copy-start(bf16[2048]{0:T(1024)(128)(2,1)} %param.27) | copy-start | bytes 12292
  31.5 1.3 %collective-permute-start = (bf16[16,2048]{1,0:T(8,128)(2,1)S(1)}, bf16[16,2048]{1,0:T(8,128)(2,1)S(1)}, u32[]{:S(2)}, u32[]{:S(2)}) collective-permute-start(bf16[16,2048]{1,0:T(8,128)(2,1)S(1)} %output.1), channel_id=1, source_target_pairs={{0,1},{1,0},{2,3},{3,2},{4,5},{5,4},{6,7},{7,6},{8,9},{9,8},{10,11... | collective-permute-start | bytes 196616 | tf_op jit(solution)/shard_map/ppermute | solution.py:350
  32.7 4.1 %collective-permute-start.1 = (bf16[16,2048]{1,0:T(8,128)(2,1)S(1)}, bf16[16,2048]{1,0:T(8,128)(2,1)S(1)}, u32[]{:S(2)}, u32[]{:S(2)}) collective-permute-start(bf16[16,2048]{1,0:T(8,128)(2,1)S(1)} %add_convert_fusion.1.here_ref), channel_id=1, source_target_pairs={{0,3},{1,2},{2,1},{3,0},{4,7},{5,6},{6,5},{7,4},{8,11},{9,10},{10,... | collective-permute-start | bytes 196616 | tf_op jit(solution)/shard_map/ppermute | solution.py:350
  38.7 1.3 %collective-permute-start.2 = (bf16[16,2048]{1,0:T(8,128)(2,1)S(1)}, bf16[16,2048]{1,0:T(8,128)(2,1)S(1)}, u32[]{:S(2)}, u32[]{:S(2)}) collective-permute-start(bf16[16,2048]{1,0:T(8,128)(2,1)S(1)} %get-tuple-element.27), channel_id=1, source_target_pairs={{0,1},{1,0},{2,3},{3,2},{4,5},{5,4},{6,7},{7,6},{8,9},{9,8},{10,11... | collective-permute-start | bytes 196616 | tf_op jit(solution)/shard_map/ppermute | solution.py:350
  40.0 4.1 %collective-permute-start.3 = (bf16[16,2048]{1,0:T(8,128)(2,1)S(1)}, bf16[16,2048]{1,0:T(8,128)(2,1)S(1)}, u32[]{:S(2)}, u32[]{:S(2)}) collective-permute-start(bf16[16,2048]{1,0:T(8,128)(2,1)S(1)} %add_convert_fusion), channel_id=1, source_target_pairs={{0,3},{1,2},{2,1},{3,0},{4,7},{5,6},{6,5},{7,4},{8,11},{9,10},{10,... | collective-permute-start | bytes 196616 | tf_op jit(solution)/shard_map/ppermute | solution.py:350
